TPU v7x, 32 devices: a whole 2x2x4 slice. The times are simulated.
32 devices in a mesh: ka: 8 (over z, y), gz: 4 (over x, core).
Axes of the slice: x: 2, y: 2, z: 4, core: 2. Of those that a mesh axis runs over, the one named last changes fastest.
Arguments:
- fields: float32 [8, 2, 32, 3, 25600], P('ka', None, None, None, 'gz'), may hold values from -0.25 to 0.25
- bvectors: float32 [2, 3], replicated, may hold values from -0.5 to 0.5
- gshift: int32 [8, 2, 3], replicated, may hold values from -1 to 1
Outputs:
- intersections: float32 [8, 4, 2, 32, 32], P('ka')
All inputs are finite; a program needn't handle non-finite values.
Results may differ from a plain program's by a relative error of at most 0.0003.
Values sent between devices are 32-bit elements; how exact they have to be, the bound alone decides.
No kernel may reach another device: no remote copies, remote signals or barrier semaphores. Data moves between devices by JAX's collectives and lax.ppermute only.
A program may use at most 128 MiB of HBM per device.

v0:
```python
import math

import jax
import jax.numpy as jnp
from jax import lax
from jax.sharding import PartitionSpec as P

GX = 40
GY = 40
KX = 4


two_pi = 2.0 * math.pi


def shifted(value, axis, steps):
    count = lax.axis_size(axis)
    pairs = [(source, (source + steps) % count) for source in range(count)]
    return lax.ppermute(value, axis, pairs)


def phase_angle(q_vector, xcoord, ycoord, zcoord, x_extent, y_extent, z_extent):
    return -two_pi * (
        q_vector[0] * xcoord / x_extent
        + q_vector[1] * ycoord / y_extent
        + q_vector[2] * zcoord / z_extent
    )


def intersection(left_field, right_field, angles):
    cosine_part = jnp.cos(angles)
    sine_part = jnp.sin(angles)
    r_real = right_field[0]
    r_imag = right_field[1]
    w_real = cosine_part * r_real - sine_part * r_imag
    w_imag = sine_part * r_real + cosine_part * r_imag
    band_count = left_field.shape[1]
    left_rows = jnp.concatenate(
        [left_field[0].reshape(band_count, -1), left_field[1].reshape(band_count, -1)], axis=1
    )
    upper_rows = jnp.concatenate(
        [w_real.reshape(band_count, -1), w_imag.reshape(band_count, -1)], axis=1
    )
    lower_rows = jnp.concatenate(
        [w_imag.reshape(band_count, -1), -w_real.reshape(band_count, -1)], axis=1
    )
    right_rows = jnp.concatenate([upper_rows, lower_rows], axis=0)
    product = lax.dot_general(
        left_rows,
        right_rows,
        (((1,), (1,)), ((), ())),
        precision=lax.Precision.HIGHEST,
        preferred_element_type=jnp.float32,
    )
    return jnp.stack([product[:, :band_count], product[:, band_count:]])


def adjoint(block):
    return jnp.stack([block[0].T, -block[1].T])


def per_device(fields, bvectors, gshift):
    local_field = fields[0]
    local_cells = local_field.shape[-1]
    plane_cells = GX * GY
    slab_depth = local_cells // plane_cells
    z_extent = slab_depth * lax.axis_size("gz")
    cell_index = jnp.arange(local_cells, dtype=jnp.int32)
    xcoord = (cell_index % GX).astype(jnp.float32)
    ycoord = (cell_index // GX % GY).astype(jnp.float32)
    zcoord = (lax.axis_index("gz") * slab_depth + cell_index // plane_cells).astype(jnp.float32)
    kpoint = lax.axis_index("ka")
    shifts_float = gshift.astype(jnp.float32)

    def angles_of(q_vector):
        return phase_angle(q_vector, xcoord, ycoord, zcoord, GX, GY, z_extent)

    q_plus_x = bvectors[0] + shifts_float[kpoint, 0]
    q_plus_y = bvectors[1] + shifts_float[kpoint, 1]

    def forward_neighbour(offset):
        return shifted(local_field, "ka", offset)

    forward = jnp.stack(
        [
            intersection(local_field, forward_neighbour(-1), angles_of(q_plus_x)),
            intersection(local_field, forward_neighbour(-KX), angles_of(q_plus_y)),
        ]
    )
    forward = lax.psum(forward, "gz")

    def returned(offset):
        return shifted(forward, "ka", offset)

    from_left = returned(1)
    from_below = returned(KX)
    summed = jnp.stack([forward[0], adjoint(from_left[0]), forward[1], adjoint(from_below[1])])
    return summed[None]


def solution(mesh):
    in_specs = (P("ka", None, None, None, "gz"), P(), P())
    out_specs = P("ka", None, None, None, None)
    return jax.shard_map(
        per_device, mesh=mesh, in_specs=in_specs, out_specs=out_specs, check_vma=False
    )
```

profile of v0, /device:TPU:8, one launch (start us, length us, event | category | flops | bytes accessed | tf_op | source)
XLA Modules:
  0.0 372.9 jit_solution(3932739088529129570)
XLA Ops:
  0.0 2.6 collective-permute-start.1
  2.6 1.4 collective-permute-start
  4.0 2.7 fusion.42
  6.8 1.7 copy.7
  8.4 0.4 copy.18
  8.9 1.7 copy.8
  10.6 0.0 copy-start.2
  10.6 0.0 copy-start.3
  10.6 1.8 copy.19
  12.5 0.0 copy-done.2
  12.5 0.2 dynamic-slice_reduce_fusion.1
  12.6 0.0 copy-done.3
  12.7 0.7 fusion.44
  13.3 2.1 fusion.32
  15.5 2.1 fusion.33
  17.8 2.0 fusion.34
  19.9 2.0 fusion.35
  22.0 0.0 copy-start
  22.0 0.2 constant_dynamic-update-slice_fusion.1
  22.2 1.5 copy-done
  23.7 0.2 constant_dynamic-update-slice_fusion
  23.8 0.0 copy-start.1
  23.9 2.3 copy-done.1
  26.1 292.6 %collective-permute-done.1 = f32[2,32,3,6400]{3,1,2,0:T(8,128)} collective-permute-done((f32[2,32,3,6400]{3,1,2,0:T(8,128)}, f32[2,32,3,6400]{3,1,2,0:T(8,128)}, u32[]{:S(2)}, u32[]{:S(2)}) %collective-permute-start.1) | collective-permute-done | bytes 4915232 | tf_op jit(solution)/shard_map/ppermute | solution.py:19
  318.7 2.8 fusion.41
  321.5 1.7 copy.12
  323.2 0.4 copy.23
  323.6 1.7 copy.11
  325.3 0.0 slice-start
  325.3 0.4 copy.22
  325.8 0.0 slice-start.1
  325.8 0.6 fusion.39
  326.4 1.1 slice-done
  327.5 0.3 slice-done.1
  327.8 8.0 %fusion.8 = f32[32,64]{1,0:T(8,128)S(1)} fusion(f32[32,38400]{1,0:T(8,128)S(1)} %bitcast.88, f32[32,19200]{1,0:T(8,128)S(1)} %get-tuple-element.9, f32[32,19200]{1,0:T(8,128)S(1)} %get-tuple-element.12, f32[32,19200]{1,0:T(8,128)S(1)} %get-tuple-element.10), kind=kOutput, calls=%fused_computation.8 | convolution fusion | flops 951091200 | bytes 12296192 | tf_op jit(solution)/shard_map/dot_general | solution.py:48
  335.8 0.1 slice_bitcast_fusion.3
  335.8 0.0 collective-permute-done
  335.9 2.8 fusion.40
  338.6 1.7 copy.10
  340.3 0.4 copy.21
  340.7 1.7 copy.9
  342.4 0.7 copy.20
  343.1 0.6 fusion.38
  343.7 7.8 %fusion = f32[32,64]{1,0:T(8,128)S(1)} fusion(f32[32,38400]{1,0:T(8,128)S(1)} %bitcast.88, f32[32,19200]{1,0:T(8,128)S(1)} %get-tuple-element.7, f32[32,19200]{1,0:T(8,128)S(1)} %get-tuple-element.11, f32[32,19200]{1,0:T(8,128)S(1)} %get-tuple-element.8), kind=kOutput, calls=%fused_computation | convolution fusion | flops 951091200 | bytes 12296192 | tf_op jit(solution)/shard_map/dot_general | solution.py:48
  351.5 0.1 slice_bitcast_fusion.5
  351.6 11.8 %psum.7 = f32[2,2,32,32]{3,2,1,0:T(8,128)S(1)} all-reduce(f32[2,2,32,32]{3,2,1,0:T(8,128)S(1)} %pad_maximum_fusion), channel_id=1, replica_groups=mesh['ka'=8,'gz'=4] {'gz'}, use_global_device_ids=true, to_apply=%region_0.1 | all-reduce | flops 4096 | bytes 32768 | tf_op jit(solution)/shard_map/psum | solution.py:90
  363.4 3.4 collective-permute-start.3
  366.9 0.0 collective-permute-start.2
  366.9 0.1 copy.17
  367.0 0.1 copy.16
  367.0 2.1 collective-permute-done.3
  369.1 2.9 collective-permute-done.2
  372.1 0.8 copy.15
  (20 shorter events, 0.3 us)
Async XLA Ops:
  0.0 318.7 %collective-permute-start.1 = (f32[2,32,3,6400]{3,1,2,0:T(8,128)}, f32[2,32,3,6400]{3,1,2,0:T(8,128)}, u32[]{:S(2)}, u32[]{:S(2)}) collective-permute-start(f32[2,32,3,6400]{3,1,2,0:T(8,128)} %bitcast.85), channel_id=1, source_target_pairs={{0,16},{4,20},{8,24},{12,28},{16,0},{20,4},{24,8},{28,12},{1,17},{... | collective-permute-start | bytes 14745608 | tf_op jit(solution)/shard_map/ppermute | solution.py:19
  2.6 333.3 %collective-permute-start = (f32[2,32,3,6400]{3,1,2,0:T(8,128)}, f32[2,32,3,6400]{3,1,2,0:T(8,128)}, u32[]{:S(2)}, u32[]{:S(2)}) collective-permute-start(f32[2,32,3,6400]{3,1,2,0:T(8,128)} %bitcast.86), channel_id=1, source_target_pairs={{0,28},{4,0},{8,4},{12,8},{16,12},{20,16},{24,20},{28,24},{1,29},{... | collective-permute-start | bytes 14745608 | tf_op jit(solution)/shard_map/ppermute | solution.py:19
  10.6 1.9 copy-start.2
  10.6 2.0 copy-start.3
  22.0 1.7 copy-start
  23.8 2.3 copy-start.1
  325.3 2.2 slice-start
  325.8 2.0 slice-start.1
  363.4 5.7 %collective-permute-start.3 = (f32[2,2,32,32]{3,2,1,0:T(8,128)S(1)}, f32[2,2,32,32]{3,2,1,0:T(8,128)S(1)}, u32[]{:S(2)}, u32[]{:S(2)}) collective-permute-start(f32[2,2,32,32]{3,2,1,0:T(8,128)S(1)} %psum.7), channel_id=1, source_target_pairs={{0,16},{4,20},{8,24},{12,28},{16,0},{20,4},{24,8},{28,12},{1,17},{... | collective-permute-start | bytes 49160 | tf_op jit(solution)/shard_map/ppermute | solution.py:19
  366.9 5.2 %collective-permute-start.2 = (f32[2,2,32,32]{3,2,1,0:T(8,128)S(1)}, f32[2,2,32,32]{3,2,1,0:T(8,128)S(1)}, u32[]{:S(2)}, u32[]{:S(2)}) collective-permute-start(f32[2,2,32,32]{3,2,1,0:T(8,128)S(1)} %psum.7), channel_id=1, source_target_pairs={{0,4},{4,8},{8,12},{12,16},{16,20},{20,24},{24,28},{28,0},{1,5},{5... | collective-permute-start | bytes 49160 | tf_op jit(solution)/shard_map/ppermute | solution.py:19
where the time goes:
time: 373 us
  waiting for transfers between devices  298 us (80%)
  local copies, waits for them, and re-layouts  30.3 us (8%)
  matrix products  15.8 us (4%)
  blocking collectives  11.8 us (3%)
  other arithmetic  9.61 us (3%)
  starting transfers between devices  7.44 us (2%)
    ppermute x4, waiting for transfers between devices, shifted(): return lax.ppermute(value, axis, pairs)  298 us
    dot_general x2, matrix products, intersection(): lax.dot_general(left_rows, right_rows, (((1,), (1,)), ((), ())), precisio...  15.8 us
    psum x1, blocking collectives, per_device(): forward = lax.psum(forward, 'gz')  11.8 us
    unnamed x21, local copies, waits for them, and re-layouts  9.8 us
    slice x4, local copies, waits for them, and re-layouts, intersection(): r_real = right_field[0]  8.88 us
  transfers between devices with their start and end apart: 4, of which 3 were waited for; matrix products, arithmetic and copies ran while one was open for 9% of the time, Pallas kernels for 0%

commit v1 on v0

v1 whole, which is shorter than its diff:
```python
import functools
import math

import jax
import jax.numpy as jnp
from jax import lax
from jax.experimental import pallas as pl
from jax.experimental.pallas import tpu as pltpu
from jax.sharding import PartitionSpec as P

GX = 40
GY = 40
KX = 4
LANES = 128
CHUNKS = 3

two_pi = 2.0 * math.pi


def shifted(value, axis, steps):
    count = lax.axis_size(axis)
    pairs = [(source, (source + steps) % count) for source in range(count)]
    return lax.ppermute(value, axis, pairs)


def phase_angle(q_vector, xcoord, ycoord, zcoord, x_extent, y_extent, z_extent):
    return -two_pi * (
        q_vector[0] * xcoord / x_extent
        + q_vector[1] * ycoord / y_extent
        + q_vector[2] * zcoord / z_extent
    )


class Parts:
    def __init__(self, components, cells, count):
        self.components = components
        self.count = count
        tiles = cells // LANES
        self.tiles = tiles
        self.main = tiles // count
        self.rest = tiles - self.main * count
        self.extra = -(-components * self.rest // count)
        self.units = components * self.main + self.extra

    def pieces(self, start, stop):
        runs = []
        unit = start
        while unit < stop:
            if unit < self.components * self.main:
                component, tile = divmod(unit, self.main)
                length = min(self.main - tile, stop - unit)
                runs.append((component, tile, length))
            else:
                length = 1
                runs.append((None, unit - self.components * self.main, 1))
            unit += length
        return runs

    def extra_unit(self, part, slot):
        number = slot * self.count + part
        valid = number < self.components * self.rest
        number = jnp.minimum(number, self.components * self.rest - 1)
        return number // self.rest, self.main * self.count + number % self.rest, valid

    def take(self, field, part, start, stop):
        bands = field.shape[2]
        found = []
        for component, tile, length in self.pieces(start, stop):
            if component is None:
                which, at, _ = self.extra_unit(part, tile)
                origin = (0, which, 0, at * LANES)
            else:
                origin = (0, component, 0, (part * self.main + tile) * LANES)
            found.append(lax.dynamic_slice(field, origin, (2, 1, bands, length * LANES))[:, 0])
        return found[0] if len(found) == 1 else jnp.concatenate(found, axis=2)

    def cell_index(self, part, start, stop):
        cells, valid = [], []
        lane = jnp.arange(LANES, dtype=jnp.int32)
        for component, tile, length in self.pieces(start, stop):
            if component is None:
                _, at, good = self.extra_unit(part, tile)
                cells.append(at * LANES + lane)
                valid.append(jnp.full((LANES,), 1.0, jnp.float32) * good.astype(jnp.float32))
            else:
                run = jnp.arange(length * LANES, dtype=jnp.int32)
                cells.append((part * self.main + tile) * LANES + run)
                valid.append(jnp.ones((length * LANES,), jnp.float32))
        return jnp.concatenate(cells), jnp.concatenate(valid)


def split_parts(value):
    high = value.astype(jnp.bfloat16)
    low = (value - high.astype(jnp.float32)).astype(jnp.bfloat16)
    return high, low


def chunk_kernel(count, offsets, first, *refs):
    blocks = refs[:count]
    cosine_ref, sine_ref = refs[count], refs[count + 1]
    rest = refs[count + 2 :]
    if first:
        total_ref, held, sems = rest
        before_ref = None
    else:
        before_ref, total_ref, held, sems = rest
    copies = [
        pltpu.make_async_copy(blocks[step], held.at[step], sems.at[step]) for step in range(count)
    ]
    for copy in copies:
        copy.start()
    for copy in copies:
        copy.wait()

    @pl.loop(0, count)
    def _(step):
        left = held[step]
        bands, cells = left.shape[1], left.shape[2]
        left_high, left_low = split_parts(left.reshape(2 * bands, cells))
        left_rows = jnp.concatenate([left_high, left_low], axis=0)
        highs, lows = [], []
        for direction, offset in enumerate(offsets):
            right = held[lax.rem(step + offset, count)]
            cosine = cosine_ref[step * len(offsets) + direction]
            sine = sine_ref[step * len(offsets) + direction]
            w_real = cosine * right[0] - sine * right[1]
            w_imag = sine * right[0] + cosine * right[1]
            high, low = split_parts(jnp.concatenate([w_real, w_imag], axis=0))
            highs.append(high)
            lows.append(low)
        right_rows = jnp.concatenate(highs + lows, axis=0)
        product = lax.dot_general(
            left_rows,
            right_rows,
            (((1,), (1,)), ((), ())),
            preferred_element_type=jnp.float32,
        )
        half = product.shape[1] // 2
        rows = product[: 2 * bands] + product[2 * bands :]
        summed = rows[:, :half] + rows[:, half:]
        if not first:
            summed = summed + before_ref[step]
        total_ref[step] = summed


def chunk_products(blocks, cosine, sine, before, offsets):
    count = len(blocks)
    _, bands, cells = blocks[0].shape
    width = 2 * len(offsets) * bands
    operands = list(blocks) + [cosine, sine]
    anywhere = pl.BlockSpec(memory_space=pl.ANY)
    inside = pl.BlockSpec(memory_space=pltpu.VMEM)
    in_specs = [anywhere] * count + [inside, inside]
    if before is not None:
        operands.append(before)
        in_specs.append(inside)
    flops = 2 * count * (4 * bands) * (2 * width) * cells
    return pl.pallas_call(
        functools.partial(chunk_kernel, count, offsets, before is None),
        out_shape=jax.ShapeDtypeStruct((count, 2 * bands, width), jnp.float32),
        in_specs=in_specs,
        out_specs=inside,
        scratch_shapes=[
            pltpu.VMEM((count, 2, bands, cells), jnp.float32),
            pltpu.SemaphoreType.DMA((count,)),
        ],
        compiler_params=pltpu.CompilerParams(vmem_limit_bytes=32 * 1024 * 1024),
        cost_estimate=pl.CostEstimate(
            flops=flops, bytes_accessed=4 * count * 2 * bands * cells, transcendentals=0
        ),
    )(*operands)


def block_factor(count):
    best = 1
    for factor in range(1, math.isqrt(count) + 1):
        if count % factor == 0:
            best = factor
    return best


def messages_kernel(count, offsets, factor, total_ref, out_ref, forward):
    me = lax.axis_index("ka")
    bands = total_ref.shape[1] // 2
    width = total_ref.shape[2]
    lane = lax.broadcasted_iota(jnp.int32, (bands, width), 1)
    real_lane = lane % (2 * bands) < bands

    @pl.loop(0, count)
    def _(step):
        with_real = total_ref[step, :bands]
        with_imag = total_ref[step, bands:]
        after = pltpu.roll(with_imag, width - bands, 1)
        ahead = pltpu.roll(with_imag, bands, 1)
        forward[step] = with_real + jnp.where(real_lane, after, -ahead)

    @pl.loop(0, count)
    def _(step):
        target = lax.rem(me + step, count)
        low = lax.rem(target, factor) + factor - lax.rem(me, factor)
        turn = lax.rem(low, factor)
        group = target // factor
        out_ref[turn, group, 0] = forward[step]
        back = jnp.zeros((bands, width), jnp.float32)
        for direction, offset in enumerate(offsets):
            other = forward[lax.rem(step + count - offset, count)]
            back = jnp.where(lane // (2 * bands) == direction, other, back)
        out_ref[turn, group, 1] = back


def messages(total, offsets, factor):
    count, rows, width = total.shape
    inside = pl.BlockSpec(memory_space=pltpu.VMEM)
    return pl.pallas_call(
        functools.partial(messages_kernel, count, offsets, factor),
        out_shape=jax.ShapeDtypeStruct((factor, count // factor, 2, rows // 2, width), jnp.float32),
        in_specs=[inside],
        out_specs=inside,
        scratch_shapes=[pltpu.VMEM((count, rows // 2, width), jnp.float32)],
    )(total)


def result_kernel(*refs):
    out_ref = refs[-1]
    total = refs[0][...]
    for ref in refs[1:-1]:
        total = total + ref[...]
    bands = out_ref.shape[2]
    flipped = total[1].T
    for direction in range(out_ref.shape[0] // 2):
        at = 2 * bands * direction
        out_ref[2 * direction, 0] = total[0, :, at : at + bands]
        out_ref[2 * direction, 1] = total[0, :, at + bands : at + 2 * bands]
        out_ref[2 * direction + 1, 0] = flipped[at : at + bands]
        out_ref[2 * direction + 1, 1] = -flipped[at + bands : at + 2 * bands]


def result(shares):
    _, bands, width = shares[0].shape
    inside = pl.BlockSpec(memory_space=pltpu.VMEM)
    return pl.pallas_call(
        result_kernel,
        out_shape=jax.ShapeDtypeStruct((width // bands, 2, bands, bands), jnp.float32),
        in_specs=[inside] * len(shares),
        out_specs=inside,
    )(*shares)


def reduced_over_points(blocks, factor):
    groups = blocks.shape[1]
    me = lax.axis_index("ka")
    count = lax.axis_size("ka")
    total = blocks[0]
    for turn in range(1, factor):
        pairs = [
            (source, source - source % factor + (source + turn) % factor) for source in range(count)
        ]
        total = total + lax.ppermute(blocks[turn], "ka", pairs)
    group = me // factor
    mine = lax.dynamic_index_in_dim(total, group, 0, keepdims=False)
    arrived = []
    for turn in range(1, groups):
        sent = lax.dynamic_index_in_dim(total, (group + turn) % groups, 0, keepdims=False)
        arrived.append(shifted(sent, "ka", turn * factor))
    return mine + sum(arrived)


def per_device(fields, bvectors, gshift):
    count = lax.axis_size("ka")
    slabs = lax.axis_size("gz")
    me = lax.axis_index("ka")
    field = fields[0].transpose(0, 2, 1, 3)
    cells = field.shape[-1]
    plane_cells = GX * GY
    slab_depth = cells // plane_cells
    z_extent = slab_depth * slabs
    parts = Parts(field.shape[1], cells, count)
    offsets = (1 % count, KX % count)

    cell_index, valid = parts.cell_index(me, 0, parts.units)
    xcoord = (cell_index % GX).astype(jnp.float32)
    ycoord = (cell_index // GX % GY).astype(jnp.float32)
    zcoord = (lax.axis_index("gz") * slab_depth + cell_index // plane_cells).astype(jnp.float32)
    shifts_float = gshift.astype(jnp.float32)
    q_vectors = jnp.roll(bvectors[None] + shifts_float, -me, axis=0).reshape(-1, 3)
    angles = phase_angle(q_vectors.T[:, :, None], xcoord, ycoord, zcoord, GX, GY, z_extent)
    cosine = (jnp.cos(angles) * valid)[:, None]
    sine = (jnp.sin(angles) * valid)[:, None]

    order = sorted(range(1, count), key=lambda step: -min(step, count - step))
    bounds = [parts.units * chunk // CHUNKS for chunk in range(CHUNKS + 1)]
    total = None
    for start, stop in zip(bounds[:-1], bounds[1:]):
        blocks = [None] * count
        for step in order:
            sent = parts.take(field, (me + count - step) % count, start, stop)
            blocks[step] = shifted(sent, "ka", -step)
        blocks[0] = parts.take(field, me, start, stop)
        lanes = slice(start * LANES, stop * LANES)
        total = chunk_products(blocks, cosine[:, :, lanes], sine[:, :, lanes], total, offsets)

    factor = block_factor(count)
    share = reduced_over_points(messages(total, offsets, factor), factor)
    shares = [share] + [shifted(share, "gz", step) for step in range(1, slabs)]
    return result(shares)[None]


def solution(mesh):
    in_specs = (P("ka", None, None, None, "gz"), P(), P())
    out_specs = P("ka", None, None, None, None)
    return jax.shard_map(
        per_device, mesh=mesh, in_specs=in_specs, out_specs=out_specs, check_vma=False
    )
```

time: 373 us -> 162 us (0.43)
  the two profiles are of different devices: /device:TPU:8 before, /device:TPU:1 now
where the time goes in v1:
time: 162 us
  starting transfers between devices  71.7 us (44%)
  waiting for transfers between devices  53.6 us (33%)
  Pallas kernels  18 us (11%)
  other arithmetic  9.96 us (6%)
  local copies, waits for them, and re-layouts  7.59 us (5%)
    ppermute x27, starting transfers between devices, shifted(): return lax.ppermute(value, axis, pairs)  71.6 us
    ppermute x27, waiting for transfers between devices, shifted(): return lax.ppermute(value, axis, pairs)  49.3 us
    pallas_call x3, Pallas kernels, chunk_products(): pl.pallas_call(functools.partial(chunk_kernel, count, offsets, before is...  14 us
    squeeze x2, local copies, waits for them, and re-layouts, take(): lax.dynamic_slice(field, origin, (2, 1, bands, length * LANES))[:, 0]  4.99 us
    mul x1, other arithmetic, per_device(): sine = (jnp.sin(angles) * valid)[:, None]  4.62 us
    ppermute x1, waiting for transfers between devices, reduced_over_points(): total = total + lax.ppermute(blocks[turn], 'ka', pairs)  4.35 us
    mul x1, other arithmetic, per_device(): cosine = (jnp.cos(angles) * valid)[:, None]  4.06 us
  transfers between devices with their start and end apart: 28, of which 13 were waited for; matrix products, arithmetic and copies ran while one was open for 6% of the time, Pallas kernels for 6%

profile of v1, /device:TPU:1, one launch (start us, length us, event | category | flops | bytes accessed | tf_op | source)
XLA Modules:
  0.0 161.6 jit_solution(2318436089455155153)
XLA Ops:
  0.0 4.0 %dynamic-slice_bitcast_fusion = (f32[2,32,768]{2,1,0:T(8,128)}, f32[2,32,768]{2,1,0:T(8,128)}, f32[2,32,768]{2,1,0:T(8,128)}, f32[2,32,768]{2,1,0:T(8,128)}, f32...) fusion(f32[1,2,32,3,6400]{4,2,3,1,0:T(8,128)} %param.3, ...), kind=kLoop, calls=%fused_computation.8 | loop fusion | bytes 9437216 | tf_op jit(solution)/shard_map/squeeze | solution.py:74
  4.0 5.2 %collective-permute-start.14 = (f32[2,32,768]{2,1,0:T(8,128)}, f32[2,32,768]{2,1,0:T(8,128)S(1)}, u32[]{:S(2)}, u32[]{:S(2)}) collective-permute-start(f32[2,32,768]{2,1,0:T(8,128)} %get-tuple-element.12), channel_id=1, source_target_pairs={{0,28},{4,0},{8,4},{12,8},{16,12},{20,16},{24,20},{28,24},{1,29},{... | collective-permute-start | bytes 589832 | tf_op jit(solution)/shard_map/ppermute | solution.py:23
  9.2 0.2 collective-permute-start.15
  9.4 0.0 collective-permute-start.16
  9.4 2.4 %collective-permute-start.17 = (f32[2,32,768]{2,1,0:T(8,128)}, f32[2,32,768]{2,1,0:T(8,128)S(1)}, u32[]{:S(2)}, u32[]{:S(2)}) collective-permute-start(f32[2,32,768]{2,1,0:T(8,128)} %get-tuple-element.9), channel_id=1, source_target_pairs={{0,16},{4,20},{8,24},{12,28},{16,0},{20,4},{24,8},{28,12},{1,17},{... | collective-permute-start | bytes 589832 | tf_op jit(solution)/shard_map/ppermute | solution.py:23
  11.8 0.0 collective-permute-start.18
  12.1 0.1 copy.8
  12.2 0.1 convert_add_fusion
  12.3 0.1 fusion.8
  12.3 0.1 copy.9
  12.4 0.1 reshape.636
  12.6 4.6 %sine_multiply_fusion = (f32[16,1,2432]{2,1,0:T(1,128)S(1)}, f32[16,1,2432]{2,1,0:T(1,128)S(1)}) fusion(f32[2432]{0:T(1024)S(1)} %pad_maximum_fusion.8, f32[2432]{0:T(1024)S(1)} %get-tuple-element.48, f32[16]{0:T(128)S(1)} %get-tuple-element.50, f32[2432]{0:T(1024)S(1)} %get-tuple-element.47, f32[16]{0:T(128)S(1)} %get-tuple-element.51, ...), kind=kLoop, calls=%fused_computation.34 | loop fusion | flops 350208 | bytes 350400 | tf_op jit(solution)/shard_map/mul | solution.py:288
  17.3 4.1 %cosine_multiply_fusion = f32[16,1,2432]{2,1,0:T(1,128)S(1)} fusion(f32[16,1,2432]{2,1,0:T(1,128)S(1)} %get-tuple-element.6, f32[2432]{0:T(1024)S(1)} %pad_maximum_fusion.8), kind=kLoop, calls=%fused_computation.35 | loop fusion | flops 38912 | bytes 321024 | tf_op jit(solution)/shard_map/mul | solution.py:287
  21.4 1.0 dynamic-slice_bitcast_fusion.27
  22.4 1.0 collective-permute-start.19
  23.5 0.0 collective-permute-done.15.refs_2_
  23.5 1.2 collective-permute-start.20
  24.6 0.0 collective-permute-done.16.refs_3_
  24.6 15.0 %collective-permute-start.10 = (f32[2,32,768]{2,1,0:T(8,128)}, f32[2,32,768]{2,1,0:T(8,128)S(1)}, u32[]{:S(2)}, u32[]{:S(2)}) collective-permute-start(f32[2,32,768]{2,1,0:T(8,128)} %get-tuple-element.17), channel_id=1, source_target_pairs={{0,16},{4,20},{8,24},{12,28},{16,0},{20,4},{24,8},{28,12},{1,17},{... | collective-permute-start | bytes 589832 | tf_op jit(solution)/shard_map/ppermute | solution.py:23
  39.6 6.9 %collective-permute-done.17.refs_4_ = f32[2,32,768]{2,1,0:T(8,128)S(1)} collective-permute-done((f32[2,32,768]{2,1,0:T(8,128)}, f32[2,32,768]{2,1,0:T(8,128)S(1)}, u32[]{:S(2)}, u32[]{:S(2)}) %collective-permute-start.17) | collective-permute-done | bytes 196640 | tf_op jit(solution)/shard_map/ppermute | solution.py:23
  46.6 3.9 %collective-permute-done.18.refs_5_ = f32[2,32,768]{2,1,0:T(8,128)S(1)} collective-permute-done((f32[2,32,768]{2,1,0:T(8,128)}, f32[2,32,768]{2,1,0:T(8,128)S(1)}, u32[]{:S(2)}, u32[]{:S(2)}) %collective-permute-start.18) | collective-permute-done | bytes 196640 | tf_op jit(solution)/shard_map/ppermute | solution.py:23
  50.5 4.2 %collective-permute-start.7 = (f32[2,32,768]{2,1,0:T(8,128)}, f32[2,32,768]{2,1,0:T(8,128)S(1)}, u32[]{:S(2)}, u32[]{:S(2)}) collective-permute-start(f32[2,32,768]{2,1,0:T(8,128)} %get-tuple-element.20), channel_id=1, source_target_pairs={{0,28},{4,0},{8,4},{12,8},{16,12},{20,16},{24,20},{28,24},{1,29},{... | collective-permute-start | bytes 589832 | tf_op jit(solution)/shard_map/ppermute | solution.py:23
  54.7 0.0 collective-permute-done.10.refs_4_
  54.7 1.5 collective-permute-start.8
  56.2 9.0 %collective-permute-done.11.refs_5_ = f32[2,32,768]{2,1,0:T(8,128)S(1)} collective-permute-done((f32[2,32,768]{2,1,0:T(8,128)}, f32[2,32,768]{2,1,0:T(8,128)S(1)}, u32[]{:S(2)}, u32[]{:S(2)}) %collective-permute-start.11) | collective-permute-done | bytes 196640 | tf_op jit(solution)/shard_map/ppermute | solution.py:23
  65.2 0.0 collective-permute-done.12.refs_6_
  65.2 0.0 collective-permute-start.1
  65.2 0.0 collective-permute-done.13.refs_7_
  65.2 16.1 %collective-permute-start.2 = (f32[2,32,896]{2,1,0:T(8,128)S(1)}, f32[2,32,896]{2,1,0:T(8,128)S(1)}, u32[]{:S(2)}, u32[]{:S(2)}) collective-permute-start(f32[2,32,896]{2,1,0:T(8,128)S(1)} %pad_maximum_fusion.3), channel_id=1, source_target_pairs={{0,20},{4,24},{8,28},{12,0},{16,4},{20,8},{24,12},{28,16},{1,21},{... | collective-permute-start | bytes 688136 | tf_op jit(solution)/shard_map/ppermute | solution.py:23
  81.4 0.0 collective-permute-done.7.refs_1_
  81.4 14.1 %collective-permute-start.3 = (f32[2,32,896]{2,1,0:T(8,128)S(1)}, f32[2,32,896]{2,1,0:T(8,128)S(1)}, u32[]{:S(2)}, u32[]{:S(2)}) collective-permute-start(f32[2,32,896]{2,1,0:T(8,128)S(1)} %pad_maximum_fusion.4), channel_id=1, source_target_pairs={{0,16},{4,20},{8,24},{12,28},{16,0},{20,4},{24,8},{28,12},{1,17},{... | collective-permute-start | bytes 688136 | tf_op jit(solution)/shard_map/ppermute | solution.py:23
  95.5 0.0 collective-permute-done.8.refs_2_
  95.5 2.4 %collective-permute-start.4 = (f32[2,32,896]{2,1,0:T(8,128)S(1)}, f32[2,32,896]{2,1,0:T(8,128)S(1)}, u32[]{:S(2)}, u32[]{:S(2)}) collective-permute-start(f32[2,32,896]{2,1,0:T(8,128)S(1)} %pad_maximum_fusion.5), channel_id=1, source_target_pairs={{0,12},{4,16},{8,20},{12,24},{16,28},{20,0},{24,4},{28,8},{1,13},{... | collective-permute-start | bytes 688136 | tf_op jit(solution)/shard_map/ppermute | solution.py:23
  97.8 0.0 collective-permute-done.9.refs_3_
  97.8 0.0 collective-permute-start.5
  97.8 0.0 collective-permute-done.1.refs_2_
  97.9 0.3 collective-permute-start.6
  98.2 8.9 %collective-permute-done.2.refs_3_ = f32[2,32,896]{2,1,0:T(8,128)S(1)} collective-permute-done((f32[2,32,896]{2,1,0:T(8,128)S(1)}, f32[2,32,896]{2,1,0:T(8,128)S(1)}, u32[]{:S(2)}, u32[]{:S(2)}) %collective-permute-start.2) | collective-permute-done | bytes 229408 | tf_op jit(solution)/shard_map/ppermute | solution.py:23
  107.0 0.0 collective-permute-start
  107.2 4.6 %shard_map.37.refs_10_ = f32[8,64,128]{2,1,0:T(8,128)S(1)} custom-call(f32[2,32,768]{2,1,0:T(8,128)S(1)} %get-tuple-element.13.refs_0_, f32[2,32,768]{2,1,0:T(8,128)S(1)} %collective-permute-done.14.refs_1_, f32[2,32,768]{2,1,0:T(8,128)S(1)} %collective-permute-done.15.refs_2_, f32[2,32,768]{2,1,0:T(8,128)S(1)} %collective-permute-done.16.refs_3_, ...), custom_call_target="tpu_custom_call" | custom-call | flops 402653184 | bytes 1572864 | tf_op jit(solution)/shard_map/pallas_call | solution.py:158
  111.8 4.6 %shard_map.38.refs_10_ = f32[8,64,128]{2,1,0:T(8,128)S(1)} custom-call(f32[2,32,768]{2,1,0:T(8,128)S(1)} %get-tuple-element.21.refs_0_, f32[2,32,768]{2,1,0:T(8,128)S(1)} %collective-permute-done.7.refs_1_, f32[2,32,768]{2,1,0:T(8,128)S(1)} %collective-permute-done.8.refs_2_, f32[2,32,768]{2,1,0:T(8,128)S(1)} %collective-permute-done.9.refs_3_, ...), custom_call_target="tpu_custom_call" | custom-call | flops 402653184 | bytes 1572864 | tf_op jit(solution)/shard_map/pallas_call | solution.py:158
  116.3 9.5 %collective-permute-done.3.refs_4_ = f32[2,32,896]{2,1,0:T(8,128)S(1)} collective-permute-done((f32[2,32,896]{2,1,0:T(8,128)S(1)}, f32[2,32,896]{2,1,0:T(8,128)S(1)}, u32[]{:S(2)}, u32[]{:S(2)}) %collective-permute-start.3) | collective-permute-done | bytes 229408 | tf_op jit(solution)/shard_map/ppermute | solution.py:23
  125.9 0.7 collective-permute-done.6.refs_7_
  126.6 5.6 %collective-permute-done.refs_1_ = f32[2,32,896]{2,1,0:T(8,128)S(1)} collective-permute-done((f32[2,32,896]{2,1,0:T(8,128)S(1)}, f32[2,32,896]{2,1,0:T(8,128)S(1)}, u32[]{:S(2)}, u32[]{:S(2)}) %collective-permute-start) | collective-permute-done | bytes 229408 | tf_op jit(solution)/shard_map/ppermute | solution.py:23
  132.2 4.9 %shard_map.39.total_ref = f32[8,64,128]{2,1,0:T(8,128)S(1)} custom-call(f32[2,32,896]{2,1,0:T(8,128)S(1)} %pad_maximum_fusion.refs_0_, f32[2,32,896]{2,1,0:T(8,128)S(1)} %collective-permute-done.refs_1_, f32[2,32,896]{2,1,0:T(8,128)S(1)} %collective-permute-done.1.refs_2_, f32[2,32,896]{2,1,0:T(8,128)S(1)} %collective-permute-done.2.refs_3_, ...), custom_call_target="tpu_custom_call" | custom-call | flops 469762048 | bytes 1835008 | tf_op jit(solution)/shard_map/pallas_call | solution.py:158
  137.1 0.7 copy-done
  137.8 2.4 %shard_map.40 = f32[2,4,2,32,128]{4,3,2,1,0:T(8,128)} custom-call(f32[8,64,128]{2,1,0:T(8,128)} %copy-done), custom_call_target="tpu_custom_call" | custom-call | tf_op jit(solution)/shard_map/pallas_call | solution.py:214
  140.2 0.9 slice_bitcast_fusion
  141.1 0.1 collective-permute-start.21
  141.2 4.4 %collective-permute-done.21 = f32[4,2,32,128]{3,2,1,0:T(8,128)S(1)} collective-permute-done((f32[4,2,32,128]{3,2,1,0:T(8,128)S(1)}, f32[4,2,32,128]{3,2,1,0:T(8,128)S(1)}, u32[]{:S(2)}, u32[]{:S(2)}) %collective-permute-start.21) | collective-permute-done | bytes 131104 | tf_op jit(solution)/shard_map/ppermute | solution.py:258
  145.6 0.9 fusion.1
  146.5 0.1 collective-permute-start.22
  146.6 0.1 collective-permute-start.23
  146.7 3.2 %collective-permute-start.24 = (f32[2,32,128]{2,1,0:T(8,128)S(1)}, f32[2,32,128]{2,1,0:T(8,128)S(1)}, u32[]{:S(2)}, u32[]{:S(2)}) collective-permute-start(f32[2,32,128]{2,1,0:T(8,128)S(1)} %get-tuple-element.44), channel_id=1, source_target_pairs={{0,24},{4,28},{8,0},{12,4},{16,8},{20,12},{24,16},{28,20},{1,25},{... | collective-permute-start | bytes 98312 | tf_op jit(solution)/shard_map/ppermute | solution.py:23
  149.9 1.3 collective-permute-done.22
  151.2 0.3 collective-permute-done.24
  151.5 4.3 %collective-permute-start.25 = (f32[2,32,128]{2,1,0:T(8,128)S(1)}, f32[2,32,128]{2,1,0:T(8,128)S(1)}, u32[]{:S(2)}, u32[]{:S(2)}) collective-permute-start(f32[2,32,128]{2,1,0:T(8,128)S(1)} %bitcast_add_fusion.refs_0_), channel_id=1, source_target_pairs={{0,1},{1,2},{2,3},{3,0},{4,5},{5,6},{6,7},{7,4},{8,9},{9,10},{10,1... | collective-permute-start | bytes 98312 | tf_op jit(solution)/shard_map/ppermute | solution.py:23
  155.8 0.3 collective-permute-start.26
  156.1 0.2 collective-permute-start.27
  156.3 0.6 collective-permute-done.25.refs_1_
  156.9 1.7 %collective-permute-done.26.refs_2_ = f32[2,32,128]{2,1,0:T(8,128)S(1)} collective-permute-done((f32[2,32,128]{2,1,0:T(8,128)S(1)}, f32[2,32,128]{2,1,0:T(8,128)S(1)}, u32[]{:S(2)}, u32[]{:S(2)}) %collective-permute-start.26) | collective-permute-done | bytes 32800 | tf_op jit(solution)/shard_map/ppermute | solution.py:23
  158.6 0.8 collective-permute-done.27.refs_3_
  159.4 0.6 copy-done.4
  160.0 1.6 shard_map.41
  (43 shorter events, 0.4 us)
Async XLA Ops:
  0.0 12.1 %copy-start.6 = (f32[2,3]{1,0:T(2,128)S(1)}, f32[2,3]{1,0:T(2,128)}, u32[]{:S(2)}) copy-start(f32[2,3]{1,0:T(2,128)} %param.4) | copy-start | bytes 76
  0.0 12.2 %copy-start.5 = (s32[8,2,3]{0,1,2:T(2,128)S(1)}, s32[8,2,3]{0,1,2:T(2,128)}, u32[]{:S(2)}) copy-start(s32[8,2,3]{0,1,2:T(2,128)} %param.5) | copy-start | bytes 580
  4.0 18.3 %collective-permute-start.14 = (f32[2,32,768]{2,1,0:T(8,128)}, f32[2,32,768]{2,1,0:T(8,128)S(1)}, u32[]{:S(2)}, u32[]{:S(2)}) collective-permute-start(f32[2,32,768]{2,1,0:T(8,128)} %get-tuple-element.12), channel_id=1, source_target_pairs={{0,28},{4,0},{8,4},{12,8},{16,12},{20,16},{24,20},{28,24},{1,29},{... | collective-permute-start | bytes 589832 | tf_op jit(solution)/shard_map/ppermute | solution.py:23
  9.2 14.3 %collective-permute-start.15 = (f32[2,32,768]{2,1,0:T(8,128)}, f32[2,32,768]{2,1,0:T(8,128)S(1)}, u32[]{:S(2)}, u32[]{:S(2)}) collective-permute-start(f32[2,32,768]{2,1,0:T(8,128)} %get-tuple-element.11), channel_id=1, source_target_pairs={{0,24},{4,28},{8,0},{12,4},{16,8},{20,12},{24,16},{28,20},{1,25},{... | collective-permute-start | bytes 589832 | tf_op jit(solution)/shard_map/ppermute | solution.py:23
  9.4 15.3 %collective-permute-start.16 = (f32[2,32,768]{2,1,0:T(8,128)}, f32[2,32,768]{2,1,0:T(8,128)S(1)}, u32[]{:S(2)}, u32[]{:S(2)}) collective-permute-start(f32[2,32,768]{2,1,0:T(8,128)} %get-tuple-element.10), channel_id=1, source_target_pairs={{0,20},{4,24},{8,28},{12,0},{16,4},{20,8},{24,12},{28,16},{1,21},{... | collective-permute-start | bytes 589832 | tf_op jit(solution)/shard_map/ppermute | solution.py:23
  9.4 37.2 %collective-permute-start.17 = (f32[2,32,768]{2,1,0:T(8,128)}, f32[2,32,768]{2,1,0:T(8,128)S(1)}, u32[]{:S(2)}, u32[]{:S(2)}) collective-permute-start(f32[2,32,768]{2,1,0:T(8,128)} %get-tuple-element.9), channel_id=1, source_target_pairs={{0,16},{4,20},{8,24},{12,28},{16,0},{20,4},{24,8},{28,12},{1,17},{... | collective-permute-start | bytes 589832 | tf_op jit(solution)/shard_map/ppermute | solution.py:23
  11.8 38.7 %collective-permute-start.18 = (f32[2,32,768]{2,1,0:T(8,128)}, f32[2,32,768]{2,1,0:T(8,128)S(1)}, u32[]{:S(2)}, u32[]{:S(2)}) collective-permute-start(f32[2,32,768]{2,1,0:T(8,128)} %get-tuple-element.8), channel_id=1, source_target_pairs={{0,12},{4,16},{8,20},{12,24},{16,28},{20,0},{24,4},{28,8},{1,13},{... | collective-permute-start | bytes 589832 | tf_op jit(solution)/shard_map/ppermute | solution.py:23
  22.4 28.1 %collective-permute-start.19 = (f32[2,32,768]{2,1,0:T(8,128)}, f32[2,32,768]{2,1,0:T(8,128)S(1)}, u32[]{:S(2)}, u32[]{:S(2)}) collective-permute-start(f32[2,32,768]{2,1,0:T(8,128)} %get-tuple-element.30), channel_id=1, source_target_pairs={{0,8},{4,12},{8,16},{12,20},{16,24},{20,28},{24,0},{28,4},{1,9},{5... | collective-permute-start | bytes 589832 | tf_op jit(solution)/shard_map/ppermute | solution.py:23
  23.5 27.1 %collective-permute-start.20 = (f32[2,32,768]{2,1,0:T(8,128)}, f32[2,32,768]{2,1,0:T(8,128)S(1)}, u32[]{:S(2)}, u32[]{:S(2)}) collective-permute-start(f32[2,32,768]{2,1,0:T(8,128)} %get-tuple-element.7), channel_id=1, source_target_pairs={{0,4},{4,8},{8,12},{12,16},{16,20},{20,24},{24,28},{28,0},{1,5},{5... | collective-permute-start | bytes 589832 | tf_op jit(solution)/shard_map/ppermute | solution.py:23
  24.6 30.1 %collective-permute-start.10 = (f32[2,32,768]{2,1,0:T(8,128)}, f32[2,32,768]{2,1,0:T(8,128)S(1)}, u32[]{:S(2)}, u32[]{:S(2)}) collective-permute-start(f32[2,32,768]{2,1,0:T(8,128)} %get-tuple-element.17), channel_id=1, source_target_pairs={{0,16},{4,20},{8,24},{12,28},{16,0},{20,4},{24,8},{28,12},{1,17},{... | collective-permute-start | bytes 589832 | tf_op jit(solution)/shard_map/ppermute | solution.py:23
  46.6 18.6 %collective-permute-start.11 = (f32[2,32,768]{2,1,0:T(8,128)}, f32[2,32,768]{2,1,0:T(8,128)S(1)}, u32[]{:S(2)}, u32[]{:S(2)}) collective-permute-start(f32[2,32,768]{2,1,0:T(8,128)} %get-tuple-element.16), channel_id=1, source_target_pairs={{0,12},{4,16},{8,20},{12,24},{16,28},{20,0},{24,4},{28,8},{1,13},{... | collective-permute-start | bytes 589832 | tf_op jit(solution)/shard_map/ppermute | solution.py:23
  50.5 14.8 %collective-permute-start.12 = (f32[2,32,768]{2,1,0:T(8,128)}, f32[2,32,768]{2,1,0:T(8,128)S(1)}, u32[]{:S(2)}, u32[]{:S(2)}) collective-permute-start(f32[2,32,768]{2,1,0:T(8,128)} %get-tuple-element.15), channel_id=1, source_target_pairs={{0,8},{4,12},{8,16},{12,20},{16,24},{20,28},{24,0},{28,4},{1,9},{5... | collective-permute-start | bytes 589832 | tf_op jit(solution)/shard_map/ppermute | solution.py:23
  50.5 14.8 %collective-permute-start.13 = (f32[2,32,768]{2,1,0:T(8,128)}, f32[2,32,768]{2,1,0:T(8,128)S(1)}, u32[]{:S(2)}, u32[]{:S(2)}) collective-permute-start(f32[2,32,768]{2,1,0:T(8,128)} %get-tuple-element.14), channel_id=1, source_target_pairs={{0,4},{4,8},{8,12},{12,16},{16,20},{20,24},{24,28},{28,0},{1,5},{5... | collective-permute-start | bytes 589832 | tf_op jit(solution)/shard_map/ppermute | solution.py:23
  50.5 30.8 %collective-permute-start.7 = (f32[2,32,768]{2,1,0:T(8,128)}, f32[2,32,768]{2,1,0:T(8,128)S(1)}, u32[]{:S(2)}, u32[]{:S(2)}) collective-permute-start(f32[2,32,768]{2,1,0:T(8,128)} %get-tuple-element.20), channel_id=1, source_target_pairs={{0,28},{4,0},{8,4},{12,8},{16,12},{20,16},{24,20},{28,24},{1,29},{... | collective-permute-start | bytes 589832 | tf_op jit(solution)/shard_map/ppermute | solution.py:23
  54.7 40.7 %collective-permute-start.8 = (f32[2,32,768]{2,1,0:T(8,128)}, f32[2,32,768]{2,1,0:T(8,128)S(1)}, u32[]{:S(2)}, u32[]{:S(2)}) collective-permute-start(f32[2,32,768]{2,1,0:T(8,128)} %get-tuple-element.19), channel_id=1, source_target_pairs={{0,24},{4,28},{8,0},{12,4},{16,8},{20,12},{24,16},{28,20},{1,25},{... | collective-permute-start | bytes 589832 | tf_op jit(solution)/shard_map/ppermute | solution.py:23
  65.2 32.6 %collective-permute-start.9 = (f32[2,32,768]{2,1,0:T(8,128)S(1)}, f32[2,32,768]{2,1,0:T(8,128)S(1)}, u32[]{:S(2)}, u32[]{:S(2)}) collective-permute-start(f32[2,32,768]{2,1,0:T(8,128)S(1)} %get-tuple-element.18), channel_id=1, source_target_pairs={{0,20},{4,24},{8,28},{12,0},{16,4},{20,8},{24,12},{28,16},{1,21},{... | collective-permute-start | bytes 589832 | tf_op jit(solution)/shard_map/ppermute | solution.py:23
  65.2 32.6 %collective-permute-start.1 = (f32[2,32,896]{2,1,0:T(8,128)S(1)}, f32[2,32,896]{2,1,0:T(8,128)S(1)}, u32[]{:S(2)}, u32[]{:S(2)}) collective-permute-start(f32[2,32,896]{2,1,0:T(8,128)S(1)} %pad_maximum_fusion.2), channel_id=1, source_target_pairs={{0,24},{4,28},{8,0},{12,4},{16,8},{20,12},{24,16},{28,20},{1,25},{... | collective-permute-start | bytes 688136 | tf_op jit(solution)/shard_map/ppermute | solution.py:23
  65.2 41.8 %collective-permute-start.2 = (f32[2,32,896]{2,1,0:T(8,128)S(1)}, f32[2,32,896]{2,1,0:T(8,128)S(1)}, u32[]{:S(2)}, u32[]{:S(2)}) collective-permute-start(f32[2,32,896]{2,1,0:T(8,128)S(1)} %pad_maximum_fusion.3), channel_id=1, source_target_pairs={{0,20},{4,24},{8,28},{12,0},{16,4},{20,8},{24,12},{28,16},{1,21},{... | collective-permute-start | bytes 688136 | tf_op jit(solution)/shard_map/ppermute | solution.py:23
  81.4 44.5 %collective-permute-start.3 = (f32[2,32,896]{2,1,0:T(8,128)S(1)}, f32[2,32,896]{2,1,0:T(8,128)S(1)}, u32[]{:S(2)}, u32[]{:S(2)}) collective-permute-start(f32[2,32,896]{2,1,0:T(8,128)S(1)} %pad_maximum_fusion.4), channel_id=1, source_target_pairs={{0,16},{4,20},{8,24},{12,28},{16,0},{20,4},{24,8},{28,12},{1,17},{... | collective-permute-start | bytes 688136 | tf_op jit(solution)/shard_map/ppermute | solution.py:23
  95.5 30.4 %collective-permute-start.4 = (f32[2,32,896]{2,1,0:T(8,128)S(1)}, f32[2,32,896]{2,1,0:T(8,128)S(1)}, u32[]{:S(2)}, u32[]{:S(2)}) collective-permute-start(f32[2,32,896]{2,1,0:T(8,128)S(1)} %pad_maximum_fusion.5), channel_id=1, source_target_pairs={{0,12},{4,16},{8,20},{12,24},{16,28},{20,0},{24,4},{28,8},{1,13},{... | collective-permute-start | bytes 688136 | tf_op jit(solution)/shard_map/ppermute | solution.py:23
  97.8 28.0 %collective-permute-start.5 = (f32[2,32,896]{2,1,0:T(8,128)S(1)}, f32[2,32,896]{2,1,0:T(8,128)S(1)}, u32[]{:S(2)}, u32[]{:S(2)}) collective-permute-start(f32[2,32,896]{2,1,0:T(8,128)S(1)} %pad_maximum_fusion.6), channel_id=1, source_target_pairs={{0,8},{4,12},{8,16},{12,20},{16,24},{20,28},{24,0},{28,4},{1,9},{5... | collective-permute-start | bytes 688136 | tf_op jit(solution)/shard_map/ppermute | solution.py:23
  97.9 28.7 %collective-permute-start.6 = (f32[2,32,896]{2,1,0:T(8,128)S(1)}, f32[2,32,896]{2,1,0:T(8,128)S(1)}, u32[]{:S(2)}, u32[]{:S(2)}) collective-permute-start(f32[2,32,896]{2,1,0:T(8,128)S(1)} %pad_maximum_fusion.7), channel_id=1, source_target_pairs={{0,4},{4,8},{8,12},{12,16},{16,20},{20,24},{24,28},{28,0},{1,5},{5... | collective-permute-start | bytes 688136 | tf_op jit(solution)/shard_map/ppermute | solution.py:23
  107.0 25.1 %collective-permute-start = (f32[2,32,896]{2,1,0:T(8,128)S(1)}, f32[2,32,896]{2,1,0:T(8,128)S(1)}, u32[]{:S(2)}, u32[]{:S(2)}) collective-permute-start(f32[2,32,896]{2,1,0:T(8,128)S(1)} %pad_maximum_fusion.1), channel_id=1, source_target_pairs={{0,28},{4,0},{8,4},{12,8},{16,12},{20,16},{24,20},{28,24},{1,29},{... | collective-permute-start | bytes 688136 | tf_op jit(solution)/shard_map/ppermute | solution.py:23
  137.1 0.7 copy-start
  141.1 4.5 %collective-permute-start.21 = (f32[4,2,32,128]{3,2,1,0:T(8,128)S(1)}, f32[4,2,32,128]{3,2,1,0:T(8,128)S(1)}, u32[]{:S(2)}, u32[]{:S(2)}) collective-permute-start(f32[4,2,32,128]{3,2,1,0:T(8,128)S(1)} %slice_bitcast_fusion), channel_id=1, source_target_pairs={{0,4},{4,0},{8,12},{12,8},{16,20},{20,16},{24,28},{28,24},{1,5},{5... | collective-permute-start | bytes 393224 | tf_op jit(solution)/shard_map/ppermute | solution.py:258
  146.5 4.6 %collective-permute-start.22 = (f32[2,32,128]{2,1,0:T(8,128)S(1)}, f32[2,32,128]{2,1,0:T(8,128)S(1)}, u32[]{:S(2)}, u32[]{:S(2)}) collective-permute-start(f32[2,32,128]{2,1,0:T(8,128)S(1)} %get-tuple-element.45), channel_id=1, source_target_pairs={{0,8},{4,12},{8,16},{12,20},{16,24},{20,28},{24,0},{28,4},{1,9},{5... | collective-permute-start | bytes 98312 | tf_op jit(solution)/shard_map/ppermute | solution.py:23
  146.6 4.6 %collective-permute-start.23 = (f32[2,32,128]{2,1,0:T(8,128)S(1)}, f32[2,32,128]{2,1,0:T(8,128)S(1)}, u32[]{:S(2)}, u32[]{:S(2)}) collective-permute-start(f32[2,32,128]{2,1,0:T(8,128)S(1)} %get-tuple-element.43), channel_id=1, source_target_pairs={{0,16},{4,20},{8,24},{12,28},{16,0},{20,4},{24,8},{28,12},{1,17},{... | collective-permute-start | bytes 98312 | tf_op jit(solution)/shard_map/ppermute | solution.py:23
  146.7 4.8 %collective-permute-start.24 = (f32[2,32,128]{2,1,0:T(8,128)S(1)}, f32[2,32,128]{2,1,0:T(8,128)S(1)}, u32[]{:S(2)}, u32[]{:S(2)}) collective-permute-start(f32[2,32,128]{2,1,0:T(8,128)S(1)} %get-tuple-element.44), channel_id=1, source_target_pairs={{0,24},{4,28},{8,0},{12,4},{16,8},{20,12},{24,16},{28,20},{1,25},{... | collective-permute-start | bytes 98312 | tf_op jit(solution)/shard_map/ppermute | solution.py:23
  151.5 7.9 %copy-start.1 = (f32[2,32,128]{2,1,0:T(8,128)}, f32[2,32,128]{2,1,0:T(8,128)S(1)}, u32[]{:S(2)}) copy-start(f32[2,32,128]{2,1,0:T(8,128)S(1)} %bitcast_add_fusion.refs_0_) | copy-start | bytes 98308
  151.5 5.3 %collective-permute-start.25 = (f32[2,32,128]{2,1,0:T(8,128)S(1)}, f32[2,32,128]{2,1,0:T(8,128)S(1)}, u32[]{:S(2)}, u32[]{:S(2)}) collective-permute-start(f32[2,32,128]{2,1,0:T(8,128)S(1)} %bitcast_add_fusion.refs_0_), channel_id=1, source_target_pairs={{0,1},{1,2},{2,3},{3,0},{4,5},{5,6},{6,7},{7,4},{8,9},{9,10},{10,1... | collective-permute-start | bytes 98312 | tf_op jit(solution)/shard_map/ppermute | solution.py:23
  155.8 2.8 %collective-permute-start.26 = (f32[2,32,128]{2,1,0:T(8,128)S(1)}, f32[2,32,128]{2,1,0:T(8,128)S(1)}, u32[]{:S(2)}, u32[]{:S(2)}) collective-permute-start(f32[2,32,128]{2,1,0:T(8,128)S(1)} %bitcast_add_fusion.refs_0_), channel_id=1, source_target_pairs={{0,2},{1,3},{2,0},{3,1},{4,6},{5,7},{6,4},{7,5},{8,10},{9,11},{10,... | collective-permute-start | bytes 98312 | tf_op jit(solution)/shard_map/ppermute | solution.py:23
  156.1 3.3 %collective-permute-start.27 = (f32[2,32,128]{2,1,0:T(8,128)S(1)}, f32[2,32,128]{2,1,0:T(8,128)S(1)}, u32[]{:S(2)}, u32[]{:S(2)}) collective-permute-start(f32[2,32,128]{2,1,0:T(8,128)S(1)} %bitcast_add_fusion.refs_0_), channel_id=1, source_target_pairs={{0,3},{1,0},{2,1},{3,2},{4,7},{5,4},{6,5},{7,6},{8,11},{9,8},{10,9... | collective-permute-start | bytes 98312 | tf_op jit(solution)/shard_map/ppermute | solution.py:23
  156.9 2.6 %copy-start.2 = (f32[2,32,128]{2,1,0:T(8,128)}, f32[2,32,128]{2,1,0:T(8,128)S(1)}, u32[]{:S(2)}) copy-start(f32[2,32,128]{2,1,0:T(8,128)S(1)} %collective-permute-done.25.refs_1_) | copy-start | bytes 98308
  158.6 0.8 copy-start.3
  159.4 0.6 copy-start.4

commit v2 on v1

--- a/solution.py
+++ b/solution.py
@@ -12,7 +12,8 @@
 GY = 40
 KX = 4
 LANES = 128
-CHUNKS = 3
+SHARES = (0.32, 0.32, 0.26, 0.10)
+AHEAD = 2
 
 two_pi = 2.0 * math.pi
 
@@ -29,6 +30,27 @@
         + q_vector[1] * ycoord / y_extent
         + q_vector[2] * zcoord / z_extent
     )
+
+
+def exchange(count):
+    if count & (count - 1) == 0:
+        half = count // 2
+        turns = [turn for low in range(half) for turn in (half + low, low) if turn]
+        return [functools.partial(lambda turn, me: me ^ turn, turn) for turn in turns]
+    turns = sorted(range(1, count), key=lambda turn: -min(turn, count - turn))
+    return [functools.partial(lambda turn, me: (me + turn) % count, turn) for turn in turns]
+
+
+def exchange_back(count):
+    if count & (count - 1) == 0:
+        return exchange(count)
+    turns = sorted(range(1, count), key=lambda turn: -min(turn, count - turn))
+    return [functools.partial(lambda turn, me: (me + count - turn) % count, turn) for turn in turns]
+
+
+def sent_round(value, to):
+    pairs = [(source, to(source)) for source in range(lax.axis_size("ka"))]
+    return lax.ppermute(value, "ka", pairs)
 
 
 class Parts:
@@ -62,17 +84,16 @@
         number = jnp.minimum(number, self.components * self.rest - 1)
         return number // self.rest, self.main * self.count + number % self.rest, valid
 
-    def take(self, field, part, start, stop):
-        bands = field.shape[2]
-        found = []
+    def runs(self, part, start, stop):
+        found, place = [], 0
         for component, tile, length in self.pieces(start, stop):
             if component is None:
-                which, at, _ = self.extra_unit(part, tile)
-                origin = (0, which, 0, at * LANES)
+                component, at, _ = self.extra_unit(part, tile)
             else:
-                origin = (0, component, 0, (part * self.main + tile) * LANES)
-            found.append(lax.dynamic_slice(field, origin, (2, 1, bands, length * LANES))[:, 0])
-        return found[0] if len(found) == 1 else jnp.concatenate(found, axis=2)
+                at = part * self.main + tile
+            found.append((component, pl.multiple_of(at * LANES, LANES), place, length * LANES))
+            place += length * LANES
+        return found
 
     def cell_index(self, part, start, stop):
         cells, valid = [], []
@@ -89,23 +110,108 @@
         return jnp.concatenate(cells), jnp.concatenate(valid)
 
 
+def chunk_bounds(units):
+    bounds = [0]
+    for chunk in range(1, len(SHARES) + 1):
+        bound = round(units * sum(SHARES[:chunk]))
+        if bound > bounds[-1]:
+            bounds.append(bound)
+    return bounds
+
+
 def split_parts(value):
     high = value.astype(jnp.bfloat16)
     low = (value - high.astype(jnp.float32)).astype(jnp.bfloat16)
     return high, low
 
 
-def chunk_kernel(count, offsets, first, *refs):
-    blocks = refs[:count]
-    cosine_ref, sine_ref = refs[count], refs[count + 1]
-    rest = refs[count + 2 :]
-    if first:
-        total_ref, held, sems = rest
-        before_ref = None
+def copies_of(parts, field_ref, part, start, stop, out_ref, sems, first_sem):
+    copies = []
+    for number, (component, origin, place, cells) in enumerate(parts.runs(part, start, stop)):
+        copies.append(
+            pltpu.make_async_copy(
+                field_ref.at[:, component, :, pl.ds(origin, cells)],
+                out_ref.at[:, :, pl.ds(place, cells)],
+                sems.at[first_sem + number],
+            )
+        )
+    return copies
+
+
+def pack_kernel(parts, targets, start, stop, field_ref, *refs):
+    outs, sems = refs[:-1], refs[-1]
+    me = lax.axis_index("ka")
+    copies = []
+    for to, out_ref in zip(targets, outs):
+        part = to(me)
+        copies += copies_of(parts, field_ref, part, start, stop, out_ref, sems, len(copies))
+    for copy in copies:
+        copy.start()
+    for copy in copies:
+        copy.wait()
+
+
+def pack(parts, field, targets, start, stop):
+    shape = (2, field.shape[2], (stop - start) * LANES)
+    anywhere = pl.BlockSpec(memory_space=pl.ANY)
+    size = 4 * math.prod(shape) * len(targets)
+    return pl.pallas_call(
+        functools.partial(pack_kernel, parts, targets, start, stop),
+        out_shape=[jax.ShapeDtypeStruct(shape, jnp.float32)] * len(targets),
+        in_specs=[anywhere],
+        out_specs=[pl.BlockSpec(memory_space=pltpu.VMEM)] * len(targets),
+        scratch_shapes=[
+            pltpu.SemaphoreType.DMA((len(targets) * len(parts.pieces(start, stop)),)),
+        ],
+        compiler_params=pltpu.CompilerParams(vmem_limit_bytes=4 * 1024 * 1024),
+        cost_estimate=pl.CostEstimate(flops=0, bytes_accessed=2 * size, transcendentals=0),
+    )(field)
+
+
+def write_messages(count, offsets, factor, total_ref, out_refs, forward):
+    me = lax.axis_index("ka")
+    bands = total_ref.shape[1] // 2
+    width = total_ref.shape[2]
+    lane = lax.broadcasted_iota(jnp.int32, (bands, width), 1)
+    real_lane = lane % (2 * bands) < bands
+    for step in range(count):
+        with_real = total_ref[step, :bands]
+        with_imag = total_ref[step, bands:]
+        after = pltpu.roll(with_imag, width - bands, 1)
+        ahead = pltpu.roll(with_imag, bands, 1)
+        forward[step] = with_real + jnp.where(real_lane, after, -ahead)
+    for step in range(count):
+        turn = lax.rem(step % factor + factor - lax.rem(me, factor), factor)
+        group = step // factor
+        back = jnp.zeros((bands, width), jnp.float32)
+        for direction, offset in enumerate(offsets):
+            other = forward[(step + count - offset) % count]
+            back = jnp.where(lane // (2 * bands) == direction, other, back)
+        for place, out_ref in enumerate(out_refs):
+
+            @pl.when(turn == place)
+            def _():
+                out_ref[group, 0] = forward[step]
+                out_ref[group, 1] = back
+
+
+def chunk_kernel(parts, offsets, start, stop, factor, *refs):
+    count = parts.count
+    blocks, refs = refs[:count], refs[count:]
+    (cosine_ref, sine_ref), refs = refs[:2], refs[2:]
+    before_ref = None
+    if start > 0:
+        before_ref, refs = refs[0], refs[1:]
+    last = stop == parts.units
+    if last:
+        outs, (held, sems, total_ref, forward) = refs[:factor], refs[factor:]
     else:
-        before_ref, total_ref, held, sems = rest
+        total_ref, held, sems = refs
+    me = lax.axis_index("ka")
+    sources = [lambda place: place] + exchange_back(count)
     copies = [
-        pltpu.make_async_copy(blocks[step], held.at[step], sems.at[step]) for step in range(count)
+        pltpu.make_async_copy(block, held.at[source(me)], sems.at[number])
+        for number, (block, source) in enumerate(zip(blocks, sources))
     ]
     for copy in copies:
         copy.start()
@@ -138,14 +244,18 @@
         half = product.shape[1] // 2
         rows = product[: 2 * bands] + product[2 * bands :]
         summed = rows[:, :half] + rows[:, half:]
-        if not first:
+        if before_ref is not None:
             summed = summed + before_ref[step]
         total_ref[step] = summed
 
-
-def chunk_products(blocks, cosine, sine, before, offsets):
-    count = len(blocks)
-    _, bands, cells = blocks[0].shape
+    if last:
+        write_messages(count, offsets, factor, total_ref, outs, forward)
+
+
+def chunk_products(parts, blocks, cosine, sine, before, offsets, start, stop, factor):
+    count = parts.count
+    bands = blocks[0].shape[1]
+    cells = (stop - start) * LANES
     width = 2 * len(offsets) * bands
     operands = list(blocks) + [cosine, sine]
     anywhere = pl.BlockSpec(memory_space=pl.ANY)
@@ -154,17 +264,28 @@
     if before is not None:
         operands.append(before)
         in_specs.append(inside)
+    total_shape = (count, 2 * bands, width)
+    scratch = [
+        pltpu.VMEM((count, 2, bands, cells), jnp.float32),
+        pltpu.SemaphoreType.DMA((count,)),
+    ]
+    if stop == parts.units:
+        message = jax.ShapeDtypeStruct((count // factor, 2, bands, width), jnp.float32)
+        out_shape, out_specs = [message] * factor, [inside] * factor
+        scratch += [
+            pltpu.VMEM(total_shape, jnp.float32),
+            pltpu.VMEM((count, bands, width), jnp.float32),
+        ]
+    else:
+        out_shape, out_specs = jax.ShapeDtypeStruct(total_shape, jnp.float32), inside
     flops = 2 * count * (4 * bands) * (2 * width) * cells
     return pl.pallas_call(
-        functools.partial(chunk_kernel, count, offsets, before is None),
-        out_shape=jax.ShapeDtypeStruct((count, 2 * bands, width), jnp.float32),
+        functools.partial(chunk_kernel, parts, offsets, start, stop, factor),
+        out_shape=out_shape,
         in_specs=in_specs,
-        out_specs=inside,
-        scratch_shapes=[
-            pltpu.VMEM((count, 2, bands, cells), jnp.float32),
-            pltpu.SemaphoreType.DMA((count,)),
-        ],
-        compiler_params=pltpu.CompilerParams(vmem_limit_bytes=32 * 1024 * 1024),
+        out_specs=out_specs,
+        scratch_shapes=scratch,
+        compiler_params=pltpu.CompilerParams(vmem_limit_bytes=12 * 1024 * 1024),
         cost_estimate=pl.CostEstimate(
             flops=flops, bytes_accessed=4 * count * 2 * bands * cells, transcendentals=0
         ),
@@ -177,47 +298,6 @@
         if count % factor == 0:
             best = factor
     return best
-
-
-def messages_kernel(count, offsets, factor, total_ref, out_ref, forward):
-    me = lax.axis_index("ka")
-    bands = total_ref.shape[1] // 2
-    width = total_ref.shape[2]
-    lane = lax.broadcasted_iota(jnp.int32, (bands, width), 1)
-    real_lane = lane % (2 * bands) < bands
-
-    @pl.loop(0, count)
-    def _(step):
-        with_real = total_ref[step, :bands]
-        with_imag = total_ref[step, bands:]
-        after = pltpu.roll(with_imag, width - bands, 1)
-        ahead = pltpu.roll(with_imag, bands, 1)
-        forward[step] = with_real + jnp.where(real_lane, after, -ahead)
-
-    @pl.loop(0, count)
-    def _(step):
-        target = lax.rem(me + step, count)
-        low = lax.rem(target, factor) + factor - lax.rem(me, factor)
-        turn = lax.rem(low, factor)
-        group = target // factor
-        out_ref[turn, group, 0] = forward[step]
-        back = jnp.zeros((bands, width), jnp.float32)
-        for direction, offset in enumerate(offsets):
-            other = forward[lax.rem(step + count - offset, count)]
-            back = jnp.where(lane // (2 * bands) == direction, other, back)
-        out_ref[turn, group, 1] = back
-
-
-def messages(total, offsets, factor):
-    count, rows, width = total.shape
-    inside = pl.BlockSpec(memory_space=pltpu.VMEM)
-    return pl.pallas_call(
-        functools.partial(messages_kernel, count, offsets, factor),
-        out_shape=jax.ShapeDtypeStruct((factor, count // factor, 2, rows // 2, width), jnp.float32),
-        in_specs=[inside],
-        out_specs=inside,
-        scratch_shapes=[pltpu.VMEM((count, rows // 2, width), jnp.float32)],
-    )(total)
 
 
 def result_kernel(*refs):
@@ -243,11 +323,12 @@
         out_shape=jax.ShapeDtypeStruct((width // bands, 2, bands, bands), jnp.float32),
         in_specs=[inside] * len(shares),
         out_specs=inside,
+        compiler_params=pltpu.CompilerParams(vmem_limit_bytes=2 * 1024 * 1024),
     )(*shares)
 
 
 def reduced_over_points(blocks, factor):
-    groups = blocks.shape[1]
+    groups = blocks[0].shape[0]
     me = lax.axis_index("ka")
     count = lax.axis_size("ka")
     total = blocks[0]
@@ -282,25 +363,31 @@
     ycoord = (cell_index // GX % GY).astype(jnp.float32)
     zcoord = (lax.axis_index("gz") * slab_depth + cell_index // plane_cells).astype(jnp.float32)
     shifts_float = gshift.astype(jnp.float32)
-    q_vectors = jnp.roll(bvectors[None] + shifts_float, -me, axis=0).reshape(-1, 3)
+    q_vectors = (bvectors[None] + shifts_float).reshape(-1, 3)
     angles = phase_angle(q_vectors.T[:, :, None], xcoord, ycoord, zcoord, GX, GY, z_extent)
     cosine = (jnp.cos(angles) * valid)[:, None]
     sine = (jnp.sin(angles) * valid)[:, None]
 
-    order = sorted(range(1, count), key=lambda step: -min(step, count - step))
-    bounds = [parts.units * chunk // CHUNKS for chunk in range(CHUNKS + 1)]
-    total = None
-    for start, stop in zip(bounds[:-1], bounds[1:]):
-        blocks = [None] * count
-        for step in order:
-            sent = parts.take(field, (me + count - step) % count, start, stop)
-            blocks[step] = shifted(sent, "ka", -step)
-        blocks[0] = parts.take(field, me, start, stop)
+    rounds = exchange(count)
+    factor = block_factor(count)
+    bounds = chunk_bounds(parts.units)
+    totals = []
+    for chunk, (start, stop) in enumerate(zip(bounds[:-1], bounds[1:])):
+        source = field
+        if chunk >= AHEAD:
+            source, totals[chunk - AHEAD] = lax.optimization_barrier((field, totals[chunk - AHEAD]))
+        own, *sent = pack(parts, source, [lambda place: place] + rounds, start, stop)
+        blocks = [own] + [sent_round(value, to) for value, to in zip(sent, rounds)]
         lanes = slice(start * LANES, stop * LANES)
-        total = chunk_products(blocks, cosine[:, :, lanes], sine[:, :, lanes], total, offsets)
-
-    factor = block_factor(count)
-    share = reduced_over_points(messages(total, offsets, factor), factor)
+        before = totals[-1] if totals else None
+        totals.append(
+            chunk_products(
+                parts, blocks, cosine[:, :, lanes], sine[:, :, lanes], before,
+                offsets, start, stop, factor,
+            )
+        )
+
+    share = reduced_over_points(totals[-1], factor)
     shares = [share] + [shifted(share, "gz", step) for step in range(1, slabs)]
     return result(shares)[None]
 

time: 162 us -> 143 us (0.88)
  waiting for transfers between devices: 53.6 us -> 33.3 us
  starting transfers between devices: 71.7 us -> 76.1 us
  local copies, waits for them, and re-layouts: 7.59 us -> 5.2 us
    ppermute x0 -> x28, starting transfers between devices: none -> 65.8 us  [sent_round(): return lax.ppermute(value, 'ka', pairs)]
    ppermute x27 -> x6, starting transfers between devices: 71.6 us -> 9.53 us  [shifted(): return lax.ppermute(value, axis, pairs)]
    ppermute x27 -> x6, waiting for transfers between devices: 49.3 us -> 6.39 us  [shifted(): return lax.ppermute(value, axis, pairs)]
    ppermute x0 -> x28, waiting for transfers between devices: none -> 23.8 us  [sent_round(): return lax.ppermute(value, 'ka', pairs)]
    squeeze x3 -> x0, local copies, waits for them, and re-layouts: 5.9 us -> none  [the longest x2 4.99 us: take(): lax.dynamic_slice(field, origin, (2, 1, bands, length * LANES))[:, 0]]
    unnamed x15 -> x13, local copies, waits for them, and re-layouts: 1.4 us -> 4.9 us
    pallas_call x4 -> x8, Pallas kernels: 16.4 us -> 17 us  [the longest x4 15.6 us: chunk_products(): pl.pallas_call(functools.partial(chunk_kernel, parts, offsets, start, sto...]
  transfers between devices with their start and end apart: 28 -> 35, of which waited for: 13 -> 15; matrix products, arithmetic and copies ran while one was open for 6% -> 6% of each run, Pallas kernels for 6% -> 10%
where the time goes in v2:
time: 143 us; the launch traced here: 141 us
  starting transfers between devices  76.1 us (53%)
  waiting for transfers between devices  33.3 us (23%)
  Pallas kernels  17.8 us (12%)
  other arithmetic  8.81 us (6%)
  local copies, waits for them, and re-layouts  5.2 us (4%)
    ppermute x28, starting transfers between devices, sent_round(): return lax.ppermute(value, 'ka', pairs)  65.8 us
    ppermute x28, waiting for transfers between devices, sent_round(): return lax.ppermute(value, 'ka', pairs)  23.8 us
    pallas_call x4, Pallas kernels, chunk_products(): pl.pallas_call(functools.partial(chunk_kernel, parts, offsets, start, sto...  15.6 us
    ppermute x6, starting transfers between devices, shifted(): return lax.ppermute(value, axis, pairs)  9.53 us
    ppermute x6, waiting for transfers between devices, shifted(): return lax.ppermute(value, axis, pairs)  6.39 us
    unnamed x13, local copies, waits for them, and re-layouts  4.9 us
    mul x1, other arithmetic, per_device(): sine = (jnp.sin(angles) * valid)[:, None]  4.62 us
    mul x1, other arithmetic, per_device(): cosine = (jnp.cos(angles) * valid)[:, None]  4.03 us
  transfers between devices with their start and end apart: 35, of which 15 were waited for; matrix products, arithmetic and copies ran while one was open for 6% of the time, Pallas kernels for 10%

profile of v2, /device:TPU:1, one launch (start us, length us, event | category | flops | bytes accessed | tf_op | source)
XLA Modules:
  0.0 141.4 jit_solution(561951677614928649)
XLA Ops:
  0.0 2.4 %copy-done = f32[1,2,32,3,6400]{4,2,3,1,0:T(8,128)S(1)} copy-done((f32[1,2,32,3,6400]{4,2,3,1,0:T(8,128)S(1)}, f32[1,2,32,3,6400]{4,2,3,1,0:T(8,128)}, u32[]{:S(2)}) %copy-start) | copy-done | bytes 4915224
  2.4 0.3 shard_map.38
  2.8 3.2 %collective-permute-start.7 = (f32[2,32,768]{2,1,0:T(8,128)S(1)}, f32[2,32,768]{2,1,0:T(8,128)S(1)}, u32[]{:S(2)}, u32[]{:S(2)}) collective-permute-start(f32[2,32,768]{2,1,0:T(8,128)S(1)} %get-tuple-element.50), channel_id=1, source_target_pairs={{0,16},{4,20},{8,24},{12,28},{16,0},{20,4},{24,8},{28,12},{1,17},{... | collective-permute-start | bytes 589832 | tf_op jit(solution)/shard_map/ppermute | solution.py:53
  6.0 1.0 collective-permute-start.8
  7.0 0.2 collective-permute-start.9
  7.2 3.3 %collective-permute-start.10 = (f32[2,32,768]{2,1,0:T(8,128)S(1)}, f32[2,32,768]{2,1,0:T(8,128)S(1)}, u32[]{:S(2)}, u32[]{:S(2)}) collective-permute-start(f32[2,32,768]{2,1,0:T(8,128)S(1)} %get-tuple-element.53), channel_id=1, source_target_pairs={{0,24},{4,28},{8,16},{12,20},{16,8},{20,12},{24,0},{28,4},{1,25},{... | collective-permute-start | bytes 589832 | tf_op jit(solution)/shard_map/ppermute | solution.py:53
  10.5 0.0 collective-permute-start.11
  10.5 0.1 copy.8
  10.6 0.1 convert_add_fusion
  10.7 0.1 copy.9
  10.8 0.1 reshape.508
  11.0 4.6 %sine_multiply_fusion = (f32[16,1,2432]{2,1,0:T(1,128)S(1)}, f32[16,1,2432]{2,1,0:T(1,128)S(1)}) fusion(f32[2432]{0:T(1024)S(1)} %pad_maximum_fusion, f32[2432]{0:T(1024)S(1)} %get-tuple-element.88, f32[16]{0:T(128)S(1)} %get-tuple-element.90, f32[2432]{0:T(1024)S(1)} %get-tuple-element.87, f32[16]{0:T(128)S(1)} %get-tuple-element.91, ...), kind=kLoop, calls=%fused_computation.2 | loop fusion | flops 350208 | bytes 350400 | tf_op jit(solution)/shard_map/mul | solution.py:369
  15.6 0.0 copy-start.1
  15.6 2.4 %copy-done.1 = f32[1,2,32,3,6400]{4,2,3,1,0:T(8,128)S(1)} copy-done((f32[1,2,32,3,6400]{4,2,3,1,0:T(8,128)S(1)}, f32[1,2,32,3,6400]{4,2,3,1,0:T(8,128)}, u32[]{:S(2)}) %copy-start.1) | copy-done | bytes 4915224
  18.0 0.3 shard_map.37
  18.4 4.9 %collective-permute-done.7.refs_1_ = f32[2,32,768]{2,1,0:T(8,128)S(1)} collective-permute-done((f32[2,32,768]{2,1,0:T(8,128)S(1)}, f32[2,32,768]{2,1,0:T(8,128)S(1)}, u32[]{:S(2)}, u32[]{:S(2)}) %collective-permute-start.7) | collective-permute-done | bytes 196640 | tf_op jit(solution)/shard_map/ppermute | solution.py:53
  23.3 4.9 %collective-permute-start.12 = (f32[2,32,768]{2,1,0:T(8,128)S(1)}, f32[2,32,768]{2,1,0:T(8,128)S(1)}, u32[]{:S(2)}, u32[]{:S(2)}) collective-permute-start(f32[2,32,768]{2,1,0:T(8,128)S(1)} %get-tuple-element.55), channel_id=1, source_target_pairs={{0,28},{4,24},{8,20},{12,16},{16,12},{20,8},{24,4},{28,0},{1,29},{... | collective-permute-start | bytes 589832 | tf_op jit(solution)/shard_map/ppermute | solution.py:53
  28.2 0.0 collective-permute-done.8.refs_2_
  28.2 1.4 collective-permute-start.13
  29.6 0.0 collective-permute-done.9.refs_3_
  29.6 3.0 %collective-permute-start = (f32[2,32,768]{2,1,0:T(8,128)S(1)}, f32[2,32,768]{2,1,0:T(8,128)S(1)}, u32[]{:S(2)}, u32[]{:S(2)}) collective-permute-start(f32[2,32,768]{2,1,0:T(8,128)S(1)} %get-tuple-element.42), channel_id=1, source_target_pairs={{0,16},{4,20},{8,24},{12,28},{16,0},{20,4},{24,8},{28,12},{1,17},{... | collective-permute-start | bytes 589832 | tf_op jit(solution)/shard_map/ppermute | solution.py:53
  32.6 7.9 %collective-permute-start.1 = (f32[2,32,768]{2,1,0:T(8,128)S(1)}, f32[2,32,768]{2,1,0:T(8,128)S(1)}, u32[]{:S(2)}, u32[]{:S(2)}) collective-permute-start(f32[2,32,768]{2,1,0:T(8,128)S(1)} %get-tuple-element.43), channel_id=1, source_target_pairs={{0,20},{4,16},{8,28},{12,24},{16,4},{20,0},{24,12},{28,8},{1,21},{... | collective-permute-start | bytes 589832 | tf_op jit(solution)/shard_map/ppermute | solution.py:53
  40.5 4.0 %cosine_multiply_fusion = f32[16,1,2432]{2,1,0:T(1,128)S(1)} fusion(f32[16,1,2432]{2,1,0:T(1,128)S(1)} %get-tuple-element.78, f32[2432]{0:T(1024)S(1)} %pad_maximum_fusion), kind=kLoop, calls=%fused_computation.3 | loop fusion | flops 38912 | bytes 321024 | tf_op jit(solution)/shard_map/mul | solution.py:368
  44.5 1.3 collective-permute-start.2
  45.9 11.3 %collective-permute-start.4 = (f32[2,32,768]{2,1,0:T(8,128)S(1)}, f32[2,32,768]{2,1,0:T(8,128)S(1)}, u32[]{:S(2)}, u32[]{:S(2)}) collective-permute-start(f32[2,32,768]{2,1,0:T(8,128)S(1)} %get-tuple-element.46), channel_id=1, source_target_pairs={{0,8},{4,12},{8,0},{12,4},{16,24},{20,28},{24,16},{28,20},{1,9},{5... | collective-permute-start | bytes 589832 | tf_op jit(solution)/shard_map/ppermute | solution.py:53
  57.1 4.9 %collective-permute-start.5 = (f32[2,32,768]{2,1,0:T(8,128)S(1)}, f32[2,32,768]{2,1,0:T(8,128)S(1)}, u32[]{:S(2)}, u32[]{:S(2)}) collective-permute-start(f32[2,32,768]{2,1,0:T(8,128)S(1)} %get-tuple-element.47), channel_id=1, source_target_pairs={{0,28},{4,24},{8,20},{12,16},{16,12},{20,8},{24,4},{28,0},{1,29},{... | collective-permute-start | bytes 589832 | tf_op jit(solution)/shard_map/ppermute | solution.py:53
  62.0 1.4 collective-permute-start.6
  63.5 4.6 %shard_map.39.refs_10_ = f32[8,64,128]{2,1,0:T(8,128)S(1)} custom-call(f32[2,32,768]{2,1,0:T(8,128)S(1)} %get-tuple-element.49.refs_0_, f32[2,32,768]{2,1,0:T(8,128)S(1)} %collective-permute-done.7.refs_1_, f32[2,32,768]{2,1,0:T(8,128)S(1)} %collective-permute-done.8.refs_2_, f32[2,32,768]{2,1,0:T(8,128)S(1)} %collective-permute-done.9.refs_3_, ...), custom_call_target="tpu_custom_call" | custom-call | flops 402653184 | bytes 1572864 | tf_op jit(solution)/shard_map/pallas_call | solution.py:282
  68.1 0.3 shard_map.42
  68.4 3.1 %collective-permute-start.21 = (f32[2,32,640]{2,1,0:T(8,128)S(1)}, f32[2,32,640]{2,1,0:T(8,128)S(1)}, u32[]{:S(2)}, u32[]{:S(2)}) collective-permute-start(f32[2,32,640]{2,1,0:T(8,128)S(1)} %get-tuple-element.68), channel_id=1, source_target_pairs={{0,16},{4,20},{8,24},{12,28},{16,0},{20,4},{24,8},{28,12},{1,17},{... | collective-permute-start | bytes 491528 | tf_op jit(solution)/shard_map/ppermute | solution.py:53
  71.5 2.3 %collective-permute-start.22 = (f32[2,32,640]{2,1,0:T(8,128)S(1)}, f32[2,32,640]{2,1,0:T(8,128)S(1)}, u32[]{:S(2)}, u32[]{:S(2)}) collective-permute-start(f32[2,32,640]{2,1,0:T(8,128)S(1)} %get-tuple-element.69), channel_id=1, source_target_pairs={{0,20},{4,16},{8,28},{12,24},{16,4},{20,0},{24,12},{28,8},{1,21},{... | collective-permute-start | bytes 491528 | tf_op jit(solution)/shard_map/ppermute | solution.py:53
  73.8 0.5 collective-permute-done.6.refs_7_
  74.2 4.5 %shard_map.40.refs_10_ = f32[8,64,128]{2,1,0:T(8,128)S(1)} custom-call(f32[2,32,768]{2,1,0:T(8,128)S(1)} %get-tuple-element.41.refs_0_, f32[2,32,768]{2,1,0:T(8,128)S(1)} %collective-permute-done.refs_1_, f32[2,32,768]{2,1,0:T(8,128)S(1)} %collective-permute-done.1.refs_2_, f32[2,32,768]{2,1,0:T(8,128)S(1)} %collective-permute-done.2.refs_3_, ...), custom_call_target="tpu_custom_call" | custom-call | flops 402653184 | bytes 1572864 | tf_op jit(solution)/shard_map/pallas_call | solution.py:282
  78.8 0.4 shard_map.41
  79.2 10.8 %collective-permute-start.14 = (f32[2,32,256]{2,1,0:T(8,128)S(1)}, f32[2,32,256]{2,1,0:T(8,128)S(1)}, u32[]{:S(2)}, u32[]{:S(2)}) collective-permute-start(f32[2,32,256]{2,1,0:T(8,128)S(1)} %get-tuple-element.59), channel_id=1, source_target_pairs={{0,16},{4,20},{8,24},{12,28},{16,0},{20,4},{24,8},{28,12},{1,17},{... | collective-permute-start | bytes 196616 | tf_op jit(solution)/shard_map/ppermute | solution.py:53
  90.0 0.3 collective-permute-start.15
  90.3 0.9 collective-permute-start.23
  91.3 3.6 %collective-permute-done.14.refs_1_ = f32[2,32,256]{2,1,0:T(8,128)S(1)} collective-permute-done((f32[2,32,256]{2,1,0:T(8,128)S(1)}, f32[2,32,256]{2,1,0:T(8,128)S(1)}, u32[]{:S(2)}, u32[]{:S(2)}) %collective-permute-start.14) | collective-permute-done | bytes 65568 | tf_op jit(solution)/shard_map/ppermute | solution.py:53
  94.9 1.9 %collective-permute-done.15.refs_2_ = f32[2,32,256]{2,1,0:T(8,128)S(1)} collective-permute-done((f32[2,32,256]{2,1,0:T(8,128)S(1)}, f32[2,32,256]{2,1,0:T(8,128)S(1)}, u32[]{:S(2)}, u32[]{:S(2)}) %collective-permute-start.15) | collective-permute-done | bytes 65568 | tf_op jit(solution)/shard_map/ppermute | solution.py:53
  96.8 2.1 %collective-permute-start.26 = (f32[2,32,640]{2,1,0:T(8,128)S(1)}, f32[2,32,640]{2,1,0:T(8,128)S(1)}, u32[]{:S(2)}, u32[]{:S(2)}) collective-permute-start(f32[2,32,640]{2,1,0:T(8,128)S(1)} %get-tuple-element.73), channel_id=1, source_target_pairs={{0,28},{4,24},{8,20},{12,16},{16,12},{20,8},{24,4},{28,0},{1,29},{... | collective-permute-start | bytes 491528 | tf_op jit(solution)/shard_map/ppermute | solution.py:53
  98.9 0.7 collective-permute-start.27
  99.6 0.9 collective-permute-start.16
  100.6 1.4 %collective-permute-done.24.refs_4_ = f32[2,32,640]{2,1,0:T(8,128)S(1)} collective-permute-done((f32[2,32,640]{2,1,0:T(8,128)S(1)}, f32[2,32,640]{2,1,0:T(8,128)S(1)}, u32[]{:S(2)}, u32[]{:S(2)}) %collective-permute-start.24) | collective-permute-done | bytes 163872 | tf_op jit(solution)/shard_map/ppermute | solution.py:53
  102.0 0.2 collective-permute-start.17
  102.3 4.8 %collective-permute-done.25.refs_5_ = f32[2,32,640]{2,1,0:T(8,128)S(1)} collective-permute-done((f32[2,32,640]{2,1,0:T(8,128)S(1)}, f32[2,32,640]{2,1,0:T(8,128)S(1)}, u32[]{:S(2)}, u32[]{:S(2)}) %collective-permute-start.25) | collective-permute-done | bytes 163872 | tf_op jit(solution)/shard_map/ppermute | solution.py:53
  107.1 2.7 %collective-permute-done.26.refs_6_ = f32[2,32,640]{2,1,0:T(8,128)S(1)} collective-permute-done((f32[2,32,640]{2,1,0:T(8,128)S(1)}, f32[2,32,640]{2,1,0:T(8,128)S(1)}, u32[]{:S(2)}, u32[]{:S(2)}) %collective-permute-start.26) | collective-permute-done | bytes 163872 | tf_op jit(solution)/shard_map/ppermute | solution.py:53
  109.7 0.5 collective-permute-start.19
  110.2 3.0 %collective-permute-done.27.refs_7_ = f32[2,32,640]{2,1,0:T(8,128)S(1)} collective-permute-done((f32[2,32,640]{2,1,0:T(8,128)S(1)}, f32[2,32,640]{2,1,0:T(8,128)S(1)}, u32[]{:S(2)}, u32[]{:S(2)}) %collective-permute-start.27) | collective-permute-done | bytes 163872 | tf_op jit(solution)/shard_map/ppermute | solution.py:53
  113.3 3.9 %shard_map.43.refs_10_ = f32[8,64,128]{2,1,0:T(8,128)S(1)} custom-call(f32[2,32,640]{2,1,0:T(8,128)S(1)} %get-tuple-element.67.refs_0_, f32[2,32,640]{2,1,0:T(8,128)S(1)} %collective-permute-done.21.refs_1_, f32[2,32,640]{2,1,0:T(8,128)S(1)} %collective-permute-done.22.refs_2_, f32[2,32,640]{2,1,0:T(8,128)S(1)} %collective-permute-done.23.refs_3_, ...), custom_call_target="tpu_custom_call" | custom-call | flops 335544320 | bytes 1310720 | tf_op jit(solution)/shard_map/pallas_call | solution.py:282
  117.2 0.6 collective-permute-done.19.refs_6_
  117.8 0.3 collective-permute-done.20.refs_7_
  118.2 2.6 %shard_map.44 = (f32[4,2,32,128]{3,2,1,0:T(8,128)S(1)}, f32[4,2,32,128]{3,2,1,0:T(8,128)S(1)}) custom-call(f32[2,32,256]{2,1,0:T(8,128)S(1)} %get-tuple-element.58.refs_0_, f32[2,32,256]{2,1,0:T(8,128)S(1)} %collective-permute-done.14.refs_1_, f32[2,32,256]{2,1,0:T(8,128)S(1)} %collective-permute-done.15.refs_2_, ...), custom_call_target="tpu_custom_call" | custom-call | flops 134217728 | bytes 524288 | tf_op jit(solution)/shard_map/pallas_call | solution.py:282
  120.8 0.7 collective-permute-start.28
  121.5 3.1 %collective-permute-done.28 = f32[4,2,32,128]{3,2,1,0:T(8,128)S(1)} collective-permute-done((f32[4,2,32,128]{3,2,1,0:T(8,128)S(1)}, f32[4,2,32,128]{3,2,1,0:T(8,128)S(1)}, u32[]{:S(2)}, u32[]{:S(2)}) %collective-permute-start.28) | collective-permute-done | bytes 131104 | tf_op jit(solution)/shard_map/ppermute | solution.py:339
  124.7 1.4 %collective-permute-start.30 = (f32[2,32,128]{2,1,0:T(8,128)S(1)}, f32[2,32,128]{2,1,0:T(8,128)S(1)}, u32[]{:S(2)}, u32[]{:S(2)}) collective-permute-start(f32[2,32,128]{2,1,0:T(8,128)S(1)} %get-tuple-element.83), channel_id=1, source_target_pairs={{0,16},{4,20},{8,24},{12,28},{16,0},{20,4},{24,8},{28,12},{1,17},{... | collective-permute-start | bytes 98312 | tf_op jit(solution)/shard_map/ppermute | solution.py:24
  126.1 2.4 %collective-permute-start.31 = (f32[2,32,128]{2,1,0:T(8,128)S(1)}, f32[2,32,128]{2,1,0:T(8,128)S(1)}, u32[]{:S(2)}, u32[]{:S(2)}) collective-permute-start(f32[2,32,128]{2,1,0:T(8,128)S(1)} %get-tuple-element.84), channel_id=1, source_target_pairs={{0,24},{4,28},{8,0},{12,4},{16,8},{20,12},{24,16},{28,20},{1,25},{... | collective-permute-start | bytes 98312 | tf_op jit(solution)/shard_map/ppermute | solution.py:24
  128.5 1.0 collective-permute-done.31
  129.5 3.7 %collective-permute-done.29 = f32[2,32,128]{2,1,0:T(8,128)S(1)} collective-permute-done((f32[2,32,128]{2,1,0:T(8,128)S(1)}, f32[2,32,128]{2,1,0:T(8,128)S(1)}, u32[]{:S(2)}, u32[]{:S(2)}) %collective-permute-start.29) | collective-permute-done | bytes 32800 | tf_op jit(solution)/shard_map/ppermute | solution.py:24
  133.2 4.0 %collective-permute-start.34 = (f32[2,32,128]{2,1,0:T(8,128)S(1)}, f32[2,32,128]{2,1,0:T(8,128)S(1)}, u32[]{:S(2)}, u32[]{:S(2)}) collective-permute-start(f32[2,32,128]{2,1,0:T(8,128)S(1)} %bitcast_add_fusion.refs_0_), channel_id=1, source_target_pairs={{0,3},{1,0},{2,1},{3,2},{4,7},{5,4},{6,5},{7,6},{8,11},{9,8},{10,9... | collective-permute-start | bytes 98312 | tf_op jit(solution)/shard_map/ppermute | solution.py:24
  137.2 1.2 collective-permute-start.33
  138.4 0.5 collective-permute-start.32
  138.9 1.3 collective-permute-done.34.refs_3_
  140.2 0.5 collective-permute-done.33.refs_2_
  140.6 0.8 shard_map.45
  (50 shorter events, 0.3 us)
Async XLA Ops:
  0.0 10.5 %copy-start.3 = (f32[2,3]{1,0:T(2,128)S(1)}, f32[2,3]{1,0:T(2,128)}, u32[]{:S(2)}) copy-start(f32[2,3]{1,0:T(2,128)} %param.4) | copy-start | bytes 76
  0.0 2.4 %copy-start = (f32[1,2,32,3,6400]{4,2,3,1,0:T(8,128)S(1)}, f32[1,2,32,3,6400]{4,2,3,1,0:T(8,128)}, u32[]{:S(2)}) copy-start(f32[1,2,32,3,6400]{4,2,3,1,0:T(8,128)} %param.3) | copy-start | bytes 14745604
  2.4 8.2 %copy-start.2 = (s32[8,2,3]{0,1,2:T(2,128)S(1)}, s32[8,2,3]{0,1,2:T(2,128)}, u32[]{:S(2)}) copy-start(s32[8,2,3]{0,1,2:T(2,128)} %param.5) | copy-start | bytes 580
  2.4 65.6 %slice-start = ((s8[4915200]{0:T(1024)(128)(4,1)}), s8[720896]{0:T(1024)(128)(4,1)S(1)}, s32[]{:S(2)}) async-start(s8[4915200]{0:T(1024)(128)(4,1)} %bitcast.23), calls=%async_computation | async-start | bytes 1441792
  2.8 20.5 %collective-permute-start.7 = (f32[2,32,768]{2,1,0:T(8,128)S(1)}, f32[2,32,768]{2,1,0:T(8,128)S(1)}, u32[]{:S(2)}, u32[]{:S(2)}) collective-permute-start(f32[2,32,768]{2,1,0:T(8,128)S(1)} %get-tuple-element.50), channel_id=1, source_target_pairs={{0,16},{4,20},{8,24},{12,28},{16,0},{20,4},{24,8},{28,12},{1,17},{... | collective-permute-start | bytes 589832 | tf_op jit(solution)/shard_map/ppermute | solution.py:53
  6.0 22.2 %collective-permute-start.8 = (f32[2,32,768]{2,1,0:T(8,128)S(1)}, f32[2,32,768]{2,1,0:T(8,128)S(1)}, u32[]{:S(2)}, u32[]{:S(2)}) collective-permute-start(f32[2,32,768]{2,1,0:T(8,128)S(1)} %get-tuple-element.51), channel_id=1, source_target_pairs={{0,20},{4,16},{8,28},{12,24},{16,4},{20,0},{24,12},{28,8},{1,21},{... | collective-permute-start | bytes 589832 | tf_op jit(solution)/shard_map/ppermute | solution.py:53
  7.0 22.6 %collective-permute-start.9 = (f32[2,32,768]{2,1,0:T(8,128)S(1)}, f32[2,32,768]{2,1,0:T(8,128)S(1)}, u32[]{:S(2)}, u32[]{:S(2)}) collective-permute-start(f32[2,32,768]{2,1,0:T(8,128)S(1)} %get-tuple-element.52), channel_id=1, source_target_pairs={{0,4},{4,0},{8,12},{12,8},{16,20},{20,16},{24,28},{28,24},{1,5},{5... | collective-permute-start | bytes 589832 | tf_op jit(solution)/shard_map/ppermute | solution.py:53
  7.2 25.4 %collective-permute-start.10 = (f32[2,32,768]{2,1,0:T(8,128)S(1)}, f32[2,32,768]{2,1,0:T(8,128)S(1)}, u32[]{:S(2)}, u32[]{:S(2)}) collective-permute-start(f32[2,32,768]{2,1,0:T(8,128)S(1)} %get-tuple-element.53), channel_id=1, source_target_pairs={{0,24},{4,28},{8,16},{12,20},{16,8},{20,12},{24,0},{28,4},{1,25},{... | collective-permute-start | bytes 589832 | tf_op jit(solution)/shard_map/ppermute | solution.py:53
  10.5 34.0 %collective-permute-start.11 = (f32[2,32,768]{2,1,0:T(8,128)S(1)}, f32[2,32,768]{2,1,0:T(8,128)S(1)}, u32[]{:S(2)}, u32[]{:S(2)}) collective-permute-start(f32[2,32,768]{2,1,0:T(8,128)S(1)} %get-tuple-element.54), channel_id=1, source_target_pairs={{0,8},{4,12},{8,0},{12,4},{16,24},{20,28},{24,16},{28,20},{1,9},{5... | collective-permute-start | bytes 589832 | tf_op jit(solution)/shard_map/ppermute | solution.py:53
  15.6 2.4 %copy-start.1 = (f32[1,2,32,3,6400]{4,2,3,1,0:T(8,128)S(1)}, f32[1,2,32,3,6400]{4,2,3,1,0:T(8,128)}, u32[]{:S(2)}) copy-start(f32[1,2,32,3,6400]{4,2,3,1,0:T(8,128)} %param.3) | copy-start | bytes 14745604
  18.0 50.1 %slice-start.1 = ((s8[4915200]{0:T(1024)(128)(4,1)}), s8[4194304]{0:T(1024)(128)(4,1)S(1)}, s32[]{:S(2)}) async-start(s8[4915200]{0:T(1024)(128)(4,1)} %bitcast.23), calls=%async_computation.1 | async-start | bytes 8388608
  23.3 22.6 %collective-permute-start.12 = (f32[2,32,768]{2,1,0:T(8,128)S(1)}, f32[2,32,768]{2,1,0:T(8,128)S(1)}, u32[]{:S(2)}, u32[]{:S(2)}) collective-permute-start(f32[2,32,768]{2,1,0:T(8,128)S(1)} %get-tuple-element.55), channel_id=1, source_target_pairs={{0,28},{4,24},{8,20},{12,16},{16,12},{20,8},{24,4},{28,0},{1,29},{... | collective-permute-start | bytes 589832 | tf_op jit(solution)/shard_map/ppermute | solution.py:53
  28.2 17.7 %collective-permute-start.13 = (f32[2,32,768]{2,1,0:T(8,128)S(1)}, f32[2,32,768]{2,1,0:T(8,128)S(1)}, u32[]{:S(2)}, u32[]{:S(2)}) collective-permute-start(f32[2,32,768]{2,1,0:T(8,128)S(1)} %get-tuple-element.56), channel_id=1, source_target_pairs={{0,12},{4,8},{8,4},{12,0},{16,28},{20,24},{24,20},{28,16},{1,13},{... | collective-permute-start | bytes 589832 | tf_op jit(solution)/shard_map/ppermute | solution.py:53
  29.6 27.6 %collective-permute-start = (f32[2,32,768]{2,1,0:T(8,128)S(1)}, f32[2,32,768]{2,1,0:T(8,128)S(1)}, u32[]{:S(2)}, u32[]{:S(2)}) collective-permute-start(f32[2,32,768]{2,1,0:T(8,128)S(1)} %get-tuple-element.42), channel_id=1, source_target_pairs={{0,16},{4,20},{8,24},{12,28},{16,0},{20,4},{24,8},{28,12},{1,17},{... | collective-permute-start | bytes 589832 | tf_op jit(solution)/shard_map/ppermute | solution.py:53
  32.6 29.4 %collective-permute-start.1 = (f32[2,32,768]{2,1,0:T(8,128)S(1)}, f32[2,32,768]{2,1,0:T(8,128)S(1)}, u32[]{:S(2)}, u32[]{:S(2)}) collective-permute-start(f32[2,32,768]{2,1,0:T(8,128)S(1)} %get-tuple-element.43), channel_id=1, source_target_pairs={{0,20},{4,16},{8,28},{12,24},{16,4},{20,0},{24,12},{28,8},{1,21},{... | collective-permute-start | bytes 589832 | tf_op jit(solution)/shard_map/ppermute | solution.py:53
  44.5 23.9 %collective-permute-start.2 = (f32[2,32,768]{2,1,0:T(8,128)S(1)}, f32[2,32,768]{2,1,0:T(8,128)S(1)}, u32[]{:S(2)}, u32[]{:S(2)}) collective-permute-start(f32[2,32,768]{2,1,0:T(8,128)S(1)} %get-tuple-element.44), channel_id=1, source_target_pairs={{0,4},{4,0},{8,12},{12,8},{16,20},{20,16},{24,28},{28,24},{1,5},{5... | collective-permute-start | bytes 589832 | tf_op jit(solution)/shard_map/ppermute | solution.py:53
  45.8 25.6 %collective-permute-start.3 = (f32[2,32,768]{2,1,0:T(8,128)S(1)}, f32[2,32,768]{2,1,0:T(8,128)S(1)}, u32[]{:S(2)}, u32[]{:S(2)}) collective-permute-start(f32[2,32,768]{2,1,0:T(8,128)S(1)} %get-tuple-element.45), channel_id=1, source_target_pairs={{0,24},{4,28},{8,16},{12,20},{16,8},{20,12},{24,0},{28,4},{1,25},{... | collective-permute-start | bytes 589832 | tf_op jit(solution)/shard_map/ppermute | solution.py:53
  45.9 27.9 %collective-permute-start.4 = (f32[2,32,768]{2,1,0:T(8,128)S(1)}, f32[2,32,768]{2,1,0:T(8,128)S(1)}, u32[]{:S(2)}, u32[]{:S(2)}) collective-permute-start(f32[2,32,768]{2,1,0:T(8,128)S(1)} %get-tuple-element.46), channel_id=1, source_target_pairs={{0,8},{4,12},{8,0},{12,4},{16,24},{20,28},{24,16},{28,20},{1,9},{5... | collective-permute-start | bytes 589832 | tf_op jit(solution)/shard_map/ppermute | solution.py:53
  57.1 16.6 %collective-permute-start.5 = (f32[2,32,768]{2,1,0:T(8,128)S(1)}, f32[2,32,768]{2,1,0:T(8,128)S(1)}, u32[]{:S(2)}, u32[]{:S(2)}) collective-permute-start(f32[2,32,768]{2,1,0:T(8,128)S(1)} %get-tuple-element.47), channel_id=1, source_target_pairs={{0,28},{4,24},{8,20},{12,16},{16,12},{20,8},{24,4},{28,0},{1,29},{... | collective-permute-start | bytes 589832 | tf_op jit(solution)/shard_map/ppermute | solution.py:53
  62.0 12.2 %collective-permute-start.6 = (f32[2,32,768]{2,1,0:T(8,128)S(1)}, f32[2,32,768]{2,1,0:T(8,128)S(1)}, u32[]{:S(2)}, u32[]{:S(2)}) collective-permute-start(f32[2,32,768]{2,1,0:T(8,128)S(1)} %get-tuple-element.48), channel_id=1, source_target_pairs={{0,12},{4,8},{8,4},{12,0},{16,28},{20,24},{24,20},{28,16},{1,13},{... | collective-permute-start | bytes 589832 | tf_op jit(solution)/shard_map/ppermute | solution.py:53
  68.4 28.3 %collective-permute-start.21 = (f32[2,32,640]{2,1,0:T(8,128)S(1)}, f32[2,32,640]{2,1,0:T(8,128)S(1)}, u32[]{:S(2)}, u32[]{:S(2)}) collective-permute-start(f32[2,32,640]{2,1,0:T(8,128)S(1)} %get-tuple-element.68), channel_id=1, source_target_pairs={{0,16},{4,20},{8,24},{12,28},{16,0},{20,4},{24,8},{28,12},{1,17},{... | collective-permute-start | bytes 491528 | tf_op jit(solution)/shard_map/ppermute | solution.py:53
  71.5 27.4 %collective-permute-start.22 = (f32[2,32,640]{2,1,0:T(8,128)S(1)}, f32[2,32,640]{2,1,0:T(8,128)S(1)}, u32[]{:S(2)}, u32[]{:S(2)}) collective-permute-start(f32[2,32,640]{2,1,0:T(8,128)S(1)} %get-tuple-element.69), channel_id=1, source_target_pairs={{0,20},{4,16},{8,28},{12,24},{16,4},{20,0},{24,12},{28,8},{1,21},{... | collective-permute-start | bytes 491528 | tf_op jit(solution)/shard_map/ppermute | solution.py:53
  79.2 15.7 %collective-permute-start.14 = (f32[2,32,256]{2,1,0:T(8,128)S(1)}, f32[2,32,256]{2,1,0:T(8,128)S(1)}, u32[]{:S(2)}, u32[]{:S(2)}) collective-permute-start(f32[2,32,256]{2,1,0:T(8,128)S(1)} %get-tuple-element.59), channel_id=1, source_target_pairs={{0,16},{4,20},{8,24},{12,28},{16,0},{20,4},{24,8},{28,12},{1,17},{... | collective-permute-start | bytes 196616 | tf_op jit(solution)/shard_map/ppermute | solution.py:53
  90.0 6.7 %collective-permute-start.15 = (f32[2,32,256]{2,1,0:T(8,128)S(1)}, f32[2,32,256]{2,1,0:T(8,128)S(1)}, u32[]{:S(2)}, u32[]{:S(2)}) collective-permute-start(f32[2,32,256]{2,1,0:T(8,128)S(1)} %get-tuple-element.60), channel_id=1, source_target_pairs={{0,20},{4,16},{8,28},{12,24},{16,4},{20,0},{24,12},{28,8},{1,21},{... | collective-permute-start | bytes 196616 | tf_op jit(solution)/shard_map/ppermute | solution.py:53
  90.3 9.3 %collective-permute-start.23 = (f32[2,32,640]{2,1,0:T(8,128)S(1)}, f32[2,32,640]{2,1,0:T(8,128)S(1)}, u32[]{:S(2)}, u32[]{:S(2)}) collective-permute-start(f32[2,32,640]{2,1,0:T(8,128)S(1)} %get-tuple-element.70), channel_id=1, source_target_pairs={{0,4},{4,0},{8,12},{12,8},{16,20},{20,16},{24,28},{28,24},{1,5},{5... | collective-permute-start | bytes 491528 | tf_op jit(solution)/shard_map/ppermute | solution.py:53
  94.9 7.1 %collective-permute-start.24 = (f32[2,32,640]{2,1,0:T(8,128)S(1)}, f32[2,32,640]{2,1,0:T(8,128)S(1)}, u32[]{:S(2)}, u32[]{:S(2)}) collective-permute-start(f32[2,32,640]{2,1,0:T(8,128)S(1)} %get-tuple-element.71), channel_id=1, source_target_pairs={{0,24},{4,28},{8,16},{12,20},{16,8},{20,12},{24,0},{28,4},{1,25},{... | collective-permute-start | bytes 491528 | tf_op jit(solution)/shard_map/ppermute | solution.py:53
  96.8 10.3 %collective-permute-start.25 = (f32[2,32,640]{2,1,0:T(8,128)S(1)}, f32[2,32,640]{2,1,0:T(8,128)S(1)}, u32[]{:S(2)}, u32[]{:S(2)}) collective-permute-start(f32[2,32,640]{2,1,0:T(8,128)S(1)} %get-tuple-element.72), channel_id=1, source_target_pairs={{0,8},{4,12},{8,0},{12,4},{16,24},{20,28},{24,16},{28,20},{1,9},{5... | collective-permute-start | bytes 491528 | tf_op jit(solution)/shard_map/ppermute | solution.py:53
  96.8 13.0 %collective-permute-start.26 = (f32[2,32,640]{2,1,0:T(8,128)S(1)}, f32[2,32,640]{2,1,0:T(8,128)S(1)}, u32[]{:S(2)}, u32[]{:S(2)}) collective-permute-start(f32[2,32,640]{2,1,0:T(8,128)S(1)} %get-tuple-element.73), channel_id=1, source_target_pairs={{0,28},{4,24},{8,20},{12,16},{16,12},{20,8},{24,4},{28,0},{1,29},{... | collective-permute-start | bytes 491528 | tf_op jit(solution)/shard_map/ppermute | solution.py:53
  98.9 14.3 %collective-permute-start.27 = (f32[2,32,640]{2,1,0:T(8,128)S(1)}, f32[2,32,640]{2,1,0:T(8,128)S(1)}, u32[]{:S(2)}, u32[]{:S(2)}) collective-permute-start(f32[2,32,640]{2,1,0:T(8,128)S(1)} %get-tuple-element.74), channel_id=1, source_target_pairs={{0,12},{4,8},{8,4},{12,0},{16,28},{20,24},{24,20},{28,16},{1,13},{... | collective-permute-start | bytes 491528 | tf_op jit(solution)/shard_map/ppermute | solution.py:53
  99.6 17.5 %collective-permute-start.16 = (f32[2,32,256]{2,1,0:T(8,128)S(1)}, f32[2,32,256]{2,1,0:T(8,128)S(1)}, u32[]{:S(2)}, u32[]{:S(2)}) collective-permute-start(f32[2,32,256]{2,1,0:T(8,128)S(1)} %get-tuple-element.61), channel_id=1, source_target_pairs={{0,4},{4,0},{8,12},{12,8},{16,20},{20,16},{24,28},{28,24},{1,5},{5... | collective-permute-start | bytes 196616 | tf_op jit(solution)/shard_map/ppermute | solution.py:53
  102.0 15.1 %collective-permute-start.17 = (f32[2,32,256]{2,1,0:T(8,128)S(1)}, f32[2,32,256]{2,1,0:T(8,128)S(1)}, u32[]{:S(2)}, u32[]{:S(2)}) collective-permute-start(f32[2,32,256]{2,1,0:T(8,128)S(1)} %get-tuple-element.62), channel_id=1, source_target_pairs={{0,24},{4,28},{8,16},{12,20},{16,8},{20,12},{24,0},{28,4},{1,25},{... | collective-permute-start | bytes 196616 | tf_op jit(solution)/shard_map/ppermute | solution.py:53
  107.1 10.1 %collective-permute-start.18 = (f32[2,32,256]{2,1,0:T(8,128)S(1)}, f32[2,32,256]{2,1,0:T(8,128)S(1)}, u32[]{:S(2)}, u32[]{:S(2)}) collective-permute-start(f32[2,32,256]{2,1,0:T(8,128)S(1)} %get-tuple-element.63), channel_id=1, source_target_pairs={{0,8},{4,12},{8,0},{12,4},{16,24},{20,28},{24,16},{28,20},{1,9},{5... | collective-permute-start | bytes 196616 | tf_op jit(solution)/shard_map/ppermute | solution.py:53
  109.7 8.1 %collective-permute-start.19 = (f32[2,32,256]{2,1,0:T(8,128)S(1)}, f32[2,32,256]{2,1,0:T(8,128)S(1)}, u32[]{:S(2)}, u32[]{:S(2)}) collective-permute-start(f32[2,32,256]{2,1,0:T(8,128)S(1)} %get-tuple-element.64), channel_id=1, source_target_pairs={{0,28},{4,24},{8,20},{12,16},{16,12},{20,8},{24,4},{28,0},{1,29},{... | collective-permute-start | bytes 196616 | tf_op jit(solution)/shard_map/ppermute | solution.py:53
  113.2 5.0 %collective-permute-start.20 = (f32[2,32,256]{2,1,0:T(8,128)S(1)}, f32[2,32,256]{2,1,0:T(8,128)S(1)}, u32[]{:S(2)}, u32[]{:S(2)}) collective-permute-start(f32[2,32,256]{2,1,0:T(8,128)S(1)} %get-tuple-element.65), channel_id=1, source_target_pairs={{0,12},{4,8},{8,4},{12,0},{16,28},{20,24},{24,20},{28,16},{1,13},{... | collective-permute-start | bytes 196616 | tf_op jit(solution)/shard_map/ppermute | solution.py:53
  120.8 3.9 %collective-permute-start.28 = (f32[4,2,32,128]{3,2,1,0:T(8,128)S(1)}, f32[4,2,32,128]{3,2,1,0:T(8,128)S(1)}, u32[]{:S(2)}, u32[]{:S(2)}) collective-permute-start(f32[4,2,32,128]{3,2,1,0:T(8,128)S(1)} %get-tuple-element.76), channel_id=1, source_target_pairs={{0,4},{4,0},{8,12},{12,8},{16,20},{20,16},{24,28},{28,24},{1,5},{5... | collective-permute-start | bytes 393224 | tf_op jit(solution)/shard_map/ppermute | solution.py:339
  124.7 3.8 %collective-permute-start.30 = (f32[2,32,128]{2,1,0:T(8,128)S(1)}, f32[2,32,128]{2,1,0:T(8,128)S(1)}, u32[]{:S(2)}, u32[]{:S(2)}) collective-permute-start(f32[2,32,128]{2,1,0:T(8,128)S(1)} %get-tuple-element.83), channel_id=1, source_target_pairs={{0,16},{4,20},{8,24},{12,28},{16,0},{20,4},{24,8},{28,12},{1,17},{... | collective-permute-start | bytes 98312 | tf_op jit(solution)/shard_map/ppermute | solution.py:24
  126.1 3.4 %collective-permute-start.31 = (f32[2,32,128]{2,1,0:T(8,128)S(1)}, f32[2,32,128]{2,1,0:T(8,128)S(1)}, u32[]{:S(2)}, u32[]{:S(2)}) collective-permute-start(f32[2,32,128]{2,1,0:T(8,128)S(1)} %get-tuple-element.84), channel_id=1, source_target_pairs={{0,24},{4,28},{8,0},{12,4},{16,8},{20,12},{24,16},{28,20},{1,25},{... | collective-permute-start | bytes 98312 | tf_op jit(solution)/shard_map/ppermute | solution.py:24
  128.5 4.7 %collective-permute-start.29 = (f32[2,32,128]{2,1,0:T(8,128)S(1)}, f32[2,32,128]{2,1,0:T(8,128)S(1)}, u32[]{:S(2)}, u32[]{:S(2)}) collective-permute-start(f32[2,32,128]{2,1,0:T(8,128)S(1)} %get-tuple-element.85), channel_id=1, source_target_pairs={{0,8},{4,12},{8,16},{12,20},{16,24},{20,28},{24,0},{28,4},{1,9},{5... | collective-permute-start | bytes 98312 | tf_op jit(solution)/shard_map/ppermute | solution.py:24
  133.2 7.0 %collective-permute-start.34 = (f32[2,32,128]{2,1,0:T(8,128)S(1)}, f32[2,32,128]{2,1,0:T(8,128)S(1)}, u32[]{:S(2)}, u32[]{:S(2)}) collective-permute-start(f32[2,32,128]{2,1,0:T(8,128)S(1)} %bitcast_add_fusion.refs_0_), channel_id=1, source_target_pairs={{0,3},{1,0},{2,1},{3,2},{4,7},{5,4},{6,5},{7,6},{8,11},{9,8},{10,9... | collective-permute-start | bytes 98312 | tf_op jit(solution)/shard_map/ppermute | solution.py:24
  137.2 3.4 %collective-permute-start.33 = (f32[2,32,128]{2,1,0:T(8,128)S(1)}, f32[2,32,128]{2,1,0:T(8,128)S(1)}, u32[]{:S(2)}, u32[]{:S(2)}) collective-permute-start(f32[2,32,128]{2,1,0:T(8,128)S(1)} %bitcast_add_fusion.refs_0_), channel_id=1, source_target_pairs={{0,2},{1,3},{2,0},{3,1},{4,6},{5,7},{6,4},{7,5},{8,10},{9,11},{10,... | collective-permute-start | bytes 98312 | tf_op jit(solution)/shard_map/ppermute | solution.py:24
  138.4 2.2 %collective-permute-start.32 = (f32[2,32,128]{2,1,0:T(8,128)S(1)}, f32[2,32,128]{2,1,0:T(8,128)S(1)}, u32[]{:S(2)}, u32[]{:S(2)}) collective-permute-start(f32[2,32,128]{2,1,0:T(8,128)S(1)} %bitcast_add_fusion.refs_0_), channel_id=1, source_target_pairs={{0,1},{1,2},{2,3},{3,0},{4,5},{5,6},{6,7},{7,4},{8,9},{9,10},{10,1... | collective-permute-start | bytes 98312 | tf_op jit(solution)/shard_map/ppermute | solution.py:24

commit v3 on v2

--- a/solution.py
+++ b/solution.py
@@ -12,8 +12,9 @@
 GY = 40
 KX = 4
 LANES = 128
-SHARES = (0.32, 0.32, 0.26, 0.10)
+SHARES = (0.37,0.37,0.26)
 AHEAD = 2
+EARLY = 1
 
 two_pi = 2.0 * math.pi
 
@@ -33,24 +34,13 @@
 
 
 def exchange(count):
-    if count & (count - 1) == 0:
-        half = count // 2
-        turns = [turn for low in range(half) for turn in (half + low, low) if turn]
-        return [functools.partial(lambda turn, me: me ^ turn, turn) for turn in turns]
-    turns = sorted(range(1, count), key=lambda turn: -min(turn, count - turn))
-    return [functools.partial(lambda turn, me: (me + turn) % count, turn) for turn in turns]
-
-
-def exchange_back(count):
-    if count & (count - 1) == 0:
-        return exchange(count)
-    turns = sorted(range(1, count), key=lambda turn: -min(turn, count - turn))
-    return [functools.partial(lambda turn, me: (me + count - turn) % count, turn) for turn in turns]
-
-
-def sent_round(value, to):
-    pairs = [(source, to(source)) for source in range(lax.axis_size("ka"))]
-    return lax.ppermute(value, "ka", pairs)
+    turns = sorted(range(1, count), key=lambda turn: (-min(turn, count - turn), turn))
+    far, near = turns[: (count + 1) // 2], turns[(count + 1) // 2 :]
+    near.sort(reverse=True)
+    found = []
+    for place, turn in enumerate(far):
+        found += [turn] + near[place : place + 1]
+    return found
 
 
 class Parts:
@@ -138,12 +128,12 @@
     return copies
 
 
-def pack_kernel(parts, targets, start, stop, field_ref, *refs):
+def pack_kernel(parts, turns, start, stop, field_ref, *refs):
     outs, sems = refs[:-1], refs[-1]
     me = lax.axis_index("ka")
     copies = []
-    for to, out_ref in zip(targets, outs):
-        part = to(me)
+    for turn, out_ref in zip(turns, outs):
+        part = lax.rem(me + (parts.count - turn), parts.count)
         copies += copies_of(parts, field_ref, part, start, stop, out_ref, sems, len(copies))
     for copy in copies:
         copy.start()
@@ -151,38 +141,41 @@
         copy.wait()
 
 
-def pack(parts, field, targets, start, stop):
+def pack(parts, field, turns, start, stop, mebibytes):
     shape = (2, field.shape[2], (stop - start) * LANES)
     anywhere = pl.BlockSpec(memory_space=pl.ANY)
-    size = 4 * math.prod(shape) * len(targets)
+    size = 4 * math.prod(shape) * len(turns)
     return pl.pallas_call(
-        functools.partial(pack_kernel, parts, targets, start, stop),
-        out_shape=[jax.ShapeDtypeStruct(shape, jnp.float32)] * len(targets),
+        functools.partial(pack_kernel, parts, turns, start, stop),
+        out_shape=[jax.ShapeDtypeStruct(shape, jnp.float32)] * len(turns),
         in_specs=[anywhere],
-        out_specs=[pl.BlockSpec(memory_space=pltpu.VMEM)] * len(targets),
+        out_specs=[pl.BlockSpec(memory_space=pltpu.VMEM)] * len(turns),
         scratch_shapes=[
-            pltpu.SemaphoreType.DMA((len(targets) * len(parts.pieces(start, stop)),)),
+            pltpu.SemaphoreType.DMA((len(turns) * len(parts.pieces(start, stop)),)),
         ],
-        compiler_params=pltpu.CompilerParams(vmem_limit_bytes=4 * 1024 * 1024),
+        compiler_params=pltpu.CompilerParams(vmem_limit_bytes=mebibytes * 1024 * 1024),
         cost_estimate=pl.CostEstimate(flops=0, bytes_accessed=2 * size, transcendentals=0),
     )(field)
 
 
-def write_messages(count, offsets, factor, total_ref, out_refs, forward):
+def forward_matrices(rows):
+    bands, width = rows.shape[0] // 2, rows.shape[1]
+    lane = lax.broadcasted_iota(jnp.int32, (bands, width), 1)
+    with_imag = rows[bands:]
+    after = pltpu.roll(with_imag, width - bands, 1)
+    ahead = pltpu.roll(with_imag, bands, 1)
+    return rows[:bands] + jnp.where(lane % (2 * bands) < bands, after, -ahead)
+
+
+def write_messages(offsets, factor, forward, out_refs):
+    count = len(forward)
     me = lax.axis_index("ka")
-    bands = total_ref.shape[1] // 2
-    width = total_ref.shape[2]
+    bands, width = forward[0].shape
     lane = lax.broadcasted_iota(jnp.int32, (bands, width), 1)
-    real_lane = lane % (2 * bands) < bands
     for step in range(count):
-        with_real = total_ref[step, :bands]
-        with_imag = total_ref[step, bands:]
-        after = pltpu.roll(with_imag, width - bands, 1)
-        ahead = pltpu.roll(with_imag, bands, 1)
-        forward[step] = with_real + jnp.where(real_lane, after, -ahead)
-    for step in range(count):
-        turn = lax.rem(step % factor + factor - lax.rem(me, factor), factor)
-        group = step // factor
+        target = lax.rem(me + step, count)
+        turn = lax.rem(lax.rem(target, factor) + factor - lax.rem(me, factor), factor)
+        group = target // factor
         back = jnp.zeros((bands, width), jnp.float32)
         for direction, offset in enumerate(offsets):
             other = forward[(step + count - offset) % count]
@@ -195,42 +188,29 @@
                 out_ref[group, 1] = back
 
 
-def chunk_kernel(parts, offsets, start, stop, factor, *refs):
-    count = parts.count
-    blocks, refs = refs[:count], refs[count:]
-    (cosine_ref, sine_ref), refs = refs[:2], refs[2:]
+def chunk_kernel(offsets, first, factor, turns, start, *refs):
+    count = len(turns)
+    fields = {turn: ref for turn, ref in zip(turns, refs)}
+    cosine_ref, sine_ref = refs[count : count + 2]
+    outs = refs[count + 2 :]
     before_ref = None
-    if start > 0:
-        before_ref, refs = refs[0], refs[1:]
-    last = stop == parts.units
-    if last:
-        outs, (held, sems, total_ref, forward) = refs[:factor], refs[factor:]
-    else:
-        total_ref, held, sems = refs
-    me = lax.axis_index("ka")
-    sources = [lambda place: place] + exchange_back(count)
-    copies = [
-        pltpu.make_async_copy(block, held.at[source(me)], sems.at[number])
-        for number, (block, source) in enumerate(zip(blocks, sources))
-    ]
-    for copy in copies:
-        copy.start()
-    for copy in copies:
-        copy.wait()
-
-    @pl.loop(0, count)
-    def _(step):
-        left = held[step]
+    if not first:
+        before_ref, outs = outs[0], outs[1:]
+    forward = []
+    for step in range(count):
+        left = fields[step][...]
         bands, cells = left.shape[1], left.shape[2]
         left_high, left_low = split_parts(left.reshape(2 * bands, cells))
         left_rows = jnp.concatenate([left_high, left_low], axis=0)
         highs, lows = [], []
         for direction, offset in enumerate(offsets):
-            right = held[lax.rem(step + offset, count)]
-            cosine = cosine_ref[step * len(offsets) + direction]
-            sine = sine_ref[step * len(offsets) + direction]
-            w_real = cosine * right[0] - sine * right[1]
-            w_imag = sine * right[0] + cosine * right[1]
+            right = fields[(step + offset) % count]
+            right_real, right_imag = right[0], right[1]
+            row = step * len(offsets) + direction
+            cosine = cosine_ref[row : row + 1, start : start + cells]
+            sine = sine_ref[row : row + 1, start : start + cells]
+            w_real = cosine * right_real - sine * right_imag
+            w_imag = sine * right_real + cosine * right_imag
             high, low = split_parts(jnp.concatenate([w_real, w_imag], axis=0))
             highs.append(high)
             lows.append(low)
@@ -246,46 +226,35 @@
         summed = rows[:, :half] + rows[:, half:]
         if before_ref is not None:
             summed = summed + before_ref[step]
-        total_ref[step] = summed
-
-    if last:
-        write_messages(count, offsets, factor, total_ref, outs, forward)
-
-
-def chunk_products(parts, blocks, cosine, sine, before, offsets, start, stop, factor):
-    count = parts.count
-    bands = blocks[0].shape[1]
-    cells = (stop - start) * LANES
+        if factor:
+            forward.append(forward_matrices(summed))
+        else:
+            outs[0][step] = summed
+    if factor:
+        write_messages(offsets, factor, forward, outs)
+
+
+def chunk_products(blocks, turns, start, cosine, sine, before, offsets, factor):
+    count = len(blocks)
+    _, bands, cells = blocks[0].shape
     width = 2 * len(offsets) * bands
     operands = list(blocks) + [cosine, sine]
-    anywhere = pl.BlockSpec(memory_space=pl.ANY)
-    inside = pl.BlockSpec(memory_space=pltpu.VMEM)
-    in_specs = [anywhere] * count + [inside, inside]
     if before is not None:
         operands.append(before)
-        in_specs.append(inside)
-    total_shape = (count, 2 * bands, width)
-    scratch = [
-        pltpu.VMEM((count, 2, bands, cells), jnp.float32),
-        pltpu.SemaphoreType.DMA((count,)),
-    ]
-    if stop == parts.units:
+    inside = pl.BlockSpec(memory_space=pltpu.VMEM)
+    if factor:
         message = jax.ShapeDtypeStruct((count // factor, 2, bands, width), jnp.float32)
         out_shape, out_specs = [message] * factor, [inside] * factor
-        scratch += [
-            pltpu.VMEM(total_shape, jnp.float32),
-            pltpu.VMEM((count, bands, width), jnp.float32),
-        ]
     else:
-        out_shape, out_specs = jax.ShapeDtypeStruct(total_shape, jnp.float32), inside
+        out_shape = jax.ShapeDtypeStruct((count, 2 * bands, width), jnp.float32)
+        out_specs = inside
     flops = 2 * count * (4 * bands) * (2 * width) * cells
     return pl.pallas_call(
-        functools.partial(chunk_kernel, parts, offsets, start, stop, factor),
+        functools.partial(chunk_kernel, offsets, before is None, factor, turns, start),
         out_shape=out_shape,
-        in_specs=in_specs,
+        in_specs=[inside] * len(operands),
         out_specs=out_specs,
-        scratch_shapes=scratch,
-        compiler_params=pltpu.CompilerParams(vmem_limit_bytes=12 * 1024 * 1024),
+        compiler_params=pltpu.CompilerParams(vmem_limit_bytes=16 * 1024 * 1024),
         cost_estimate=pl.CostEstimate(
             flops=flops, bytes_accessed=4 * count * 2 * bands * cells, transcendentals=0
         ),
@@ -293,11 +262,7 @@
 
 
 def block_factor(count):
-    best = 1
-    for factor in range(1, math.isqrt(count) + 1):
-        if count % factor == 0:
-            best = factor
-    return best
+    return min(factor for factor in range(1, count + 1) if count % factor == 0 and factor**2 >= count)
 
 
 def result_kernel(*refs):
@@ -363,12 +328,12 @@
     ycoord = (cell_index // GX % GY).astype(jnp.float32)
     zcoord = (lax.axis_index("gz") * slab_depth + cell_index // plane_cells).astype(jnp.float32)
     shifts_float = gshift.astype(jnp.float32)
-    q_vectors = (bvectors[None] + shifts_float).reshape(-1, 3)
+    q_vectors = jnp.roll(bvectors[None] + shifts_float, -me, axis=0).reshape(-1, 3)
     angles = phase_angle(q_vectors.T[:, :, None], xcoord, ycoord, zcoord, GX, GY, z_extent)
-    cosine = (jnp.cos(angles) * valid)[:, None]
-    sine = (jnp.sin(angles) * valid)[:, None]
-
-    rounds = exchange(count)
+    cosine = jnp.cos(angles) * valid
+    sine = jnp.sin(angles) * valid
+
+    turns = exchange(count)
     factor = block_factor(count)
     bounds = chunk_bounds(parts.units)
     totals = []
@@ -376,14 +341,14 @@
         source = field
         if chunk >= AHEAD:
             source, totals[chunk - AHEAD] = lax.optimization_barrier((field, totals[chunk - AHEAD]))
-        own, *sent = pack(parts, source, [lambda place: place] + rounds, start, stop)
-        blocks = [own] + [sent_round(value, to) for value, to in zip(sent, rounds)]
-        lanes = slice(start * LANES, stop * LANES)
-        before = totals[-1] if totals else None
+        early = EARLY if chunk == 0 else 0
+        sent = pack(parts, source, turns[:early], start, stop, 60) if early else []
+        sent += pack(parts, source, turns[early:] + [0], start, stop, 4)
+        blocks = [shifted(value, "ka", -turn) for value, turn in zip(sent, turns)] + [sent[-1]]
         totals.append(
             chunk_products(
-                parts, blocks, cosine[:, :, lanes], sine[:, :, lanes], before,
-                offsets, start, stop, factor,
+                blocks, turns + [0], start * LANES, cosine, sine,
+                totals[-1] if totals else None, offsets, factor if stop == parts.units else 0,
             )
         )
 

time: 143 us -> 135 us (0.944)
  waiting for transfers between devices: 33.3 us -> 47.4 us
  Pallas kernels: 17.8 us -> 7.85 us
  starting transfers between devices: 76.1 us -> 67.3 us
  other arithmetic: 8.81 us -> 0.9 us
  local copies, waits for them, and re-layouts: 5.2 us -> 10.9 us
    ppermute x28 -> x0, starting transfers between devices: 65.8 us -> none  [sent_round(): return lax.ppermute(value, 'ka', pairs)]
    ppermute x6 -> x25, starting transfers between devices: 9.53 us -> 58.5 us  [shifted(): return lax.ppermute(value, axis, pairs)]
    ppermute x6 -> x25, waiting for transfers between devices: 6.39 us -> 45.8 us  [shifted(): return lax.ppermute(value, axis, pairs)]
    ppermute x28 -> x0, waiting for transfers between devices: 23.8 us -> none  [sent_round(): return lax.ppermute(value, 'ka', pairs)]
    pallas_call x8 -> x7, Pallas kernels: 17 us -> 7.07 us  [the longest x3 4.06 us: chunk_products(): pl.pallas_call(functools.partial(chunk_kernel, offsets, before is None, f...]
    ppermute x1 -> x3, starting transfers between devices: 0.74 us -> 8.84 us  [reduced_over_points(): total = total + lax.ppermute(blocks[turn], 'ka', pairs)]
    mul x2 -> x1, other arithmetic: 8.65 us -> 0.66 us  [per_device(): sine = jnp.sin(angles) * valid]
    unnamed x13 -> x21, local copies, waits for them, and re-layouts: 4.9 us -> 10.7 us
  transfers between devices with their start and end apart: 35 -> 28, of which waited for: 15 -> 13; matrix products, arithmetic and copies ran while one was open for 6% -> 1% of each run, Pallas kernels for 10% -> 4%
where the time goes in v3:
time: 135 us
  starting transfers between devices  67.3 us (50%)
  waiting for transfers between devices  47.4 us (35%)
  local copies, waits for them, and re-layouts  10.9 us (8%)
  Pallas kernels  7.85 us (6%)
    ppermute x25, starting transfers between devices, shifted(): return lax.ppermute(value, axis, pairs)  58.5 us
    ppermute x25, waiting for transfers between devices, shifted(): return lax.ppermute(value, axis, pairs)  45.8 us
    unnamed x21, local copies, waits for them, and re-layouts  10.7 us
    ppermute x3, starting transfers between devices, reduced_over_points(): total = total + lax.ppermute(blocks[turn], 'ka', pairs)  8.84 us
    pallas_call x3, Pallas kernels, chunk_products(): pl.pallas_call(functools.partial(chunk_kernel, offsets, before is None, f...  4.06 us
    pallas_call x4, Pallas kernels, pack(): pl.pallas_call(functools.partial(pack_kernel, parts, turns, start, stop),...  3.01 us
  transfers between devices with their start and end apart: 28, of which 13 were waited for; matrix products, arithmetic and copies ran while one was open for 1% of the time, Pallas kernels for 4%

profile of v3, /device:TPU:1, one launch (start us, length us, event | category | flops | bytes accessed | tf_op | source)
XLA Modules:
  0.0 134.6 jit_solution(17107623338439595140)
XLA Ops:
  0.0 2.4 %copy-done = f32[1,2,32,3,6400]{4,2,3,1,0:T(8,128)S(1)} copy-done((f32[1,2,32,3,6400]{4,2,3,1,0:T(8,128)S(1)}, f32[1,2,32,3,6400]{4,2,3,1,0:T(8,128)}, u32[]{:S(2)}) %copy-start) | copy-done | bytes 4915224
  2.4 0.4 shard_map.38
  2.8 2.1 %collective-permute-start.1 = (f32[2,32,896]{2,1,0:T(8,128)S(1)}, f32[2,32,896]{2,1,0:T(8,128)S(1)}, u32[]{:S(2)}, u32[]{:S(2)}) collective-permute-start(f32[2,32,896]{2,1,0:T(8,128)S(1)} %get-tuple-element.33), channel_id=1, source_target_pairs={{0,4},{4,8},{8,12},{12,16},{16,20},{20,24},{24,28},{28,0},{1,5},{5... | collective-permute-start | bytes 688136 | tf_op jit(solution)/shard_map/ppermute | solution.py:25
  4.9 3.3 %collective-permute-start.2 = (f32[2,32,896]{2,1,0:T(8,128)S(1)}, f32[2,32,896]{2,1,0:T(8,128)S(1)}, u32[]{:S(2)}, u32[]{:S(2)}) collective-permute-start(f32[2,32,896]{2,1,0:T(8,128)S(1)} %get-tuple-element.34), channel_id=1, source_target_pairs={{0,20},{4,24},{8,28},{12,0},{16,4},{20,8},{24,12},{28,16},{1,21},{... | collective-permute-start | bytes 688136 | tf_op jit(solution)/shard_map/ppermute | solution.py:25
  8.2 0.1 collective-permute-start.3
  8.3 0.3 collective-permute-start.4
  8.6 3.8 %collective-permute-start.5 = (f32[2,32,896]{2,1,0:T(8,128)S(1)}, f32[2,32,896]{2,1,0:T(8,128)S(1)}, u32[]{:S(2)}, u32[]{:S(2)}) collective-permute-start(f32[2,32,896]{2,1,0:T(8,128)S(1)} %get-tuple-element.37), channel_id=1, source_target_pairs={{0,28},{4,0},{8,4},{12,8},{16,12},{20,16},{24,20},{28,24},{1,29},{... | collective-permute-start | bytes 688136 | tf_op jit(solution)/shard_map/ppermute | solution.py:25
  12.5 0.0 copy-start.9
  12.5 0.0 copy-start.8
  12.6 1.7 %shard_map.37 = f32[2,32,896]{2,1,0:T(8,128)} custom-call(f32[2,3,32,6400]{3,2,1,0:T(8,128)} %bitcast.17), custom_call_target="tpu_custom_call" | custom-call | bytes 458752 | tf_op jit(solution)/shard_map/pallas_call | solution.py:148
  14.2 0.0 copy-start.1
  14.2 2.4 %copy-done.1 = f32[1,2,32,3,6400]{4,2,3,1,0:T(8,128)S(1)} copy-done((f32[1,2,32,3,6400]{4,2,3,1,0:T(8,128)S(1)}, f32[1,2,32,3,6400]{4,2,3,1,0:T(8,128)}, u32[]{:S(2)}) %copy-start.1) | copy-done | bytes 4915224
  16.6 0.5 shard_map.41
  17.1 0.7 copy-done.3
  17.8 0.7 copy-done.4
  18.5 0.7 copy-done.5
  19.2 0.7 copy-done.6
  19.9 0.7 copy-done.7
  20.6 0.1 copy.6
  20.7 0.1 convert_add_fusion
  20.8 0.0 collective-permute-done.1.refs_1_
  20.8 0.3 collective-permute-start.6
  21.1 0.0 collective-permute-done.2.refs_2_
  21.1 6.2 %collective-permute-start = (f32[2,32,896]{2,1,0:T(8,128)}, f32[2,32,896]{2,1,0:T(8,128)S(1)}, u32[]{:S(2)}, u32[]{:S(2)}) collective-permute-start(f32[2,32,896]{2,1,0:T(8,128)} %shard_map.37), channel_id=1, source_target_pairs={{0,16},{4,20},{8,24},{12,28},{16,0},{20,4},{24,8},{28,12},{1,17},{... | collective-permute-start | bytes 688136 | tf_op jit(solution)/shard_map/ppermute | solution.py:25
  27.3 0.0 collective-permute-done.3.refs_3_
  27.3 0.0 collective-permute-start.14
  27.3 6.8 %collective-permute-done.4.refs_4_ = f32[2,32,896]{2,1,0:T(8,128)S(1)} collective-permute-done((f32[2,32,896]{2,1,0:T(8,128)S(1)}, f32[2,32,896]{2,1,0:T(8,128)S(1)}, u32[]{:S(2)}, u32[]{:S(2)}) %collective-permute-start.4) | collective-permute-done | bytes 229408 | tf_op jit(solution)/shard_map/ppermute | solution.py:25
  34.2 0.0 collective-permute-start.15
  34.2 0.1 dynamic-slice_maximum_fusion
  34.2 0.1 copy.7
  34.3 0.1 reshape.160
  34.4 15.8 %collective-permute-start.16 = (f32[2,32,896]{2,1,0:T(8,128)}, f32[2,32,896]{2,1,0:T(8,128)S(1)}, u32[]{:S(2)}, u32[]{:S(2)}) collective-permute-start(f32[2,32,896]{2,1,0:T(8,128)} %copy-done.5), channel_id=1, source_target_pairs={{0,20},{4,24},{8,28},{12,0},{16,4},{20,8},{24,12},{28,16},{1,21},{... | collective-permute-start | bytes 688136 | tf_op jit(solution)/shard_map/ppermute | solution.py:25
  50.2 12.2 %collective-permute-done.refs_0_ = f32[2,32,896]{2,1,0:T(8,128)S(1)} collective-permute-done((f32[2,32,896]{2,1,0:T(8,128)}, f32[2,32,896]{2,1,0:T(8,128)S(1)}, u32[]{:S(2)}, u32[]{:S(2)}) %collective-permute-start) | collective-permute-done | bytes 229408 | tf_op jit(solution)/shard_map/ppermute | solution.py:25
  62.4 9.8 %collective-permute-done.14.refs_0_ = f32[2,32,896]{2,1,0:T(8,128)S(1)} collective-permute-done((f32[2,32,896]{2,1,0:T(8,128)}, f32[2,32,896]{2,1,0:T(8,128)S(1)}, u32[]{:S(2)}, u32[]{:S(2)}) %collective-permute-start.14) | collective-permute-done | bytes 229408 | tf_op jit(solution)/shard_map/ppermute | solution.py:25
  72.3 1.3 collective-permute-start.20
  73.6 0.7 sine_multiply_fusion
  74.2 1.4 %shard_map.39.refs_10_ = f32[8,64,128]{2,1,0:T(8,128)S(1)} custom-call(f32[2,32,896]{2,1,0:T(8,128)S(1)} %collective-permute-done.refs_0_, f32[2,32,896]{2,1,0:T(8,128)S(1)} %collective-permute-done.1.refs_1_, f32[2,32,896]{2,1,0:T(8,128)S(1)} %collective-permute-done.2.refs_2_, f32[2,32,896]{2,1,0:T(8,128)S(1)} %collective-permute-done.3.refs_3_, ...), custom_call_target="tpu_custom_call" | custom-call | flops 469762048 | bytes 1835008 | tf_op jit(solution)/shard_map/pallas_call | solution.py:252
  75.6 0.0 copy-start.2
  75.6 2.4 %copy-done.2 = f32[1,2,32,3,6400]{4,2,3,1,0:T(8,128)S(1)} copy-done((f32[1,2,32,3,6400]{4,2,3,1,0:T(8,128)S(1)}, f32[1,2,32,3,6400]{4,2,3,1,0:T(8,128)}, u32[]{:S(2)}) %copy-start.2) | copy-done | bytes 4915224
  78.0 0.4 shard_map.40
  78.5 1.0 collective-permute-start.10
  79.4 0.5 collective-permute-start.11
  79.9 3.0 %collective-permute-done.18.refs_4_ = f32[2,32,896]{2,1,0:T(8,128)S(1)} collective-permute-done((f32[2,32,896]{2,1,0:T(8,128)}, f32[2,32,896]{2,1,0:T(8,128)S(1)}, u32[]{:S(2)}, u32[]{:S(2)}) %collective-permute-start.18) | collective-permute-done | bytes 229408 | tf_op jit(solution)/shard_map/ppermute | solution.py:25
  82.9 0.9 collective-permute-start.12
  83.9 6.5 %collective-permute-start.13 = (f32[2,32,640]{2,1,0:T(8,128)S(1)}, f32[2,32,640]{2,1,0:T(8,128)S(1)}, u32[]{:S(2)}, u32[]{:S(2)}) collective-permute-start(f32[2,32,640]{2,1,0:T(8,128)S(1)} %get-tuple-element.47), channel_id=1, source_target_pairs={{0,24},{4,28},{8,0},{12,4},{16,8},{20,12},{24,16},{28,20},{1,25},{... | collective-permute-start | bytes 491528 | tf_op jit(solution)/shard_map/ppermute | solution.py:25
  90.4 4.7 %collective-permute-done.20.refs_6_ = f32[2,32,896]{2,1,0:T(8,128)S(1)} collective-permute-done((f32[2,32,896]{2,1,0:T(8,128)S(1)}, f32[2,32,896]{2,1,0:T(8,128)S(1)}, u32[]{:S(2)}, u32[]{:S(2)}) %collective-permute-start.20) | collective-permute-done | bytes 229408 | tf_op jit(solution)/shard_map/ppermute | solution.py:25
  95.1 3.3 %collective-permute-done.11.refs_4_ = f32[2,32,640]{2,1,0:T(8,128)S(1)} collective-permute-done((f32[2,32,640]{2,1,0:T(8,128)S(1)}, f32[2,32,640]{2,1,0:T(8,128)S(1)}, u32[]{:S(2)}, u32[]{:S(2)}) %collective-permute-start.11) | collective-permute-done | bytes 163872 | tf_op jit(solution)/shard_map/ppermute | solution.py:25
  98.4 8.4 %collective-permute-start.9 = (f32[2,32,640]{2,1,0:T(8,128)S(1)}, f32[2,32,640]{2,1,0:T(8,128)S(1)}, u32[]{:S(2)}, u32[]{:S(2)}) collective-permute-start(f32[2,32,640]{2,1,0:T(8,128)S(1)} %get-tuple-element.43), channel_id=1, source_target_pairs={{0,20},{4,24},{8,28},{12,0},{16,4},{20,8},{24,12},{28,16},{1,21},{... | collective-permute-start | bytes 491528 | tf_op jit(solution)/shard_map/ppermute | solution.py:25
  106.8 1.4 %shard_map.42.refs_10_ = f32[8,64,128]{2,1,0:T(8,128)S(1)} custom-call(f32[2,32,896]{2,1,0:T(8,128)S(1)} %collective-permute-done.14.refs_0_, f32[2,32,896]{2,1,0:T(8,128)S(1)} %collective-permute-done.15.refs_1_, f32[2,32,896]{2,1,0:T(8,128)S(1)} %collective-permute-done.16.refs_2_, f32[2,32,896]{2,1,0:T(8,128)S(1)} %collective-permute-done.17.refs_3_, ...), custom_call_target="tpu_custom_call" | custom-call | flops 469762048 | bytes 1835008 | tf_op jit(solution)/shard_map/pallas_call | solution.py:252
  108.2 1.7 %collective-permute-done.7.refs_0_ = f32[2,32,640]{2,1,0:T(8,128)S(1)} collective-permute-done((f32[2,32,640]{2,1,0:T(8,128)S(1)}, f32[2,32,640]{2,1,0:T(8,128)S(1)}, u32[]{:S(2)}, u32[]{:S(2)}) %collective-permute-start.7) | collective-permute-done | bytes 163872 | tf_op jit(solution)/shard_map/ppermute | solution.py:25
  109.8 1.3 shard_map.43
  111.2 6.5 %collective-permute-start.21 = (f32[2,2,32,128]{3,2,1,0:T(8,128)S(1)}, f32[2,2,32,128]{3,2,1,0:T(8,128)S(1)}, u32[]{:S(2)}, u32[]{:S(2)}) collective-permute-start(f32[2,2,32,128]{3,2,1,0:T(8,128)S(1)} %get-tuple-element.58), channel_id=1, source_target_pairs={{0,4},{4,8},{8,12},{12,0},{16,20},{20,24},{24,28},{28,16},{1,5},{5... | collective-permute-start | bytes 196616 | tf_op jit(solution)/shard_map/ppermute | solution.py:304
  117.7 0.1 collective-permute-start.22
  117.8 2.3 %collective-permute-start.23 = (f32[2,2,32,128]{3,2,1,0:T(8,128)S(1)}, f32[2,2,32,128]{3,2,1,0:T(8,128)S(1)}, u32[]{:S(2)}, u32[]{:S(2)}) collective-permute-start(f32[2,2,32,128]{3,2,1,0:T(8,128)S(1)} %get-tuple-element.60), channel_id=1, source_target_pairs={{0,12},{4,0},{8,4},{12,8},{16,28},{20,16},{24,20},{28,24},{1,13},{... | collective-permute-start | bytes 196616 | tf_op jit(solution)/shard_map/ppermute | solution.py:304
  120.0 0.8 collective-permute-done.22
  120.8 0.8 collective-permute-done.23
  121.7 2.6 %collective-permute-start.24 = (f32[2,32,128]{2,1,0:T(8,128)S(1)}, f32[2,32,128]{2,1,0:T(8,128)S(1)}, u32[]{:S(2)}, u32[]{:S(2)}) collective-permute-start(f32[2,32,128]{2,1,0:T(8,128)S(1)} %dynamic-slice_bitcast_fusion), channel_id=1, source_target_pairs={{0,16},{4,20},{8,24},{12,28},{16,0},{20,4},{24,8},{28,12},{1,17},{... | collective-permute-start | bytes 98312 | tf_op jit(solution)/shard_map/ppermute | solution.py:25
  124.3 1.3 collective-permute-done.24
  125.6 4.9 %collective-permute-start.25 = (f32[2,32,128]{2,1,0:T(8,128)S(1)}, f32[2,32,128]{2,1,0:T(8,128)S(1)}, u32[]{:S(2)}, u32[]{:S(2)}) collective-permute-start(f32[2,32,128]{2,1,0:T(8,128)S(1)} %bitcast_add_fusion.refs_0_), channel_id=1, source_target_pairs={{0,1},{1,2},{2,3},{3,0},{4,5},{5,6},{6,7},{7,4},{8,9},{9,10},{10,1... | collective-permute-start | bytes 98312 | tf_op jit(solution)/shard_map/ppermute | solution.py:25
  130.4 0.5 collective-permute-start.27
  130.9 0.6 collective-permute-done.25.refs_1_
  131.4 1.7 %collective-permute-done.26.refs_2_ = f32[2,32,128]{2,1,0:T(8,128)S(1)} collective-permute-done((f32[2,32,128]{2,1,0:T(8,128)S(1)}, f32[2,32,128]{2,1,0:T(8,128)S(1)}, u32[]{:S(2)}, u32[]{:S(2)}) %collective-permute-start.26) | collective-permute-done | bytes 32800 | tf_op jit(solution)/shard_map/ppermute | solution.py:25
  133.2 0.6 collective-permute-done.27.refs_3_
  133.8 0.8 shard_map.44
  (37 shorter events, 0.2 us)
Async XLA Ops:
  0.0 2.4 %copy-start = (f32[1,2,32,3,6400]{4,2,3,1,0:T(8,128)S(1)}, f32[1,2,32,3,6400]{4,2,3,1,0:T(8,128)}, u32[]{:S(2)}) copy-start(f32[1,2,32,3,6400]{4,2,3,1,0:T(8,128)} %param.3) | copy-start | bytes 14745604
  2.8 18.0 %collective-permute-start.1 = (f32[2,32,896]{2,1,0:T(8,128)S(1)}, f32[2,32,896]{2,1,0:T(8,128)S(1)}, u32[]{:S(2)}, u32[]{:S(2)}) collective-permute-start(f32[2,32,896]{2,1,0:T(8,128)S(1)} %get-tuple-element.33), channel_id=1, source_target_pairs={{0,4},{4,8},{8,12},{12,16},{16,20},{20,24},{24,28},{28,0},{1,5},{5... | collective-permute-start | bytes 688136 | tf_op jit(solution)/shard_map/ppermute | solution.py:25
  4.9 16.2 %collective-permute-start.2 = (f32[2,32,896]{2,1,0:T(8,128)S(1)}, f32[2,32,896]{2,1,0:T(8,128)S(1)}, u32[]{:S(2)}, u32[]{:S(2)}) collective-permute-start(f32[2,32,896]{2,1,0:T(8,128)S(1)} %get-tuple-element.34), channel_id=1, source_target_pairs={{0,20},{4,24},{8,28},{12,0},{16,4},{20,8},{24,12},{28,16},{1,21},{... | collective-permute-start | bytes 688136 | tf_op jit(solution)/shard_map/ppermute | solution.py:25
  8.2 19.1 %collective-permute-start.3 = (f32[2,32,896]{2,1,0:T(8,128)S(1)}, f32[2,32,896]{2,1,0:T(8,128)S(1)}, u32[]{:S(2)}, u32[]{:S(2)}) collective-permute-start(f32[2,32,896]{2,1,0:T(8,128)S(1)} %get-tuple-element.35), channel_id=1, source_target_pairs={{0,8},{4,12},{8,16},{12,20},{16,24},{20,28},{24,0},{28,4},{1,9},{5... | collective-permute-start | bytes 688136 | tf_op jit(solution)/shard_map/ppermute | solution.py:25
  8.3 25.8 %collective-permute-start.4 = (f32[2,32,896]{2,1,0:T(8,128)S(1)}, f32[2,32,896]{2,1,0:T(8,128)S(1)}, u32[]{:S(2)}, u32[]{:S(2)}) collective-permute-start(f32[2,32,896]{2,1,0:T(8,128)S(1)} %get-tuple-element.36), channel_id=1, source_target_pairs={{0,12},{4,16},{8,20},{12,24},{16,28},{20,0},{24,4},{28,8},{1,13},{... | collective-permute-start | bytes 688136 | tf_op jit(solution)/shard_map/ppermute | solution.py:25
  8.6 25.8 %collective-permute-start.5 = (f32[2,32,896]{2,1,0:T(8,128)S(1)}, f32[2,32,896]{2,1,0:T(8,128)S(1)}, u32[]{:S(2)}, u32[]{:S(2)}) collective-permute-start(f32[2,32,896]{2,1,0:T(8,128)S(1)} %get-tuple-element.37), channel_id=1, source_target_pairs={{0,28},{4,0},{8,4},{12,8},{16,12},{20,16},{24,20},{28,24},{1,29},{... | collective-permute-start | bytes 688136 | tf_op jit(solution)/shard_map/ppermute | solution.py:25
  12.5 8.1 %copy-start.9 = (f32[2,3]{1,0:T(2,128)S(1)}, f32[2,3]{1,0:T(2,128)}, u32[]{:S(2)}) copy-start(f32[2,3]{1,0:T(2,128)} %param.4) | copy-start | bytes 76
  12.5 8.1 %copy-start.8 = (s32[8,2,3]{0,1,2:T(2,128)S(1)}, s32[8,2,3]{0,1,2:T(2,128)}, u32[]{:S(2)}) copy-start(s32[8,2,3]{0,1,2:T(2,128)} %param.5) | copy-start | bytes 580
  14.2 2.4 %copy-start.1 = (f32[1,2,32,3,6400]{4,2,3,1,0:T(8,128)S(1)}, f32[1,2,32,3,6400]{4,2,3,1,0:T(8,128)}, u32[]{:S(2)}) copy-start(f32[1,2,32,3,6400]{4,2,3,1,0:T(8,128)} %param.3) | copy-start | bytes 14745604
  17.1 0.7 copy-start.3
  17.8 0.7 copy-start.4
  18.5 0.7 copy-start.5
  19.2 0.7 copy-start.6
  19.9 0.7 copy-start.7
  20.8 29.4 %collective-permute-start.6 = (f32[2,32,896]{2,1,0:T(8,128)S(1)}, f32[2,32,896]{2,1,0:T(8,128)S(1)}, u32[]{:S(2)}, u32[]{:S(2)}) collective-permute-start(f32[2,32,896]{2,1,0:T(8,128)S(1)} %get-tuple-element.38), channel_id=1, source_target_pairs={{0,24},{4,28},{8,0},{12,4},{16,8},{20,12},{24,16},{28,20},{1,25},{... | collective-permute-start | bytes 688136 | tf_op jit(solution)/shard_map/ppermute | solution.py:25
  21.1 41.3 %collective-permute-start = (f32[2,32,896]{2,1,0:T(8,128)}, f32[2,32,896]{2,1,0:T(8,128)S(1)}, u32[]{:S(2)}, u32[]{:S(2)}) collective-permute-start(f32[2,32,896]{2,1,0:T(8,128)} %shard_map.37), channel_id=1, source_target_pairs={{0,16},{4,20},{8,24},{12,28},{16,0},{20,4},{24,8},{28,12},{1,17},{... | collective-permute-start | bytes 688136 | tf_op jit(solution)/shard_map/ppermute | solution.py:25
  27.3 45.0 %collective-permute-start.14 = (f32[2,32,896]{2,1,0:T(8,128)}, f32[2,32,896]{2,1,0:T(8,128)S(1)}, u32[]{:S(2)}, u32[]{:S(2)}) collective-permute-start(f32[2,32,896]{2,1,0:T(8,128)} %copy-done.7), channel_id=1, source_target_pairs={{0,16},{4,20},{8,24},{12,28},{16,0},{20,4},{24,8},{28,12},{1,17},{... | collective-permute-start | bytes 688136 | tf_op jit(solution)/shard_map/ppermute | solution.py:25
  34.2 38.1 %collective-permute-start.15 = (f32[2,32,896]{2,1,0:T(8,128)}, f32[2,32,896]{2,1,0:T(8,128)S(1)}, u32[]{:S(2)}, u32[]{:S(2)}) collective-permute-start(f32[2,32,896]{2,1,0:T(8,128)} %copy-done.6), channel_id=1, source_target_pairs={{0,4},{4,8},{8,12},{12,16},{16,20},{20,24},{24,28},{28,0},{1,5},{5... | collective-permute-start | bytes 688136 | tf_op jit(solution)/shard_map/ppermute | solution.py:25
  34.4 44.0 %collective-permute-start.16 = (f32[2,32,896]{2,1,0:T(8,128)}, f32[2,32,896]{2,1,0:T(8,128)S(1)}, u32[]{:S(2)}, u32[]{:S(2)}) collective-permute-start(f32[2,32,896]{2,1,0:T(8,128)} %copy-done.5), channel_id=1, source_target_pairs={{0,20},{4,24},{8,28},{12,0},{16,4},{20,8},{24,12},{28,16},{1,21},{... | collective-permute-start | bytes 688136 | tf_op jit(solution)/shard_map/ppermute | solution.py:25
  50.2 29.2 %collective-permute-start.17 = (f32[2,32,896]{2,1,0:T(8,128)}, f32[2,32,896]{2,1,0:T(8,128)S(1)}, u32[]{:S(2)}, u32[]{:S(2)}) collective-permute-start(f32[2,32,896]{2,1,0:T(8,128)} %copy-done.4), channel_id=1, source_target_pairs={{0,8},{4,12},{8,16},{12,20},{16,24},{20,28},{24,0},{28,4},{1,9},{5... | collective-permute-start | bytes 688136 | tf_op jit(solution)/shard_map/ppermute | solution.py:25
  62.4 20.5 %collective-permute-start.18 = (f32[2,32,896]{2,1,0:T(8,128)}, f32[2,32,896]{2,1,0:T(8,128)S(1)}, u32[]{:S(2)}, u32[]{:S(2)}) collective-permute-start(f32[2,32,896]{2,1,0:T(8,128)} %copy-done.3), channel_id=1, source_target_pairs={{0,12},{4,16},{8,20},{12,24},{16,28},{20,0},{24,4},{28,8},{1,13},{... | collective-permute-start | bytes 688136 | tf_op jit(solution)/shard_map/ppermute | solution.py:25
  72.3 11.6 %collective-permute-start.19 = (f32[2,32,896]{2,1,0:T(8,128)S(1)}, f32[2,32,896]{2,1,0:T(8,128)S(1)}, u32[]{:S(2)}, u32[]{:S(2)}) collective-permute-start(f32[2,32,896]{2,1,0:T(8,128)S(1)} %get-tuple-element.54), channel_id=1, source_target_pairs={{0,28},{4,0},{8,4},{12,8},{16,12},{20,16},{24,20},{28,24},{1,29},{... | collective-permute-start | bytes 688136 | tf_op jit(solution)/shard_map/ppermute | solution.py:25
  72.3 22.8 %collective-permute-start.20 = (f32[2,32,896]{2,1,0:T(8,128)S(1)}, f32[2,32,896]{2,1,0:T(8,128)S(1)}, u32[]{:S(2)}, u32[]{:S(2)}) collective-permute-start(f32[2,32,896]{2,1,0:T(8,128)S(1)} %get-tuple-element.55), channel_id=1, source_target_pairs={{0,24},{4,28},{8,0},{12,4},{16,8},{20,12},{24,16},{28,20},{1,25},{... | collective-permute-start | bytes 688136 | tf_op jit(solution)/shard_map/ppermute | solution.py:25
  75.6 2.4 %copy-start.2 = (f32[1,2,32,3,6400]{4,2,3,1,0:T(8,128)S(1)}, f32[1,2,32,3,6400]{4,2,3,1,0:T(8,128)}, u32[]{:S(2)}) copy-start(f32[1,2,32,3,6400]{4,2,3,1,0:T(8,128)} %param.3) | copy-start | bytes 14745604
  78.5 16.6 %collective-permute-start.10 = (f32[2,32,640]{2,1,0:T(8,128)S(1)}, f32[2,32,640]{2,1,0:T(8,128)S(1)}, u32[]{:S(2)}, u32[]{:S(2)}) collective-permute-start(f32[2,32,640]{2,1,0:T(8,128)S(1)} %get-tuple-element.44), channel_id=1, source_target_pairs={{0,8},{4,12},{8,16},{12,20},{16,24},{20,28},{24,0},{28,4},{1,9},{5... | collective-permute-start | bytes 491528 | tf_op jit(solution)/shard_map/ppermute | solution.py:25
  79.4 18.9 %collective-permute-start.11 = (f32[2,32,640]{2,1,0:T(8,128)S(1)}, f32[2,32,640]{2,1,0:T(8,128)S(1)}, u32[]{:S(2)}, u32[]{:S(2)}) collective-permute-start(f32[2,32,640]{2,1,0:T(8,128)S(1)} %get-tuple-element.45), channel_id=1, source_target_pairs={{0,12},{4,16},{8,20},{12,24},{16,28},{20,0},{24,4},{28,8},{1,13},{... | collective-permute-start | bytes 491528 | tf_op jit(solution)/shard_map/ppermute | solution.py:25
  82.9 25.2 %collective-permute-start.12 = (f32[2,32,640]{2,1,0:T(8,128)S(1)}, f32[2,32,640]{2,1,0:T(8,128)S(1)}, u32[]{:S(2)}, u32[]{:S(2)}) collective-permute-start(f32[2,32,640]{2,1,0:T(8,128)S(1)} %get-tuple-element.46), channel_id=1, source_target_pairs={{0,28},{4,0},{8,4},{12,8},{16,12},{20,16},{24,20},{28,24},{1,29},{... | collective-permute-start | bytes 491528 | tf_op jit(solution)/shard_map/ppermute | solution.py:25
  83.9 24.3 %collective-permute-start.13 = (f32[2,32,640]{2,1,0:T(8,128)S(1)}, f32[2,32,640]{2,1,0:T(8,128)S(1)}, u32[]{:S(2)}, u32[]{:S(2)}) collective-permute-start(f32[2,32,640]{2,1,0:T(8,128)S(1)} %get-tuple-element.47), channel_id=1, source_target_pairs={{0,24},{4,28},{8,0},{12,4},{16,8},{20,12},{24,16},{28,20},{1,25},{... | collective-permute-start | bytes 491528 | tf_op jit(solution)/shard_map/ppermute | solution.py:25
  95.1 14.7 %collective-permute-start.7 = (f32[2,32,640]{2,1,0:T(8,128)S(1)}, f32[2,32,640]{2,1,0:T(8,128)S(1)}, u32[]{:S(2)}, u32[]{:S(2)}) collective-permute-start(f32[2,32,640]{2,1,0:T(8,128)S(1)} %get-tuple-element.41), channel_id=1, source_target_pairs={{0,16},{4,20},{8,24},{12,28},{16,0},{20,4},{24,8},{28,12},{1,17},{... | collective-permute-start | bytes 491528 | tf_op jit(solution)/shard_map/ppermute | solution.py:25
  95.1 14.7 %collective-permute-start.8 = (f32[2,32,640]{2,1,0:T(8,128)S(1)}, f32[2,32,640]{2,1,0:T(8,128)S(1)}, u32[]{:S(2)}, u32[]{:S(2)}) collective-permute-start(f32[2,32,640]{2,1,0:T(8,128)S(1)} %get-tuple-element.42), channel_id=1, source_target_pairs={{0,4},{4,8},{8,12},{12,16},{16,20},{20,24},{24,28},{28,0},{1,5},{5... | collective-permute-start | bytes 491528 | tf_op jit(solution)/shard_map/ppermute | solution.py:25
  98.4 11.5 %collective-permute-start.9 = (f32[2,32,640]{2,1,0:T(8,128)S(1)}, f32[2,32,640]{2,1,0:T(8,128)S(1)}, u32[]{:S(2)}, u32[]{:S(2)}) collective-permute-start(f32[2,32,640]{2,1,0:T(8,128)S(1)} %get-tuple-element.43), channel_id=1, source_target_pairs={{0,20},{4,24},{8,28},{12,0},{16,4},{20,8},{24,12},{28,16},{1,21},{... | collective-permute-start | bytes 491528 | tf_op jit(solution)/shard_map/ppermute | solution.py:25
  111.2 8.8 %collective-permute-start.21 = (f32[2,2,32,128]{3,2,1,0:T(8,128)S(1)}, f32[2,2,32,128]{3,2,1,0:T(8,128)S(1)}, u32[]{:S(2)}, u32[]{:S(2)}) collective-permute-start(f32[2,2,32,128]{3,2,1,0:T(8,128)S(1)} %get-tuple-element.58), channel_id=1, source_target_pairs={{0,4},{4,8},{8,12},{12,0},{16,20},{20,24},{24,28},{28,16},{1,5},{5... | collective-permute-start | bytes 196616 | tf_op jit(solution)/shard_map/ppermute | solution.py:304
  117.7 3.1 %collective-permute-start.22 = (f32[2,2,32,128]{3,2,1,0:T(8,128)S(1)}, f32[2,2,32,128]{3,2,1,0:T(8,128)S(1)}, u32[]{:S(2)}, u32[]{:S(2)}) collective-permute-start(f32[2,2,32,128]{3,2,1,0:T(8,128)S(1)} %get-tuple-element.59), channel_id=1, source_target_pairs={{0,8},{4,12},{8,0},{12,4},{16,24},{20,28},{24,16},{28,20},{1,9},{5... | collective-permute-start | bytes 196616 | tf_op jit(solution)/shard_map/ppermute | solution.py:304
  117.8 3.9 %collective-permute-start.23 = (f32[2,2,32,128]{3,2,1,0:T(8,128)S(1)}, f32[2,2,32,128]{3,2,1,0:T(8,128)S(1)}, u32[]{:S(2)}, u32[]{:S(2)}) collective-permute-start(f32[2,2,32,128]{3,2,1,0:T(8,128)S(1)} %get-tuple-element.60), channel_id=1, source_target_pairs={{0,12},{4,0},{8,4},{12,8},{16,28},{20,16},{24,20},{28,24},{1,13},{... | collective-permute-start | bytes 196616 | tf_op jit(solution)/shard_map/ppermute | solution.py:304
  121.7 3.9 %collective-permute-start.24 = (f32[2,32,128]{2,1,0:T(8,128)S(1)}, f32[2,32,128]{2,1,0:T(8,128)S(1)}, u32[]{:S(2)}, u32[]{:S(2)}) collective-permute-start(f32[2,32,128]{2,1,0:T(8,128)S(1)} %dynamic-slice_bitcast_fusion), channel_id=1, source_target_pairs={{0,16},{4,20},{8,24},{12,28},{16,0},{20,4},{24,8},{28,12},{1,17},{... | collective-permute-start | bytes 98312 | tf_op jit(solution)/shard_map/ppermute | solution.py:25
  125.6 5.9 %collective-permute-start.25 = (f32[2,32,128]{2,1,0:T(8,128)S(1)}, f32[2,32,128]{2,1,0:T(8,128)S(1)}, u32[]{:S(2)}, u32[]{:S(2)}) collective-permute-start(f32[2,32,128]{2,1,0:T(8,128)S(1)} %bitcast_add_fusion.refs_0_), channel_id=1, source_target_pairs={{0,1},{1,2},{2,3},{3,0},{4,5},{5,6},{6,7},{7,4},{8,9},{9,10},{10,1... | collective-permute-start | bytes 98312 | tf_op jit(solution)/shard_map/ppermute | solution.py:25
  130.4 2.8 %collective-permute-start.26 = (f32[2,32,128]{2,1,0:T(8,128)S(1)}, f32[2,32,128]{2,1,0:T(8,128)S(1)}, u32[]{:S(2)}, u32[]{:S(2)}) collective-permute-start(f32[2,32,128]{2,1,0:T(8,128)S(1)} %bitcast_add_fusion.refs_0_), channel_id=1, source_target_pairs={{0,2},{1,3},{2,0},{3,1},{4,6},{5,7},{6,4},{7,5},{8,10},{9,11},{10,... | collective-permute-start | bytes 98312 | tf_op jit(solution)/shard_map/ppermute | solution.py:25
  130.4 3.4 %collective-permute-start.27 = (f32[2,32,128]{2,1,0:T(8,128)S(1)}, f32[2,32,128]{2,1,0:T(8,128)S(1)}, u32[]{:S(2)}, u32[]{:S(2)}) collective-permute-start(f32[2,32,128]{2,1,0:T(8,128)S(1)} %bitcast_add_fusion.refs_0_), channel_id=1, source_target_pairs={{0,3},{1,0},{2,1},{3,2},{4,7},{5,4},{6,5},{7,6},{8,11},{9,8},{10,9... | collective-permute-start | bytes 98312 | tf_op jit(solution)/shard_map/ppermute | solution.py:25

commit v4 on v3

--- a/solution.py
+++ b/solution.py
@@ -12,9 +12,12 @@
 GY = 40
 KX = 4
 LANES = 128
-SHARES = (0.37,0.37,0.26)
+SHARES = (0.37, 0.37, 0.26)
 AHEAD = 2
-EARLY = 1
+GATE = 3
+ORDERS = {8: ((2, 4, 3, 6, 7, 5, 1), (4, 7, 3, 5, 1, 2, 6), (4, 7, 3, 6, 5, 2, 1))}
+FIRST = (3, 0, 1)
+ROOM = 50
 
 two_pi = 2.0 * math.pi
 
@@ -52,6 +55,11 @@
         self.main = tiles // count
         self.rest = tiles - self.main * count
         self.extra = -(-components * self.rest // count)
+        self.tail = 0
+        if components * self.rest * LANES % count == 0:
+            share = components * self.rest * LANES // count
+            if 0 < share < LANES and share % (LANES - share) == 0:
+                self.tail = share
         self.units = components * self.main + self.extra
 
     def pieces(self, start, stop):
@@ -68,6 +76,12 @@
             unit += length
         return runs
 
+    def has_tail(self, stop):
+        return self.tail > 0 and stop == self.units
+
+    def folded(self, rows):
+        return rows * self.tail // LANES
+
     def extra_unit(self, part, slot):
         number = slot * self.count + part
         valid = number < self.components * self.rest
@@ -89,7 +103,13 @@
         cells, valid = [], []
         lane = jnp.arange(LANES, dtype=jnp.int32)
         for component, tile, length in self.pieces(start, stop):
-            if component is None:
+            if component is None and self.tail:
+                place = part * self.tail + lane
+                unit = jnp.minimum(place // LANES, self.components * self.rest - 1)
+                at = self.main * self.count + unit % self.rest
+                cells.append(at * LANES + place % LANES)
+                valid.append((lane < self.tail).astype(jnp.float32))
+            elif component is None:
                 _, at, good = self.extra_unit(part, tile)
                 cells.append(at * LANES + lane)
                 valid.append(jnp.full((LANES,), 1.0, jnp.float32) * good.astype(jnp.float32))
@@ -158,6 +178,94 @@
     )(field)
 
 
+def fold(rows, tail):
+    kept = rows.shape[0] * tail // LANES
+    spare = LANES - tail
+    lane = lax.broadcasted_iota(jnp.int32, (kept, LANES), 1)
+    moved = [pltpu.roll(rows[kept:], tail - spare * turn, 1) for turn in range(tail // spare)]
+    return jnp.where(lane < tail, rows[:kept], jnp.concatenate(moved, axis=0))
+
+
+def unfold(rows, tail):
+    kept = rows.shape[0]
+    spare = LANES - tail
+    size = kept * spare // tail
+    lane = lax.broadcasted_iota(jnp.int32, (size, LANES), 1)
+    last = jnp.zeros((size, LANES), jnp.float32)
+    for turn in range(tail // spare):
+        back = pltpu.roll(rows[turn * size : (turn + 1) * size], spare * (turn + 1), 1)
+        last = jnp.where(lane // spare == turn, back, last)
+    whole = jnp.concatenate([rows, last], axis=0)
+    lane = lax.broadcasted_iota(jnp.int32, whole.shape, 1)
+    return jnp.where(lane < tail, whole, 0.0)
+
+
+def pack_tail_kernel(parts, turns, start, stop, field_ref, *refs):
+    outs, (held, packed, sems) = refs[:-3], refs[-3:]
+    me = lax.axis_index("ka")
+    bands = field_ref.shape[2]
+    first, copies = [], []
+
+    def copy(source, target):
+        sem = sems.at[len(first) + len(copies)]
+        return pltpu.make_async_copy(source, target, sem)
+
+    for unit in range(parts.components * parts.rest):
+        component, tile = divmod(unit, parts.rest)
+        origin = (parts.main * parts.count + tile) * LANES
+        first.append(copy(field_ref.at[:, component, :, pl.ds(origin, LANES)], held.at[unit]))
+    owners = [lax.rem(me + (parts.count - turn), parts.count) for turn in turns]
+    for part, out_ref in zip(owners, outs):
+        for unit in range(start, stop - 1):
+            component, tile = divmod(unit, parts.main)
+            origin = pl.multiple_of((part * parts.main + tile) * LANES, LANES)
+            for half in range(2):
+                rows = pl.ds((2 * (unit - start) + half) * bands, bands)
+                source = field_ref.at[half, component, :, pl.ds(origin, LANES)]
+                copies.append(copy(source, out_ref.at[rows]))
+    for each in first + copies:
+        each.start()
+    for each in first:
+        each.wait()
+    lane = lax.broadcasted_iota(jnp.int32, (2 * bands, LANES), 1)
+    for part in range(parts.count):
+        unit, shift = divmod(part * parts.tail, LANES)
+        rows = held[unit].reshape(2 * bands, LANES)
+        if shift:
+            rows = pltpu.roll(rows, LANES - shift, 1)
+        if shift + parts.tail > LANES:
+            after = pltpu.roll(held[unit + 1].reshape(2 * bands, LANES), LANES - shift, 1)
+            rows = jnp.where(lane < LANES - shift, rows, after)
+        packed[part] = fold(rows, parts.tail)
+    at = 2 * bands * (stop - 1 - start)
+    for part, out_ref in zip(owners, outs):
+        out_ref[at:] = packed[part]
+    for each in copies:
+        each.wait()
+
+
+def pack_tail(parts, field, turns, start, stop):
+    bands = field.shape[2]
+    folded = parts.folded(2 * bands)
+    shape = (2 * bands * (stop - 1 - start) + folded, LANES)
+    units = parts.components * parts.rest
+    copies = units + 2 * len(turns) * (stop - 1 - start)
+    size = 4 * math.prod(shape) * len(turns)
+    return pl.pallas_call(
+        functools.partial(pack_tail_kernel, parts, turns, start, stop),
+        out_shape=[jax.ShapeDtypeStruct(shape, jnp.float32)] * len(turns),
+        in_specs=[pl.BlockSpec(memory_space=pl.ANY)],
+        out_specs=[pl.BlockSpec(memory_space=pltpu.VMEM)] * len(turns),
+        scratch_shapes=[
+            pltpu.VMEM((units, 2, bands, LANES), jnp.float32),
+            pltpu.VMEM((parts.count, folded, LANES), jnp.float32),
+            pltpu.SemaphoreType.DMA((copies,)),
+        ],
+        compiler_params=pltpu.CompilerParams(vmem_limit_bytes=5 * 1024 * 1024),
+        cost_estimate=pl.CostEstimate(flops=0, bytes_accessed=2 * size, transcendentals=0),
+    )(field)
+
+
 def forward_matrices(rows):
     bands, width = rows.shape[0] // 2, rows.shape[1]
     lane = lax.broadcasted_iota(jnp.int32, (bands, width), 1)
@@ -188,7 +296,7 @@
                 out_ref[group, 1] = back
 
 
-def chunk_kernel(offsets, first, factor, turns, start, *refs):
+def chunk_kernel(offsets, first, factor, turns, start, bands, tail, *refs):
     count = len(turns)
     fields = {turn: ref for turn, ref in zip(turns, refs)}
     cosine_ref, sine_ref = refs[count : count + 2]
@@ -196,16 +304,28 @@
     before_ref = None
     if not first:
         before_ref, outs = outs[0], outs[1:]
+    if tail:
+        *outs, tails = outs
+        at = fields[0].shape[0] // (2 * bands) * 2 * bands
+        for step in range(count):
+            tails[step] = unfold(fields[step][at:], tail)
+
+    def rows_of(step):
+        ref = fields[step]
+        if not tail:
+            return ref[...].reshape(2 * bands, ref.shape[2])
+        units = [ref[row : row + 2 * bands] for row in range(0, at, 2 * bands)]
+        return jnp.concatenate(units + [tails[step]], axis=1)
+
     forward = []
     for step in range(count):
-        left = fields[step][...]
-        bands, cells = left.shape[1], left.shape[2]
-        left_high, left_low = split_parts(left.reshape(2 * bands, cells))
+        left_high, left_low = split_parts(rows_of(step))
         left_rows = jnp.concatenate([left_high, left_low], axis=0)
+        cells = left_rows.shape[1]
         highs, lows = [], []
         for direction, offset in enumerate(offsets):
-            right = fields[(step + offset) % count]
-            right_real, right_imag = right[0], right[1]
+            right = rows_of((step + offset) % count)
+            right_real, right_imag = right[:bands], right[bands:]
             row = step * len(offsets) + direction
             cosine = cosine_ref[row : row + 1, start : start + cells]
             sine = sine_ref[row : row + 1, start : start + cells]
@@ -234,9 +354,9 @@
         write_messages(offsets, factor, forward, outs)
 
 
-def chunk_products(blocks, turns, start, cosine, sine, before, offsets, factor):
+def chunk_products(blocks, turns, start, cells, tail, cosine, sine, before, offsets, factor):
     count = len(blocks)
-    _, bands, cells = blocks[0].shape
+    bands = blocks[0].size // (2 * (cells - LANES + tail if tail else cells))
     width = 2 * len(offsets) * bands
     operands = list(blocks) + [cosine, sine]
     if before is not None:
@@ -250,10 +370,11 @@
         out_specs = inside
     flops = 2 * count * (4 * bands) * (2 * width) * cells
     return pl.pallas_call(
-        functools.partial(chunk_kernel, offsets, before is None, factor, turns, start),
+        functools.partial(chunk_kernel, offsets, before is None, factor, turns, start, bands, tail),
         out_shape=out_shape,
         in_specs=[inside] * len(operands),
         out_specs=out_specs,
+        scratch_shapes=[pltpu.VMEM((count, 2 * bands, LANES), jnp.float32)] if tail else [],
         compiler_params=pltpu.CompilerParams(vmem_limit_bytes=16 * 1024 * 1024),
         cost_estimate=pl.CostEstimate(
             flops=flops, bytes_accessed=4 * count * 2 * bands * cells, transcendentals=0
@@ -262,7 +383,11 @@
 
 
 def block_factor(count):
-    return min(factor for factor in range(1, count + 1) if count % factor == 0 and factor**2 >= count)
+    best = 1
+    for factor in range(1, math.isqrt(count) + 1):
+        if count % factor == 0:
+            best = factor
+    return best
 
 
 def result_kernel(*refs):
@@ -333,24 +458,41 @@
     cosine = jnp.cos(angles) * valid
     sine = jnp.sin(angles) * valid
 
-    turns = exchange(count)
+    orders = ORDERS.get(count, [exchange(count)] * len(SHARES))
+    gate = min(GATE, count - 2)
     factor = block_factor(count)
     bounds = chunk_bounds(parts.units)
-    totals = []
-    for chunk, (start, stop) in enumerate(zip(bounds[:-1], bounds[1:])):
-        source = field
-        if chunk >= AHEAD:
-            source, totals[chunk - AHEAD] = lax.optimization_barrier((field, totals[chunk - AHEAD]))
-        early = EARLY if chunk == 0 else 0
-        sent = pack(parts, source, turns[:early], start, stop, 60) if early else []
-        sent += pack(parts, source, turns[early:] + [0], start, stop, 4)
-        blocks = [shifted(value, "ka", -turn) for value, turn in zip(sent, turns)] + [sent[-1]]
+    totals, blocks, extent = [], None, None
+
+    def multiply(blocks, turns, start, stop):
         totals.append(
             chunk_products(
-                blocks, turns + [0], start * LANES, cosine, sine,
+                blocks, turns + [0], start * LANES, (stop - start) * LANES,
+                parts.tail if parts.has_tail(stop) else 0, cosine, sine,
                 totals[-1] if totals else None, offsets, factor if stop == parts.units else 0,
             )
         )
+
+    for chunk, (start, stop) in enumerate(zip(bounds[:-1], bounds[1:])):
+        turns = list(orders[chunk])
+        source = field
+        if chunk >= AHEAD:
+            source, totals[chunk - AHEAD] = lax.optimization_barrier((source, totals[chunk - AHEAD]))
+        if chunk >= 1:
+            source, blocks[gate] = lax.optimization_barrier((source, blocks[gate]))
+            multiply(blocks, *extent)
+        if parts.has_tail(stop):
+            sent = pack_tail(parts, source, turns + [0], start, stop)
+        else:
+            first = [turns[at] for at in FIRST] if start == 0 else []
+            others = [turn for turn in turns + [0] if turn not in first]
+            room = 4 if start else ROOM
+            found = dict(zip(first, pack(parts, source, first, start, stop, room))) if first else {}
+            found.update(zip(others, pack(parts, source, others, start, stop, room)))
+            sent = [found[turn] for turn in turns + [0]]
+        blocks = [shifted(value, "ka", -turn) for value, turn in zip(sent, turns)] + [sent[-1]]
+        extent = turns, start, stop
+    multiply(blocks, *extent)
 
     share = reduced_over_points(totals[-1], factor)
     shares = [share] + [shifted(share, "gz", step) for step in range(1, slabs)]

time: 135 us -> 131 us (0.970)
  waiting for transfers between devices: 47.4 us -> 35.5 us
  starting transfers between devices: 67.3 us -> 75.8 us
  local copies, waits for them, and re-layouts: 10.9 us -> 7.83 us
  Pallas kernels: 7.85 us -> 10.9 us
    ppermute x25 -> x27, starting transfers between devices: 58.5 us -> 74.9 us  [shifted(): return lax.ppermute(value, axis, pairs)]
    ppermute x25 -> x27, waiting for transfers between devices: 45.8 us -> 31.7 us  [shifted(): return lax.ppermute(value, axis, pairs)]
    ppermute x3 -> x1, starting transfers between devices: 8.84 us -> 0.89 us  [reduced_over_points(): total = total + lax.ppermute(blocks[turn], 'ka', pairs)]
    unnamed x21 -> x17, local copies, waits for them, and re-layouts: 10.7 us -> 7.62 us
    ppermute x3 -> x1, waiting for transfers between devices: 1.59 us -> 3.74 us  [reduced_over_points(): total = total + lax.ppermute(blocks[turn], 'ka', pairs)]
    pallas_call x4 -> x3, Pallas kernels: 3.01 us -> 4.72 us  [pack(): pl.pallas_call(functools.partial(pack_kernel, parts, turns, start, stop),...]
    pallas_call x0 -> x1, Pallas kernels: none -> 1.44 us  [pack_tail(): pl.pallas_call(functools.partial(pack_tail_kernel, parts, turns, start, s...]
  transfers between devices with their start and end apart: 28 -> 28, of which waited for: 13 -> 11; matrix products, arithmetic and copies ran while one was open for 1% -> 1% of each run, Pallas kernels for 4% -> 6%
where the time goes in v4:
time: 131 us
  starting transfers between devices  75.8 us (58%)
  waiting for transfers between devices  35.5 us (27%)
  Pallas kernels  10.9 us (8%)
  local copies, waits for them, and re-layouts  7.83 us (6%)
    ppermute x27, starting transfers between devices, shifted(): return lax.ppermute(value, axis, pairs)  74.9 us
    ppermute x27, waiting for transfers between devices, shifted(): return lax.ppermute(value, axis, pairs)  31.7 us
    unnamed x17, local copies, waits for them, and re-layouts  7.62 us
    pallas_call x3, Pallas kernels, pack(): pl.pallas_call(functools.partial(pack_kernel, parts, turns, start, stop),...  4.72 us
    pallas_call x3, Pallas kernels, chunk_products(): pl.pallas_call(functools.partial(chunk_kernel, offsets, before is None, f...  3.98 us
    ppermute x1, waiting for transfers between devices, reduced_over_points(): total = total + lax.ppermute(blocks[turn], 'ka', pairs)  3.74 us
  transfers between devices with their start and end apart: 28, of which 11 were waited for; matrix products, arithmetic and copies ran while one was open for 1% of the time, Pallas kernels for 6%

profile of v4, /device:TPU:1, one launch (start us, length us, event | category | flops | bytes accessed | tf_op | source)
XLA Modules:
  0.0 131.2 jit_solution(11835810606616618665)
XLA Ops:
  0.0 1.2 shard_map.37
  1.2 2.2 %collective-permute-start.3 = (f32[2,32,896]{2,1,0:T(8,128)S(1)}, f32[2,32,896]{2,1,0:T(8,128)S(1)}, u32[]{:S(2)}, u32[]{:S(2)}) collective-permute-start(f32[2,32,896]{2,1,0:T(8,128)S(1)} %get-tuple-element.40), channel_id=1, source_target_pairs={{0,8},{4,12},{8,16},{12,20},{16,24},{20,28},{24,0},{28,4},{1,9},{5... | collective-permute-start | bytes 688136 | tf_op jit(solution)/shard_map/ppermute | solution.py:28
  3.4 2.2 %shard_map.38 = (f32[2,32,896]{2,1,0:T(8,128)S(1)}, f32[2,32,896]{2,1,0:T(8,128)}, f32[2,32,896]{2,1,0:T(8,128)}, f32[2,32,896]{2,1,0:T(8,128)S(1)}, f32[2,32,896]{2,1,0:T(8,128)S(1)}) custom-call(f32[2,3,32,6400]{3,2,1,0:T(8,128)} %bitcast.22), custom_call_target="tpu_custom_call" | custom-call | bytes 2293760 | tf_op jit(solution)/shard_map/pallas_call | solution.py:168
  5.6 3.3 %collective-permute-start.2 = (f32[2,32,896]{2,1,0:T(8,128)S(1)}, f32[2,32,896]{2,1,0:T(8,128)S(1)}, u32[]{:S(2)}, u32[]{:S(2)}) collective-permute-start(f32[2,32,896]{2,1,0:T(8,128)S(1)} %get-tuple-element.39), channel_id=1, source_target_pairs={{0,20},{4,24},{8,28},{12,0},{16,4},{20,8},{24,12},{28,16},{1,21},{... | collective-permute-start | bytes 688136 | tf_op jit(solution)/shard_map/ppermute | solution.py:28
  9.0 1.2 collective-permute-start.5
  10.2 2.9 %collective-permute-start.6 = (f32[2,32,896]{2,1,0:T(8,128)S(1)}, f32[2,32,896]{2,1,0:T(8,128)S(1)}, u32[]{:S(2)}, u32[]{:S(2)}) collective-permute-start(f32[2,32,896]{2,1,0:T(8,128)S(1)} %get-tuple-element.44), channel_id=1, source_target_pairs={{0,28},{4,0},{8,4},{12,8},{16,12},{20,16},{24,20},{28,24},{1,29},{... | collective-permute-start | bytes 688136 | tf_op jit(solution)/shard_map/ppermute | solution.py:28
  13.3 0.1 copy.6
  13.4 0.1 convert_add_fusion
  13.4 0.0 collective-permute-done.3.refs_3_
  13.4 0.3 collective-permute-start
  13.7 2.4 %copy-done = f32[1,2,32,3,6400]{4,2,3,1,0:T(8,128)S(1)} copy-done((f32[1,2,32,3,6400]{4,2,3,1,0:T(8,128)S(1)}, f32[1,2,32,3,6400]{4,2,3,1,0:T(8,128)}, u32[]{:S(2)}) %copy-start) | copy-done | bytes 4915224
  16.1 1.3 shard_map.40
  17.4 0.7 copy-done.2
  18.1 0.7 copy-done.3
  18.8 0.7 copy-done.4
  19.5 0.7 copy-done.5
  20.2 5.4 %collective-permute-start.1 = (f32[2,32,896]{2,1,0:T(8,128)S(1)}, f32[2,32,896]{2,1,0:T(8,128)S(1)}, u32[]{:S(2)}, u32[]{:S(2)}) collective-permute-start(f32[2,32,896]{2,1,0:T(8,128)S(1)} %get-tuple-element.38), channel_id=1, source_target_pairs={{0,16},{4,20},{8,24},{12,28},{16,0},{20,4},{24,8},{28,12},{1,17},{... | collective-permute-start | bytes 688136 | tf_op jit(solution)/shard_map/ppermute | solution.py:28
  25.6 1.1 collective-permute-done.4.refs_4_
  26.7 0.0 collective-permute-start.7
  26.7 6.4 %collective-permute-done.5.refs_5_ = f32[2,32,896]{2,1,0:T(8,128)S(1)} collective-permute-done((f32[2,32,896]{2,1,0:T(8,128)}, f32[2,32,896]{2,1,0:T(8,128)S(1)}, u32[]{:S(2)}, u32[]{:S(2)}) %collective-permute-start.5) | collective-permute-done | bytes 229408 | tf_op jit(solution)/shard_map/ppermute | solution.py:28
  33.1 0.1 dynamic-slice_maximum_fusion
  33.2 0.1 copy.7
  33.3 0.1 reshape.160
  33.4 0.0 collective-permute-done.6.refs_6_
  33.4 9.1 %collective-permute-start.16 = (f32[2,32,896]{2,1,0:T(8,128)}, f32[2,32,896]{2,1,0:T(8,128)S(1)}, u32[]{:S(2)}, u32[]{:S(2)}) collective-permute-start(f32[2,32,896]{2,1,0:T(8,128)} %copy-done.5), channel_id=1, source_target_pairs={{0,4},{4,8},{8,12},{12,16},{16,20},{20,24},{24,28},{28,0},{1,5},{5... | collective-permute-start | bytes 688136 | tf_op jit(solution)/shard_map/ppermute | solution.py:28
  42.5 12.1 %collective-permute-start.17 = (f32[2,32,896]{2,1,0:T(8,128)}, f32[2,32,896]{2,1,0:T(8,128)S(1)}, u32[]{:S(2)}, u32[]{:S(2)}) collective-permute-start(f32[2,32,896]{2,1,0:T(8,128)} %copy-done.4), channel_id=1, source_target_pairs={{0,20},{4,24},{8,28},{12,0},{16,4},{20,8},{24,12},{28,16},{1,21},{... | collective-permute-start | bytes 688136 | tf_op jit(solution)/shard_map/ppermute | solution.py:28
  54.6 0.0 collective-permute-done.1.refs_1_
  54.6 3.4 %collective-permute-start.18 = (f32[2,32,896]{2,1,0:T(8,128)}, f32[2,32,896]{2,1,0:T(8,128)S(1)}, u32[]{:S(2)}, u32[]{:S(2)}) collective-permute-start(f32[2,32,896]{2,1,0:T(8,128)} %copy-done.3), channel_id=1, source_target_pairs={{0,28},{4,0},{8,4},{12,8},{16,12},{20,16},{24,20},{28,24},{1,29},{... | collective-permute-start | bytes 688136 | tf_op jit(solution)/shard_map/ppermute | solution.py:28
  58.0 8.6 %collective-permute-done.7.refs_3_ = f32[2,32,896]{2,1,0:T(8,128)S(1)} collective-permute-done((f32[2,32,896]{2,1,0:T(8,128)}, f32[2,32,896]{2,1,0:T(8,128)S(1)}, u32[]{:S(2)}, u32[]{:S(2)}) %collective-permute-start.7) | collective-permute-done | bytes 229408 | tf_op jit(solution)/shard_map/ppermute | solution.py:28
  66.6 0.0 collective-permute-start.19
  66.6 1.5 %collective-permute-start.20 = (f32[2,32,896]{2,1,0:T(8,128)S(1)}, f32[2,32,896]{2,1,0:T(8,128)S(1)}, u32[]{:S(2)}, u32[]{:S(2)}) collective-permute-start(f32[2,32,896]{2,1,0:T(8,128)S(1)} %get-tuple-element.64), channel_id=1, source_target_pairs={{0,8},{4,12},{8,16},{12,20},{16,24},{20,28},{24,0},{28,4},{1,9},{5... | collective-permute-start | bytes 688136 | tf_op jit(solution)/shard_map/ppermute | solution.py:28
  68.0 0.7 sine_multiply_fusion
  68.7 1.4 %shard_map.39.refs_10_ = f32[8,64,128]{2,1,0:T(8,128)S(1)} custom-call(f32[2,32,896]{2,1,0:T(8,128)S(1)} %collective-permute-done.refs_0_, f32[2,32,896]{2,1,0:T(8,128)S(1)} %collective-permute-done.1.refs_1_, f32[2,32,896]{2,1,0:T(8,128)S(1)} %collective-permute-done.2.refs_2_, f32[2,32,896]{2,1,0:T(8,128)S(1)} %collective-permute-done.3.refs_3_, ...), custom_call_target="tpu_custom_call" | custom-call | flops 469762048 | bytes 1835008 | tf_op jit(solution)/shard_map/pallas_call | solution.py:372
  70.1 0.0 copy-start.1
  70.1 2.4 %copy-done.1 = f32[1,2,32,3,6400]{4,2,3,1,0:T(8,128)S(1)} copy-done((f32[1,2,32,3,6400]{4,2,3,1,0:T(8,128)S(1)}, f32[1,2,32,3,6400]{4,2,3,1,0:T(8,128)}, u32[]{:S(2)}) %copy-start.1) | copy-done | bytes 4915224
  72.5 1.4 %shard_map.41 = (f32[304,128]{1,0:T(8,128)S(1)}, f32[304,128]{1,0:T(8,128)S(1)}, f32[304,128]{1,0:T(8,128)S(1)}, f32[304,128]{1,0:T(8,128)S(1)}, f32[304,128]{1,...) custom-call(f32[2,3,32,6400]{3,2,1,0:T(8,128)S(1)} %bitcast.24), custom_call_target="tpu_custom_call" | custom-call | bytes 2490368 | tf_op jit(solution)/shard_map/pallas_call | solution.py:254
  73.9 0.0 collective-permute-done.16.refs_1_
  73.9 10.0 %collective-permute-start.10 = (f32[304,128]{1,0:T(8,128)S(1)}, f32[304,128]{1,0:T(8,128)S(1)}, u32[]{:S(2)}, u32[]{:S(2)}) collective-permute-start(f32[304,128]{1,0:T(8,128)S(1)} %get-tuple-element.52), channel_id=1, source_target_pairs={{0,20},{4,24},{8,28},{12,0},{16,4},{20,8},{24,12},{28,16},{1,21},{... | collective-permute-start | bytes 466952 | tf_op jit(solution)/shard_map/ppermute | solution.py:28
  83.9 0.0 collective-permute-start.11
  83.9 0.3 collective-permute-start.12
  84.3 3.0 %collective-permute-start.13 = (f32[304,128]{1,0:T(8,128)S(1)}, f32[304,128]{1,0:T(8,128)S(1)}, u32[]{:S(2)}, u32[]{:S(2)}) collective-permute-start(f32[304,128]{1,0:T(8,128)S(1)} %get-tuple-element.55), channel_id=1, source_target_pairs={{0,24},{4,28},{8,0},{12,4},{16,8},{20,12},{24,16},{28,20},{1,25},{... | collective-permute-start | bytes 466952 | tf_op jit(solution)/shard_map/ppermute | solution.py:28
  87.3 1.2 collective-permute-start.14
  88.4 0.0 collective-permute-done.10.refs_2_
  88.5 9.5 %collective-permute-start.8 = (f32[304,128]{1,0:T(8,128)S(1)}, f32[304,128]{1,0:T(8,128)S(1)}, u32[]{:S(2)}, u32[]{:S(2)}) collective-permute-start(f32[304,128]{1,0:T(8,128)S(1)} %get-tuple-element.50), channel_id=1, source_target_pairs={{0,16},{4,20},{8,24},{12,28},{16,0},{20,4},{24,8},{28,12},{1,17},{... | collective-permute-start | bytes 466952 | tf_op jit(solution)/shard_map/ppermute | solution.py:28
  97.9 0.0 collective-permute-done.11.refs_3_
  97.9 1.9 %collective-permute-start.9 = (f32[304,128]{1,0:T(8,128)S(1)}, f32[304,128]{1,0:T(8,128)S(1)}, u32[]{:S(2)}, u32[]{:S(2)}) collective-permute-start(f32[304,128]{1,0:T(8,128)S(1)} %get-tuple-element.51), channel_id=1, source_target_pairs={{0,4},{4,8},{8,12},{12,16},{16,20},{20,24},{24,28},{28,0},{1,5},{5... | collective-permute-start | bytes 466952 | tf_op jit(solution)/shard_map/ppermute | solution.py:28
  99.9 1.3 %shard_map.42.refs_10_ = f32[8,64,128]{2,1,0:T(8,128)S(1)} custom-call(f32[2,32,896]{2,1,0:T(8,128)S(1)} %collective-permute-done.15.refs_0_, f32[2,32,896]{2,1,0:T(8,128)S(1)} %collective-permute-done.16.refs_1_, f32[2,32,896]{2,1,0:T(8,128)S(1)} %collective-permute-done.17.refs_2_, f32[2,32,896]{2,1,0:T(8,128)S(1)} %collective-permute-done.7.refs_3_, ...), custom_call_target="tpu_custom_call" | custom-call | flops 469762048 | bytes 1835008 | tf_op jit(solution)/shard_map/pallas_call | solution.py:372
  101.2 0.7 collective-permute-done.13.refs_5_
  102.0 10.0 %collective-permute-done.8.refs_0_ = f32[304,128]{1,0:T(8,128)S(1)} collective-permute-done((f32[304,128]{1,0:T(8,128)S(1)}, f32[304,128]{1,0:T(8,128)S(1)}, u32[]{:S(2)}, u32[]{:S(2)}) %collective-permute-start.8) | collective-permute-done | bytes 155680 | tf_op jit(solution)/shard_map/ppermute | solution.py:28
  112.0 1.3 shard_map.43
  113.3 0.9 collective-permute-start.21
  114.2 3.7 %collective-permute-done.21 = f32[4,2,32,128]{3,2,1,0:T(8,128)S(1)} collective-permute-done((f32[4,2,32,128]{3,2,1,0:T(8,128)S(1)}, f32[4,2,32,128]{3,2,1,0:T(8,128)S(1)}, u32[]{:S(2)}, u32[]{:S(2)}) %collective-permute-start.21) | collective-permute-done | bytes 131104 | tf_op jit(solution)/shard_map/ppermute | solution.py:429
  118.0 0.1 collective-permute-start.22
  118.0 0.2 collective-permute-start.23
  118.3 3.0 %collective-permute-start.24 = (f32[2,32,128]{2,1,0:T(8,128)S(1)}, f32[2,32,128]{2,1,0:T(8,128)S(1)}, u32[]{:S(2)}, u32[]{:S(2)}) collective-permute-start(f32[2,32,128]{2,1,0:T(8,128)S(1)} %get-tuple-element.70), channel_id=1, source_target_pairs={{0,24},{4,28},{8,0},{12,4},{16,8},{20,12},{24,16},{28,20},{1,25},{... | collective-permute-start | bytes 98312 | tf_op jit(solution)/shard_map/ppermute | solution.py:28
  121.3 1.3 collective-permute-done.22
  122.6 0.3 collective-permute-done.24
  123.0 3.9 %collective-permute-start.25 = (f32[2,32,128]{2,1,0:T(8,128)S(1)}, f32[2,32,128]{2,1,0:T(8,128)S(1)}, u32[]{:S(2)}, u32[]{:S(2)}) collective-permute-start(f32[2,32,128]{2,1,0:T(8,128)S(1)} %bitcast_add_fusion.refs_0_), channel_id=1, source_target_pairs={{0,1},{1,2},{2,3},{3,0},{4,5},{5,6},{6,7},{7,4},{8,9},{9,10},{10,1... | collective-permute-start | bytes 98312 | tf_op jit(solution)/shard_map/ppermute | solution.py:28
  126.8 0.2 collective-permute-start.26
  127.1 0.2 collective-permute-start.27
  127.3 0.6 collective-permute-done.25.refs_1_
  127.9 1.7 %collective-permute-done.26.refs_2_ = f32[2,32,128]{2,1,0:T(8,128)S(1)} collective-permute-done((f32[2,32,128]{2,1,0:T(8,128)S(1)}, f32[2,32,128]{2,1,0:T(8,128)S(1)}, u32[]{:S(2)}, u32[]{:S(2)}) %collective-permute-start.26) | collective-permute-done | bytes 32800 | tf_op jit(solution)/shard_map/ppermute | solution.py:28
  129.6 0.8 collective-permute-done.27.refs_3_
  130.4 0.8 shard_map.44
  (33 shorter events, 0.2 us)
Async XLA Ops:
  0.0 13.3 %copy-start.7 = (f32[2,3]{1,0:T(2,128)S(1)}, f32[2,3]{1,0:T(2,128)}, u32[]{:S(2)}) copy-start(f32[2,3]{1,0:T(2,128)} %param.4) | copy-start | bytes 76
  0.0 13.4 %copy-start.6 = (s32[8,2,3]{0,1,2:T(2,128)S(1)}, s32[8,2,3]{0,1,2:T(2,128)}, u32[]{:S(2)}) copy-start(s32[8,2,3]{0,1,2:T(2,128)} %param.5) | copy-start | bytes 580
  1.2 12.2 %collective-permute-start.3 = (f32[2,32,896]{2,1,0:T(8,128)S(1)}, f32[2,32,896]{2,1,0:T(8,128)S(1)}, u32[]{:S(2)}, u32[]{:S(2)}) collective-permute-start(f32[2,32,896]{2,1,0:T(8,128)S(1)} %get-tuple-element.40), channel_id=1, source_target_pairs={{0,8},{4,12},{8,16},{12,20},{16,24},{20,28},{24,0},{28,4},{1,9},{5... | collective-permute-start | bytes 688136 | tf_op jit(solution)/shard_map/ppermute | solution.py:28
  5.6 14.5 %collective-permute-start.2 = (f32[2,32,896]{2,1,0:T(8,128)S(1)}, f32[2,32,896]{2,1,0:T(8,128)S(1)}, u32[]{:S(2)}, u32[]{:S(2)}) collective-permute-start(f32[2,32,896]{2,1,0:T(8,128)S(1)} %get-tuple-element.39), channel_id=1, source_target_pairs={{0,20},{4,24},{8,28},{12,0},{16,4},{20,8},{24,12},{28,16},{1,21},{... | collective-permute-start | bytes 688136 | tf_op jit(solution)/shard_map/ppermute | solution.py:28
  9.0 17.7 %collective-permute-start.4 = (f32[2,32,896]{2,1,0:T(8,128)}, f32[2,32,896]{2,1,0:T(8,128)S(1)}, u32[]{:S(2)}, u32[]{:S(2)}) collective-permute-start(f32[2,32,896]{2,1,0:T(8,128)} %get-tuple-element.42), channel_id=1, source_target_pairs={{0,4},{4,8},{8,12},{12,16},{16,20},{20,24},{24,28},{28,0},{1,5},{5... | collective-permute-start | bytes 688136 | tf_op jit(solution)/shard_map/ppermute | solution.py:28
  9.0 24.1 %collective-permute-start.5 = (f32[2,32,896]{2,1,0:T(8,128)}, f32[2,32,896]{2,1,0:T(8,128)S(1)}, u32[]{:S(2)}, u32[]{:S(2)}) collective-permute-start(f32[2,32,896]{2,1,0:T(8,128)} %get-tuple-element.43), channel_id=1, source_target_pairs={{0,12},{4,16},{8,20},{12,24},{16,28},{20,0},{24,4},{28,8},{1,13},{... | collective-permute-start | bytes 688136 | tf_op jit(solution)/shard_map/ppermute | solution.py:28
  10.2 23.2 %collective-permute-start.6 = (f32[2,32,896]{2,1,0:T(8,128)S(1)}, f32[2,32,896]{2,1,0:T(8,128)S(1)}, u32[]{:S(2)}, u32[]{:S(2)}) collective-permute-start(f32[2,32,896]{2,1,0:T(8,128)S(1)} %get-tuple-element.44), channel_id=1, source_target_pairs={{0,28},{4,0},{8,4},{12,8},{16,12},{20,16},{24,20},{28,24},{1,29},{... | collective-permute-start | bytes 688136 | tf_op jit(solution)/shard_map/ppermute | solution.py:28
  13.4 29.0 %collective-permute-start = (f32[2,32,896]{2,1,0:T(8,128)S(1)}, f32[2,32,896]{2,1,0:T(8,128)S(1)}, u32[]{:S(2)}, u32[]{:S(2)}) collective-permute-start(f32[2,32,896]{2,1,0:T(8,128)S(1)} %get-tuple-element.37), channel_id=1, source_target_pairs={{0,24},{4,28},{8,0},{12,4},{16,8},{20,12},{24,16},{28,20},{1,25},{... | collective-permute-start | bytes 688136 | tf_op jit(solution)/shard_map/ppermute | solution.py:28
  13.7 2.4 %copy-start = (f32[1,2,32,3,6400]{4,2,3,1,0:T(8,128)S(1)}, f32[1,2,32,3,6400]{4,2,3,1,0:T(8,128)}, u32[]{:S(2)}) copy-start(f32[1,2,32,3,6400]{4,2,3,1,0:T(8,128)} %param.3) | copy-start | bytes 14745604
  17.4 0.7 copy-start.2
  18.1 0.7 copy-start.3
  18.8 0.7 copy-start.4
  19.5 0.7 copy-start.5
  20.2 34.4 %collective-permute-start.1 = (f32[2,32,896]{2,1,0:T(8,128)S(1)}, f32[2,32,896]{2,1,0:T(8,128)S(1)}, u32[]{:S(2)}, u32[]{:S(2)}) collective-permute-start(f32[2,32,896]{2,1,0:T(8,128)S(1)} %get-tuple-element.38), channel_id=1, source_target_pairs={{0,16},{4,20},{8,24},{12,28},{16,0},{20,4},{24,8},{28,12},{1,17},{... | collective-permute-start | bytes 688136 | tf_op jit(solution)/shard_map/ppermute | solution.py:28
  26.7 39.9 %collective-permute-start.7 = (f32[2,32,896]{2,1,0:T(8,128)}, f32[2,32,896]{2,1,0:T(8,128)S(1)}, u32[]{:S(2)}, u32[]{:S(2)}) collective-permute-start(f32[2,32,896]{2,1,0:T(8,128)} %get-tuple-element.48), channel_id=1, source_target_pairs={{0,12},{4,16},{8,20},{12,24},{16,28},{20,0},{24,4},{28,8},{1,13},{... | collective-permute-start | bytes 688136 | tf_op jit(solution)/shard_map/ppermute | solution.py:28
  33.1 33.5 %collective-permute-start.15 = (f32[2,32,896]{2,1,0:T(8,128)}, f32[2,32,896]{2,1,0:T(8,128)S(1)}, u32[]{:S(2)}, u32[]{:S(2)}) collective-permute-start(f32[2,32,896]{2,1,0:T(8,128)} %get-tuple-element.58), channel_id=1, source_target_pairs={{0,16},{4,20},{8,24},{12,28},{16,0},{20,4},{24,8},{28,12},{1,17},{... | collective-permute-start | bytes 688136 | tf_op jit(solution)/shard_map/ppermute | solution.py:28
  33.4 40.6 %collective-permute-start.16 = (f32[2,32,896]{2,1,0:T(8,128)}, f32[2,32,896]{2,1,0:T(8,128)S(1)}, u32[]{:S(2)}, u32[]{:S(2)}) collective-permute-start(f32[2,32,896]{2,1,0:T(8,128)} %copy-done.5), channel_id=1, source_target_pairs={{0,4},{4,8},{8,12},{12,16},{16,20},{20,24},{24,28},{28,0},{1,5},{5... | collective-permute-start | bytes 688136 | tf_op jit(solution)/shard_map/ppermute | solution.py:28
  42.5 41.5 %collective-permute-start.17 = (f32[2,32,896]{2,1,0:T(8,128)}, f32[2,32,896]{2,1,0:T(8,128)S(1)}, u32[]{:S(2)}, u32[]{:S(2)}) collective-permute-start(f32[2,32,896]{2,1,0:T(8,128)} %copy-done.4), channel_id=1, source_target_pairs={{0,20},{4,24},{8,28},{12,0},{16,4},{20,8},{24,12},{28,16},{1,21},{... | collective-permute-start | bytes 688136 | tf_op jit(solution)/shard_map/ppermute | solution.py:28
  54.6 29.4 %collective-permute-start.18 = (f32[2,32,896]{2,1,0:T(8,128)}, f32[2,32,896]{2,1,0:T(8,128)S(1)}, u32[]{:S(2)}, u32[]{:S(2)}) collective-permute-start(f32[2,32,896]{2,1,0:T(8,128)} %copy-done.3), channel_id=1, source_target_pairs={{0,28},{4,0},{8,4},{12,8},{16,12},{20,16},{24,20},{28,24},{1,29},{... | collective-permute-start | bytes 688136 | tf_op jit(solution)/shard_map/ppermute | solution.py:28
  66.6 17.7 %collective-permute-start.19 = (f32[2,32,896]{2,1,0:T(8,128)}, f32[2,32,896]{2,1,0:T(8,128)S(1)}, u32[]{:S(2)}, u32[]{:S(2)}) collective-permute-start(f32[2,32,896]{2,1,0:T(8,128)} %copy-done.2), channel_id=1, source_target_pairs={{0,24},{4,28},{8,0},{12,4},{16,8},{20,12},{24,16},{28,20},{1,25},{... | collective-permute-start | bytes 688136 | tf_op jit(solution)/shard_map/ppermute | solution.py:28
  66.6 20.7 %collective-permute-start.20 = (f32[2,32,896]{2,1,0:T(8,128)S(1)}, f32[2,32,896]{2,1,0:T(8,128)S(1)}, u32[]{:S(2)}, u32[]{:S(2)}) collective-permute-start(f32[2,32,896]{2,1,0:T(8,128)S(1)} %get-tuple-element.64), channel_id=1, source_target_pairs={{0,8},{4,12},{8,16},{12,20},{16,24},{20,28},{24,0},{28,4},{1,9},{5... | collective-permute-start | bytes 688136 | tf_op jit(solution)/shard_map/ppermute | solution.py:28
  70.1 2.4 %copy-start.1 = (f32[1,2,32,3,6400]{4,2,3,1,0:T(8,128)S(1)}, f32[1,2,32,3,6400]{4,2,3,1,0:T(8,128)}, u32[]{:S(2)}) copy-start(f32[1,2,32,3,6400]{4,2,3,1,0:T(8,128)} %param.3) | copy-start | bytes 14745604
  73.9 14.5 %collective-permute-start.10 = (f32[304,128]{1,0:T(8,128)S(1)}, f32[304,128]{1,0:T(8,128)S(1)}, u32[]{:S(2)}, u32[]{:S(2)}) collective-permute-start(f32[304,128]{1,0:T(8,128)S(1)} %get-tuple-element.52), channel_id=1, source_target_pairs={{0,20},{4,24},{8,28},{12,0},{16,4},{20,8},{24,12},{28,16},{1,21},{... | collective-permute-start | bytes 466952 | tf_op jit(solution)/shard_map/ppermute | solution.py:28
  83.9 14.0 %collective-permute-start.11 = (f32[304,128]{1,0:T(8,128)S(1)}, f32[304,128]{1,0:T(8,128)S(1)}, u32[]{:S(2)}, u32[]{:S(2)}) collective-permute-start(f32[304,128]{1,0:T(8,128)S(1)} %get-tuple-element.53), channel_id=1, source_target_pairs={{0,8},{4,12},{8,16},{12,20},{16,24},{20,28},{24,0},{28,4},{1,9},{5... | collective-permute-start | bytes 466952 | tf_op jit(solution)/shard_map/ppermute | solution.py:28
  83.9 17.3 %collective-permute-start.12 = (f32[304,128]{1,0:T(8,128)S(1)}, f32[304,128]{1,0:T(8,128)S(1)}, u32[]{:S(2)}, u32[]{:S(2)}) collective-permute-start(f32[304,128]{1,0:T(8,128)S(1)} %get-tuple-element.54), channel_id=1, source_target_pairs={{0,12},{4,16},{8,20},{12,24},{16,28},{20,0},{24,4},{28,8},{1,13},{... | collective-permute-start | bytes 466952 | tf_op jit(solution)/shard_map/ppermute | solution.py:28
  84.3 17.7 %collective-permute-start.13 = (f32[304,128]{1,0:T(8,128)S(1)}, f32[304,128]{1,0:T(8,128)S(1)}, u32[]{:S(2)}, u32[]{:S(2)}) collective-permute-start(f32[304,128]{1,0:T(8,128)S(1)} %get-tuple-element.55), channel_id=1, source_target_pairs={{0,24},{4,28},{8,0},{12,4},{16,8},{20,12},{24,16},{28,20},{1,25},{... | collective-permute-start | bytes 466952 | tf_op jit(solution)/shard_map/ppermute | solution.py:28
  87.3 14.7 %collective-permute-start.14 = (f32[304,128]{1,0:T(8,128)S(1)}, f32[304,128]{1,0:T(8,128)S(1)}, u32[]{:S(2)}, u32[]{:S(2)}) collective-permute-start(f32[304,128]{1,0:T(8,128)S(1)} %get-tuple-element.56), channel_id=1, source_target_pairs={{0,28},{4,0},{8,4},{12,8},{16,12},{20,16},{24,20},{28,24},{1,29},{... | collective-permute-start | bytes 466952 | tf_op jit(solution)/shard_map/ppermute | solution.py:28
  88.5 23.6 %collective-permute-start.8 = (f32[304,128]{1,0:T(8,128)S(1)}, f32[304,128]{1,0:T(8,128)S(1)}, u32[]{:S(2)}, u32[]{:S(2)}) collective-permute-start(f32[304,128]{1,0:T(8,128)S(1)} %get-tuple-element.50), channel_id=1, source_target_pairs={{0,16},{4,20},{8,24},{12,28},{16,0},{20,4},{24,8},{28,12},{1,17},{... | collective-permute-start | bytes 466952 | tf_op jit(solution)/shard_map/ppermute | solution.py:28
  97.9 14.1 %collective-permute-start.9 = (f32[304,128]{1,0:T(8,128)S(1)}, f32[304,128]{1,0:T(8,128)S(1)}, u32[]{:S(2)}, u32[]{:S(2)}) collective-permute-start(f32[304,128]{1,0:T(8,128)S(1)} %get-tuple-element.51), channel_id=1, source_target_pairs={{0,4},{4,8},{8,12},{12,16},{16,20},{20,24},{24,28},{28,0},{1,5},{5... | collective-permute-start | bytes 466952 | tf_op jit(solution)/shard_map/ppermute | solution.py:28
  113.3 4.6 %collective-permute-start.21 = (f32[4,2,32,128]{3,2,1,0:T(8,128)S(1)}, f32[4,2,32,128]{3,2,1,0:T(8,128)S(1)}, u32[]{:S(2)}, u32[]{:S(2)}) collective-permute-start(f32[4,2,32,128]{3,2,1,0:T(8,128)S(1)} %get-tuple-element.68), channel_id=1, source_target_pairs={{0,4},{4,0},{8,12},{12,8},{16,20},{20,16},{24,28},{28,24},{1,5},{5... | collective-permute-start | bytes 393224 | tf_op jit(solution)/shard_map/ppermute | solution.py:429
  118.0 4.6 %collective-permute-start.22 = (f32[2,32,128]{2,1,0:T(8,128)S(1)}, f32[2,32,128]{2,1,0:T(8,128)S(1)}, u32[]{:S(2)}, u32[]{:S(2)}) collective-permute-start(f32[2,32,128]{2,1,0:T(8,128)S(1)} %get-tuple-element.71), channel_id=1, source_target_pairs={{0,8},{4,12},{8,16},{12,20},{16,24},{20,28},{24,0},{28,4},{1,9},{5... | collective-permute-start | bytes 98312 | tf_op jit(solution)/shard_map/ppermute | solution.py:28
  118.0 4.6 %collective-permute-start.23 = (f32[2,32,128]{2,1,0:T(8,128)S(1)}, f32[2,32,128]{2,1,0:T(8,128)S(1)}, u32[]{:S(2)}, u32[]{:S(2)}) collective-permute-start(f32[2,32,128]{2,1,0:T(8,128)S(1)} %get-tuple-element.69), channel_id=1, source_target_pairs={{0,16},{4,20},{8,24},{12,28},{16,0},{20,4},{24,8},{28,12},{1,17},{... | collective-permute-start | bytes 98312 | tf_op jit(solution)/shard_map/ppermute | solution.py:28
  118.3 4.7 %collective-permute-start.24 = (f32[2,32,128]{2,1,0:T(8,128)S(1)}, f32[2,32,128]{2,1,0:T(8,128)S(1)}, u32[]{:S(2)}, u32[]{:S(2)}) collective-permute-start(f32[2,32,128]{2,1,0:T(8,128)S(1)} %get-tuple-element.70), channel_id=1, source_target_pairs={{0,24},{4,28},{8,0},{12,4},{16,8},{20,12},{24,16},{28,20},{1,25},{... | collective-permute-start | bytes 98312 | tf_op jit(solution)/shard_map/ppermute | solution.py:28
  123.0 4.9 %collective-permute-start.25 = (f32[2,32,128]{2,1,0:T(8,128)S(1)}, f32[2,32,128]{2,1,0:T(8,128)S(1)}, u32[]{:S(2)}, u32[]{:S(2)}) collective-permute-start(f32[2,32,128]{2,1,0:T(8,128)S(1)} %bitcast_add_fusion.refs_0_), channel_id=1, source_target_pairs={{0,1},{1,2},{2,3},{3,0},{4,5},{5,6},{6,7},{7,4},{8,9},{9,10},{10,1... | collective-permute-start | bytes 98312 | tf_op jit(solution)/shard_map/ppermute | solution.py:28
  126.8 2.8 %collective-permute-start.26 = (f32[2,32,128]{2,1,0:T(8,128)S(1)}, f32[2,32,128]{2,1,0:T(8,128)S(1)}, u32[]{:S(2)}, u32[]{:S(2)}) collective-permute-start(f32[2,32,128]{2,1,0:T(8,128)S(1)} %bitcast_add_fusion.refs_0_), channel_id=1, source_target_pairs={{0,2},{1,3},{2,0},{3,1},{4,6},{5,7},{6,4},{7,5},{8,10},{9,11},{10,... | collective-permute-start | bytes 98312 | tf_op jit(solution)/shard_map/ppermute | solution.py:28
  127.1 3.3 %collective-permute-start.27 = (f32[2,32,128]{2,1,0:T(8,128)S(1)}, f32[2,32,128]{2,1,0:T(8,128)S(1)}, u32[]{:S(2)}, u32[]{:S(2)}) collective-permute-start(f32[2,32,128]{2,1,0:T(8,128)S(1)} %bitcast_add_fusion.refs_0_), channel_id=1, source_target_pairs={{0,3},{1,0},{2,1},{3,2},{4,7},{5,4},{6,5},{7,6},{8,11},{9,8},{10,9... | collective-permute-start | bytes 98312 | tf_op jit(solution)/shard_map/ppermute | solution.py:28

commit v5 on v4

--- a/solution.py
+++ b/solution.py
@@ -261,7 +261,7 @@
             pltpu.VMEM((parts.count, folded, LANES), jnp.float32),
             pltpu.SemaphoreType.DMA((copies,)),
         ],
-        compiler_params=pltpu.CompilerParams(vmem_limit_bytes=5 * 1024 * 1024),
+        compiler_params=pltpu.CompilerParams(vmem_limit_bytes=50 * 1024 * 1024),
         cost_estimate=pl.CostEstimate(flops=0, bytes_accessed=2 * size, transcendentals=0),
     )(field)
 
@@ -486,7 +486,7 @@
         else:
             first = [turns[at] for at in FIRST] if start == 0 else []
             others = [turn for turn in turns + [0] if turn not in first]
-            room = 4 if start else ROOM
+            room = ROOM
             found = dict(zip(first, pack(parts, source, first, start, stop, room))) if first else {}
             found.update(zip(others, pack(parts, source, others, start, stop, room)))
             sent = [found[turn] for turn in turns + [0]]

time: 131 us -> 131 us (level)
  local copies, waits for them, and re-layouts: 7.83 us -> 3.09 us
  starting transfers between devices: 75.8 us -> 79.8 us
  Pallas kernels: 10.9 us -> 12.6 us
    unnamed x17 -> x13, local copies, waits for them, and re-layouts: 7.62 us -> 2.88 us
    ppermute x27, starting transfers between devices: 74.9 us -> 78.4 us  [shifted(): return lax.ppermute(value, axis, pairs)]
  transfers between devices with their start and end apart: 28 -> 28, of which waited for: 11 -> 11; matrix products, arithmetic and copies ran while one was open for 1% -> 1% of each run, Pallas kernels for 6% -> 7%
where the time goes in v5:
time: 131 us
  starting transfers between devices  79.8 us (61%)
  waiting for transfers between devices  34.3 us (26%)
  Pallas kernels  12.6 us (10%)
  local copies, waits for them, and re-layouts  3.09 us (2%)
    ppermute x27, starting transfers between devices, shifted(): return lax.ppermute(value, axis, pairs)  78.4 us
    ppermute x27, waiting for transfers between devices, shifted(): return lax.ppermute(value, axis, pairs)  31.4 us
    pallas_call x3, Pallas kernels, pack(): pl.pallas_call(functools.partial(pack_kernel, parts, turns, start, stop),...  5.91 us
    pallas_call x3, Pallas kernels, chunk_products(): pl.pallas_call(functools.partial(chunk_kernel, offsets, before is None, f...  3.99 us
    ppermute x1, waiting for transfers between devices, reduced_over_points(): total = total + lax.ppermute(blocks[turn], 'ka', pairs)  2.9 us
    unnamed x13, local copies, waits for them, and re-layouts  2.88 us
  transfers between devices with their start and end apart: 28, of which 11 were waited for; matrix products, arithmetic and copies ran while one was open for 1% of the time, Pallas kernels for 7%

profile of v5, /device:TPU:1, one launch (start us, length us, event | category | flops | bytes accessed | tf_op | source)
XLA Modules:
  0.0 131.0 jit_solution(14396959923028831501)
XLA Ops:
  0.0 1.2 shard_map.37
  1.2 2.2 %collective-permute-start.3 = (f32[2,32,896]{2,1,0:T(8,128)S(1)}, f32[2,32,896]{2,1,0:T(8,128)S(1)}, u32[]{:S(2)}, u32[]{:S(2)}) collective-permute-start(f32[2,32,896]{2,1,0:T(8,128)S(1)} %get-tuple-element.40), channel_id=1, source_target_pairs={{0,8},{4,12},{8,16},{12,20},{16,24},{20,28},{24,0},{28,4},{1,9},{5... | collective-permute-start | bytes 688136 | tf_op jit(solution)/shard_map/ppermute | solution.py:28
  3.4 2.2 %shard_map.38 = (f32[2,32,896]{2,1,0:T(8,128)S(1)}, f32[2,32,896]{2,1,0:T(8,128)}, f32[2,32,896]{2,1,0:T(8,128)}, f32[2,32,896]{2,1,0:T(8,128)S(1)}, f32[2,32,896]{2,1,0:T(8,128)S(1)}) custom-call(f32[2,3,32,6400]{3,2,1,0:T(8,128)} %bitcast.22), custom_call_target="tpu_custom_call" | custom-call | bytes 2293760 | tf_op jit(solution)/shard_map/pallas_call | solution.py:168
  5.7 3.3 %collective-permute-start.2 = (f32[2,32,896]{2,1,0:T(8,128)S(1)}, f32[2,32,896]{2,1,0:T(8,128)S(1)}, u32[]{:S(2)}, u32[]{:S(2)}) collective-permute-start(f32[2,32,896]{2,1,0:T(8,128)S(1)} %get-tuple-element.39), channel_id=1, source_target_pairs={{0,20},{4,24},{8,28},{12,0},{16,4},{20,8},{24,12},{28,16},{1,21},{... | collective-permute-start | bytes 688136 | tf_op jit(solution)/shard_map/ppermute | solution.py:28
  9.0 0.0 collective-permute-start.4
  9.0 1.2 collective-permute-start.5
  10.2 2.9 %collective-permute-start.6 = (f32[2,32,896]{2,1,0:T(8,128)S(1)}, f32[2,32,896]{2,1,0:T(8,128)S(1)}, u32[]{:S(2)}, u32[]{:S(2)}) collective-permute-start(f32[2,32,896]{2,1,0:T(8,128)S(1)} %get-tuple-element.44), channel_id=1, source_target_pairs={{0,28},{4,0},{8,4},{12,8},{16,12},{20,16},{24,20},{28,24},{1,29},{... | collective-permute-start | bytes 688136 | tf_op jit(solution)/shard_map/ppermute | solution.py:28
  13.3 0.1 copy.6
  13.4 0.1 convert_add_fusion
  13.5 0.3 collective-permute-start
  13.8 2.4 %shard_map.40 = (f32[2,32,896]{2,1,0:T(8,128)}, f32[2,32,896]{2,1,0:T(8,128)S(1)}, f32[2,32,896]{2,1,0:T(8,128)S(1)}, f32[2,32,896]{2,1,0:T(8,128)}, f32[2,32,89...) custom-call(f32[2,3,32,6400]{3,2,1,0:T(8,128)} %bitcast.23), custom_call_target="tpu_custom_call" | custom-call | bytes 3670016 | tf_op jit(solution)/shard_map/pallas_call | solution.py:168
  16.2 0.7 copy-done
  16.9 0.7 copy-done.1
  17.6 0.7 copy-done.2
  18.3 0.7 copy-done.3
  19.0 6.6 %collective-permute-start.1 = (f32[2,32,896]{2,1,0:T(8,128)S(1)}, f32[2,32,896]{2,1,0:T(8,128)S(1)}, u32[]{:S(2)}, u32[]{:S(2)}) collective-permute-start(f32[2,32,896]{2,1,0:T(8,128)S(1)} %get-tuple-element.38), channel_id=1, source_target_pairs={{0,16},{4,20},{8,24},{12,28},{16,0},{20,4},{24,8},{28,12},{1,17},{... | collective-permute-start | bytes 688136 | tf_op jit(solution)/shard_map/ppermute | solution.py:28
  25.6 1.2 collective-permute-done.4.refs_4_
  26.8 6.3 %collective-permute-done.5.refs_5_ = f32[2,32,896]{2,1,0:T(8,128)S(1)} collective-permute-done((f32[2,32,896]{2,1,0:T(8,128)}, f32[2,32,896]{2,1,0:T(8,128)S(1)}, u32[]{:S(2)}, u32[]{:S(2)}) %collective-permute-start.5) | collective-permute-done | bytes 229408 | tf_op jit(solution)/shard_map/ppermute | solution.py:28
  33.1 0.1 dynamic-slice_maximum_fusion
  33.2 0.1 copy.7
  33.3 0.1 reshape.160
  33.3 0.0 collective-permute-done.6.refs_6_
  33.4 9.1 %collective-permute-start.16 = (f32[2,32,896]{2,1,0:T(8,128)}, f32[2,32,896]{2,1,0:T(8,128)S(1)}, u32[]{:S(2)}, u32[]{:S(2)}) collective-permute-start(f32[2,32,896]{2,1,0:T(8,128)} %copy-done.3), channel_id=1, source_target_pairs={{0,4},{4,8},{8,12},{12,16},{16,20},{20,24},{24,28},{28,0},{1,5},{5... | collective-permute-start | bytes 688136 | tf_op jit(solution)/shard_map/ppermute | solution.py:28
  42.4 0.0 collective-permute-done.refs_0_
  42.4 12.2 %collective-permute-start.17 = (f32[2,32,896]{2,1,0:T(8,128)}, f32[2,32,896]{2,1,0:T(8,128)S(1)}, u32[]{:S(2)}, u32[]{:S(2)}) collective-permute-start(f32[2,32,896]{2,1,0:T(8,128)} %copy-done.2), channel_id=1, source_target_pairs={{0,20},{4,24},{8,28},{12,0},{16,4},{20,8},{24,12},{28,16},{1,21},{... | collective-permute-start | bytes 688136 | tf_op jit(solution)/shard_map/ppermute | solution.py:28
  54.6 0.0 collective-permute-done.1.refs_1_
  54.6 3.4 %collective-permute-start.18 = (f32[2,32,896]{2,1,0:T(8,128)}, f32[2,32,896]{2,1,0:T(8,128)S(1)}, u32[]{:S(2)}, u32[]{:S(2)}) collective-permute-start(f32[2,32,896]{2,1,0:T(8,128)} %copy-done.1), channel_id=1, source_target_pairs={{0,28},{4,0},{8,4},{12,8},{16,12},{20,16},{24,20},{28,24},{1,29},{... | collective-permute-start | bytes 688136 | tf_op jit(solution)/shard_map/ppermute | solution.py:28
  58.0 8.6 %collective-permute-done.7.refs_3_ = f32[2,32,896]{2,1,0:T(8,128)S(1)} collective-permute-done((f32[2,32,896]{2,1,0:T(8,128)}, f32[2,32,896]{2,1,0:T(8,128)S(1)}, u32[]{:S(2)}, u32[]{:S(2)}) %collective-permute-start.7) | collective-permute-done | bytes 229408 | tf_op jit(solution)/shard_map/ppermute | solution.py:28
  66.6 0.0 collective-permute-start.19
  66.6 0.0 collective-permute-done.15.refs_0_
  66.6 1.5 %collective-permute-start.20 = (f32[2,32,896]{2,1,0:T(8,128)S(1)}, f32[2,32,896]{2,1,0:T(8,128)S(1)}, u32[]{:S(2)}, u32[]{:S(2)}) collective-permute-start(f32[2,32,896]{2,1,0:T(8,128)S(1)} %get-tuple-element.64), channel_id=1, source_target_pairs={{0,8},{4,12},{8,16},{12,20},{16,24},{20,28},{24,0},{28,4},{1,9},{5... | collective-permute-start | bytes 688136 | tf_op jit(solution)/shard_map/ppermute | solution.py:28
  68.0 0.7 sine_multiply_fusion
  68.7 1.4 %shard_map.39.refs_10_ = f32[8,64,128]{2,1,0:T(8,128)S(1)} custom-call(f32[2,32,896]{2,1,0:T(8,128)S(1)} %collective-permute-done.refs_0_, f32[2,32,896]{2,1,0:T(8,128)S(1)} %collective-permute-done.1.refs_1_, f32[2,32,896]{2,1,0:T(8,128)S(1)} %collective-permute-done.2.refs_2_, f32[2,32,896]{2,1,0:T(8,128)S(1)} %collective-permute-done.3.refs_3_, ...), custom_call_target="tpu_custom_call" | custom-call | flops 469762048 | bytes 1835008 | tf_op jit(solution)/shard_map/pallas_call | solution.py:372
  70.1 1.9 %shard_map.41 = (f32[304,128]{1,0:T(8,128)S(1)}, f32[304,128]{1,0:T(8,128)S(1)}, f32[304,128]{1,0:T(8,128)S(1)}, f32[304,128]{1,0:T(8,128)S(1)}, f32[304,128]{1,...) custom-call(f32[2,3,32,6400]{3,2,1,0:T(8,128)} %bitcast.24), custom_call_target="tpu_custom_call" | custom-call | bytes 2490368 | tf_op jit(solution)/shard_map/pallas_call | solution.py:254
  72.0 10.0 %collective-permute-start.10 = (f32[304,128]{1,0:T(8,128)S(1)}, f32[304,128]{1,0:T(8,128)S(1)}, u32[]{:S(2)}, u32[]{:S(2)}) collective-permute-start(f32[304,128]{1,0:T(8,128)S(1)} %get-tuple-element.52), channel_id=1, source_target_pairs={{0,20},{4,24},{8,28},{12,0},{16,4},{20,8},{24,12},{28,16},{1,21},{... | collective-permute-start | bytes 466952 | tf_op jit(solution)/shard_map/ppermute | solution.py:28
  82.0 0.0 collective-permute-start.11
  82.1 0.0 collective-permute-done.18.refs_4_
  82.1 0.3 collective-permute-start.12
  82.4 0.0 collective-permute-done.19.refs_5_
  82.4 4.7 %collective-permute-start.13 = (f32[304,128]{1,0:T(8,128)S(1)}, f32[304,128]{1,0:T(8,128)S(1)}, u32[]{:S(2)}, u32[]{:S(2)}) collective-permute-start(f32[304,128]{1,0:T(8,128)S(1)} %get-tuple-element.55), channel_id=1, source_target_pairs={{0,24},{4,28},{8,0},{12,4},{16,8},{20,12},{24,16},{28,20},{1,25},{... | collective-permute-start | bytes 466952 | tf_op jit(solution)/shard_map/ppermute | solution.py:28
  87.1 0.7 collective-permute-start.14
  87.8 10.2 %collective-permute-start.8 = (f32[304,128]{1,0:T(8,128)S(1)}, f32[304,128]{1,0:T(8,128)S(1)}, u32[]{:S(2)}, u32[]{:S(2)}) collective-permute-start(f32[304,128]{1,0:T(8,128)S(1)} %get-tuple-element.50), channel_id=1, source_target_pairs={{0,16},{4,20},{8,24},{12,28},{16,0},{20,4},{24,8},{28,12},{1,17},{... | collective-permute-start | bytes 466952 | tf_op jit(solution)/shard_map/ppermute | solution.py:28
  97.9 1.9 %collective-permute-start.9 = (f32[304,128]{1,0:T(8,128)S(1)}, f32[304,128]{1,0:T(8,128)S(1)}, u32[]{:S(2)}, u32[]{:S(2)}) collective-permute-start(f32[304,128]{1,0:T(8,128)S(1)} %get-tuple-element.51), channel_id=1, source_target_pairs={{0,4},{4,8},{8,12},{12,16},{16,20},{20,24},{24,28},{28,0},{1,5},{5... | collective-permute-start | bytes 466952 | tf_op jit(solution)/shard_map/ppermute | solution.py:28
  99.9 1.4 %shard_map.42.refs_10_ = f32[8,64,128]{2,1,0:T(8,128)S(1)} custom-call(f32[2,32,896]{2,1,0:T(8,128)S(1)} %collective-permute-done.15.refs_0_, f32[2,32,896]{2,1,0:T(8,128)S(1)} %collective-permute-done.16.refs_1_, f32[2,32,896]{2,1,0:T(8,128)S(1)} %collective-permute-done.17.refs_2_, f32[2,32,896]{2,1,0:T(8,128)S(1)} %collective-permute-done.7.refs_3_, ...), custom_call_target="tpu_custom_call" | custom-call | flops 469762048 | bytes 1835008 | tf_op jit(solution)/shard_map/pallas_call | solution.py:372
  101.2 0.0 collective-permute-done.12.refs_4_
  101.2 0.8 collective-permute-done.13.refs_5_
  102.0 0.0 collective-permute-done.14.refs_6_
  102.0 9.8 %collective-permute-done.8.refs_0_ = f32[304,128]{1,0:T(8,128)S(1)} collective-permute-done((f32[304,128]{1,0:T(8,128)S(1)}, f32[304,128]{1,0:T(8,128)S(1)}, u32[]{:S(2)}, u32[]{:S(2)}) %collective-permute-start.8) | collective-permute-done | bytes 155680 | tf_op jit(solution)/shard_map/ppermute | solution.py:28
  111.8 1.3 shard_map.43
  113.1 1.4 %collective-permute-start.21 = (f32[4,2,32,128]{3,2,1,0:T(8,128)S(1)}, f32[4,2,32,128]{3,2,1,0:T(8,128)S(1)}, u32[]{:S(2)}, u32[]{:S(2)}) collective-permute-start(f32[4,2,32,128]{3,2,1,0:T(8,128)S(1)} %get-tuple-element.68), channel_id=1, source_target_pairs={{0,4},{4,0},{8,12},{12,8},{16,20},{20,16},{24,28},{28,24},{1,5},{5... | collective-permute-start | bytes 393224 | tf_op jit(solution)/shard_map/ppermute | solution.py:429
  114.5 2.9 %collective-permute-done.21 = f32[4,2,32,128]{3,2,1,0:T(8,128)S(1)} collective-permute-done((f32[4,2,32,128]{3,2,1,0:T(8,128)S(1)}, f32[4,2,32,128]{3,2,1,0:T(8,128)S(1)}, u32[]{:S(2)}, u32[]{:S(2)}) %collective-permute-start.21) | collective-permute-done | bytes 131104 | tf_op jit(solution)/shard_map/ppermute | solution.py:429
  117.5 0.1 collective-permute-start.22
  117.6 0.3 collective-permute-start.23
  117.8 3.0 %collective-permute-start.24 = (f32[2,32,128]{2,1,0:T(8,128)S(1)}, f32[2,32,128]{2,1,0:T(8,128)S(1)}, u32[]{:S(2)}, u32[]{:S(2)}) collective-permute-start(f32[2,32,128]{2,1,0:T(8,128)S(1)} %get-tuple-element.70), channel_id=1, source_target_pairs={{0,24},{4,28},{8,0},{12,4},{16,8},{20,12},{24,16},{28,20},{1,25},{... | collective-permute-start | bytes 98312 | tf_op jit(solution)/shard_map/ppermute | solution.py:28
  120.8 1.3 collective-permute-done.22
  122.1 0.0 collective-permute-done.23
  122.1 0.3 collective-permute-done.24
  122.5 4.1 %collective-permute-start.25 = (f32[2,32,128]{2,1,0:T(8,128)S(1)}, f32[2,32,128]{2,1,0:T(8,128)S(1)}, u32[]{:S(2)}, u32[]{:S(2)}) collective-permute-start(f32[2,32,128]{2,1,0:T(8,128)S(1)} %bitcast_add_fusion.refs_0_), channel_id=1, source_target_pairs={{0,1},{1,2},{2,3},{3,0},{4,5},{5,6},{6,7},{7,4},{8,9},{9,10},{10,1... | collective-permute-start | bytes 98312 | tf_op jit(solution)/shard_map/ppermute | solution.py:28
  126.6 0.3 collective-permute-start.26
  126.9 0.2 collective-permute-start.27
  127.1 0.6 collective-permute-done.25.refs_1_
  127.6 1.7 %collective-permute-done.26.refs_2_ = f32[2,32,128]{2,1,0:T(8,128)S(1)} collective-permute-done((f32[2,32,128]{2,1,0:T(8,128)S(1)}, f32[2,32,128]{2,1,0:T(8,128)S(1)}, u32[]{:S(2)}, u32[]{:S(2)}) %collective-permute-start.26) | collective-permute-done | bytes 32800 | tf_op jit(solution)/shard_map/ppermute | solution.py:28
  129.4 0.8 collective-permute-done.27.refs_3_
  130.2 0.8 shard_map.44
  (29 shorter events, 0.2 us)
Async XLA Ops:
  0.0 13.3 %copy-start.5 = (f32[2,3]{1,0:T(2,128)S(1)}, f32[2,3]{1,0:T(2,128)}, u32[]{:S(2)}) copy-start(f32[2,3]{1,0:T(2,128)} %param.4) | copy-start | bytes 76
  0.0 13.4 %copy-start.4 = (s32[8,2,3]{0,1,2:T(2,128)S(1)}, s32[8,2,3]{0,1,2:T(2,128)}, u32[]{:S(2)}) copy-start(s32[8,2,3]{0,1,2:T(2,128)} %param.5) | copy-start | bytes 580
  1.2 12.2 %collective-permute-start.3 = (f32[2,32,896]{2,1,0:T(8,128)S(1)}, f32[2,32,896]{2,1,0:T(8,128)S(1)}, u32[]{:S(2)}, u32[]{:S(2)}) collective-permute-start(f32[2,32,896]{2,1,0:T(8,128)S(1)} %get-tuple-element.40), channel_id=1, source_target_pairs={{0,8},{4,12},{8,16},{12,20},{16,24},{20,28},{24,0},{28,4},{1,9},{5... | collective-permute-start | bytes 688136 | tf_op jit(solution)/shard_map/ppermute | solution.py:28
  5.7 13.3 %collective-permute-start.2 = (f32[2,32,896]{2,1,0:T(8,128)S(1)}, f32[2,32,896]{2,1,0:T(8,128)S(1)}, u32[]{:S(2)}, u32[]{:S(2)}) collective-permute-start(f32[2,32,896]{2,1,0:T(8,128)S(1)} %get-tuple-element.39), channel_id=1, source_target_pairs={{0,20},{4,24},{8,28},{12,0},{16,4},{20,8},{24,12},{28,16},{1,21},{... | collective-permute-start | bytes 688136 | tf_op jit(solution)/shard_map/ppermute | solution.py:28
  9.0 17.8 %collective-permute-start.4 = (f32[2,32,896]{2,1,0:T(8,128)}, f32[2,32,896]{2,1,0:T(8,128)S(1)}, u32[]{:S(2)}, u32[]{:S(2)}) collective-permute-start(f32[2,32,896]{2,1,0:T(8,128)} %get-tuple-element.42), channel_id=1, source_target_pairs={{0,4},{4,8},{8,12},{12,16},{16,20},{20,24},{24,28},{28,0},{1,5},{5... | collective-permute-start | bytes 688136 | tf_op jit(solution)/shard_map/ppermute | solution.py:28
  9.0 24.1 %collective-permute-start.5 = (f32[2,32,896]{2,1,0:T(8,128)}, f32[2,32,896]{2,1,0:T(8,128)S(1)}, u32[]{:S(2)}, u32[]{:S(2)}) collective-permute-start(f32[2,32,896]{2,1,0:T(8,128)} %get-tuple-element.43), channel_id=1, source_target_pairs={{0,12},{4,16},{8,20},{12,24},{16,28},{20,0},{24,4},{28,8},{1,13},{... | collective-permute-start | bytes 688136 | tf_op jit(solution)/shard_map/ppermute | solution.py:28
  10.2 23.1 %collective-permute-start.6 = (f32[2,32,896]{2,1,0:T(8,128)S(1)}, f32[2,32,896]{2,1,0:T(8,128)S(1)}, u32[]{:S(2)}, u32[]{:S(2)}) collective-permute-start(f32[2,32,896]{2,1,0:T(8,128)S(1)} %get-tuple-element.44), channel_id=1, source_target_pairs={{0,28},{4,0},{8,4},{12,8},{16,12},{20,16},{24,20},{28,24},{1,29},{... | collective-permute-start | bytes 688136 | tf_op jit(solution)/shard_map/ppermute | solution.py:28
  13.5 29.0 %collective-permute-start = (f32[2,32,896]{2,1,0:T(8,128)S(1)}, f32[2,32,896]{2,1,0:T(8,128)S(1)}, u32[]{:S(2)}, u32[]{:S(2)}) collective-permute-start(f32[2,32,896]{2,1,0:T(8,128)S(1)} %get-tuple-element.37), channel_id=1, source_target_pairs={{0,24},{4,28},{8,0},{12,4},{16,8},{20,12},{24,16},{28,20},{1,25},{... | collective-permute-start | bytes 688136 | tf_op jit(solution)/shard_map/ppermute | solution.py:28
  16.2 0.7 copy-start
  16.9 0.7 copy-start.1
  17.6 0.7 copy-start.2
  18.3 0.7 copy-start.3
  19.0 35.6 %collective-permute-start.1 = (f32[2,32,896]{2,1,0:T(8,128)S(1)}, f32[2,32,896]{2,1,0:T(8,128)S(1)}, u32[]{:S(2)}, u32[]{:S(2)}) collective-permute-start(f32[2,32,896]{2,1,0:T(8,128)S(1)} %get-tuple-element.38), channel_id=1, source_target_pairs={{0,16},{4,20},{8,24},{12,28},{16,0},{20,4},{24,8},{28,12},{1,17},{... | collective-permute-start | bytes 688136 | tf_op jit(solution)/shard_map/ppermute | solution.py:28
  26.8 39.8 %collective-permute-start.7 = (f32[2,32,896]{2,1,0:T(8,128)}, f32[2,32,896]{2,1,0:T(8,128)S(1)}, u32[]{:S(2)}, u32[]{:S(2)}) collective-permute-start(f32[2,32,896]{2,1,0:T(8,128)} %get-tuple-element.48), channel_id=1, source_target_pairs={{0,12},{4,16},{8,20},{12,24},{16,28},{20,0},{24,4},{28,8},{1,13},{... | collective-permute-start | bytes 688136 | tf_op jit(solution)/shard_map/ppermute | solution.py:28
  33.1 33.5 %collective-permute-start.15 = (f32[2,32,896]{2,1,0:T(8,128)}, f32[2,32,896]{2,1,0:T(8,128)S(1)}, u32[]{:S(2)}, u32[]{:S(2)}) collective-permute-start(f32[2,32,896]{2,1,0:T(8,128)} %get-tuple-element.58), channel_id=1, source_target_pairs={{0,16},{4,20},{8,24},{12,28},{16,0},{20,4},{24,8},{28,12},{1,17},{... | collective-permute-start | bytes 688136 | tf_op jit(solution)/shard_map/ppermute | solution.py:28
  33.4 38.6 %collective-permute-start.16 = (f32[2,32,896]{2,1,0:T(8,128)}, f32[2,32,896]{2,1,0:T(8,128)S(1)}, u32[]{:S(2)}, u32[]{:S(2)}) collective-permute-start(f32[2,32,896]{2,1,0:T(8,128)} %copy-done.3), channel_id=1, source_target_pairs={{0,4},{4,8},{8,12},{12,16},{16,20},{20,24},{24,28},{28,0},{1,5},{5... | collective-permute-start | bytes 688136 | tf_op jit(solution)/shard_map/ppermute | solution.py:28
  42.4 39.6 %collective-permute-start.17 = (f32[2,32,896]{2,1,0:T(8,128)}, f32[2,32,896]{2,1,0:T(8,128)S(1)}, u32[]{:S(2)}, u32[]{:S(2)}) collective-permute-start(f32[2,32,896]{2,1,0:T(8,128)} %copy-done.2), channel_id=1, source_target_pairs={{0,20},{4,24},{8,28},{12,0},{16,4},{20,8},{24,12},{28,16},{1,21},{... | collective-permute-start | bytes 688136 | tf_op jit(solution)/shard_map/ppermute | solution.py:28
  54.6 27.4 %collective-permute-start.18 = (f32[2,32,896]{2,1,0:T(8,128)}, f32[2,32,896]{2,1,0:T(8,128)S(1)}, u32[]{:S(2)}, u32[]{:S(2)}) collective-permute-start(f32[2,32,896]{2,1,0:T(8,128)} %copy-done.1), channel_id=1, source_target_pairs={{0,28},{4,0},{8,4},{12,8},{16,12},{20,16},{24,20},{28,24},{1,29},{... | collective-permute-start | bytes 688136 | tf_op jit(solution)/shard_map/ppermute | solution.py:28
  66.6 15.8 %collective-permute-start.19 = (f32[2,32,896]{2,1,0:T(8,128)}, f32[2,32,896]{2,1,0:T(8,128)S(1)}, u32[]{:S(2)}, u32[]{:S(2)}) collective-permute-start(f32[2,32,896]{2,1,0:T(8,128)} %copy-done), channel_id=1, source_target_pairs={{0,24},{4,28},{8,0},{12,4},{16,8},{20,12},{24,16},{28,20},{1,25},{... | collective-permute-start | bytes 688136 | tf_op jit(solution)/shard_map/ppermute | solution.py:28
  66.6 20.5 %collective-permute-start.20 = (f32[2,32,896]{2,1,0:T(8,128)S(1)}, f32[2,32,896]{2,1,0:T(8,128)S(1)}, u32[]{:S(2)}, u32[]{:S(2)}) collective-permute-start(f32[2,32,896]{2,1,0:T(8,128)S(1)} %get-tuple-element.64), channel_id=1, source_target_pairs={{0,8},{4,12},{8,16},{12,20},{16,24},{20,28},{24,0},{28,4},{1,9},{5... | collective-permute-start | bytes 688136 | tf_op jit(solution)/shard_map/ppermute | solution.py:28
  72.0 15.8 %collective-permute-start.10 = (f32[304,128]{1,0:T(8,128)S(1)}, f32[304,128]{1,0:T(8,128)S(1)}, u32[]{:S(2)}, u32[]{:S(2)}) collective-permute-start(f32[304,128]{1,0:T(8,128)S(1)} %get-tuple-element.52), channel_id=1, source_target_pairs={{0,20},{4,24},{8,28},{12,0},{16,4},{20,8},{24,12},{28,16},{1,21},{... | collective-permute-start | bytes 466952 | tf_op jit(solution)/shard_map/ppermute | solution.py:28
  82.0 15.9 %collective-permute-start.11 = (f32[304,128]{1,0:T(8,128)S(1)}, f32[304,128]{1,0:T(8,128)S(1)}, u32[]{:S(2)}, u32[]{:S(2)}) collective-permute-start(f32[304,128]{1,0:T(8,128)S(1)} %get-tuple-element.53), channel_id=1, source_target_pairs={{0,8},{4,12},{8,16},{12,20},{16,24},{20,28},{24,0},{28,4},{1,9},{5... | collective-permute-start | bytes 466952 | tf_op jit(solution)/shard_map/ppermute | solution.py:28
  82.1 19.2 %collective-permute-start.12 = (f32[304,128]{1,0:T(8,128)S(1)}, f32[304,128]{1,0:T(8,128)S(1)}, u32[]{:S(2)}, u32[]{:S(2)}) collective-permute-start(f32[304,128]{1,0:T(8,128)S(1)} %get-tuple-element.54), channel_id=1, source_target_pairs={{0,12},{4,16},{8,20},{12,24},{16,28},{20,0},{24,4},{28,8},{1,13},{... | collective-permute-start | bytes 466952 | tf_op jit(solution)/shard_map/ppermute | solution.py:28
  82.4 19.6 %collective-permute-start.13 = (f32[304,128]{1,0:T(8,128)S(1)}, f32[304,128]{1,0:T(8,128)S(1)}, u32[]{:S(2)}, u32[]{:S(2)}) collective-permute-start(f32[304,128]{1,0:T(8,128)S(1)} %get-tuple-element.55), channel_id=1, source_target_pairs={{0,24},{4,28},{8,0},{12,4},{16,8},{20,12},{24,16},{28,20},{1,25},{... | collective-permute-start | bytes 466952 | tf_op jit(solution)/shard_map/ppermute | solution.py:28
  87.1 14.9 %collective-permute-start.14 = (f32[304,128]{1,0:T(8,128)S(1)}, f32[304,128]{1,0:T(8,128)S(1)}, u32[]{:S(2)}, u32[]{:S(2)}) collective-permute-start(f32[304,128]{1,0:T(8,128)S(1)} %get-tuple-element.56), channel_id=1, source_target_pairs={{0,28},{4,0},{8,4},{12,8},{16,12},{20,16},{24,20},{28,24},{1,29},{... | collective-permute-start | bytes 466952 | tf_op jit(solution)/shard_map/ppermute | solution.py:28
  87.8 24.0 %collective-permute-start.8 = (f32[304,128]{1,0:T(8,128)S(1)}, f32[304,128]{1,0:T(8,128)S(1)}, u32[]{:S(2)}, u32[]{:S(2)}) collective-permute-start(f32[304,128]{1,0:T(8,128)S(1)} %get-tuple-element.50), channel_id=1, source_target_pairs={{0,16},{4,20},{8,24},{12,28},{16,0},{20,4},{24,8},{28,12},{1,17},{... | collective-permute-start | bytes 466952 | tf_op jit(solution)/shard_map/ppermute | solution.py:28
  97.9 13.9 %collective-permute-start.9 = (f32[304,128]{1,0:T(8,128)S(1)}, f32[304,128]{1,0:T(8,128)S(1)}, u32[]{:S(2)}, u32[]{:S(2)}) collective-permute-start(f32[304,128]{1,0:T(8,128)S(1)} %get-tuple-element.51), channel_id=1, source_target_pairs={{0,4},{4,8},{8,12},{12,16},{16,20},{20,24},{24,28},{28,0},{1,5},{5... | collective-permute-start | bytes 466952 | tf_op jit(solution)/shard_map/ppermute | solution.py:28
  113.1 4.3 %collective-permute-start.21 = (f32[4,2,32,128]{3,2,1,0:T(8,128)S(1)}, f32[4,2,32,128]{3,2,1,0:T(8,128)S(1)}, u32[]{:S(2)}, u32[]{:S(2)}) collective-permute-start(f32[4,2,32,128]{3,2,1,0:T(8,128)S(1)} %get-tuple-element.68), channel_id=1, source_target_pairs={{0,4},{4,0},{8,12},{12,8},{16,20},{20,16},{24,28},{28,24},{1,5},{5... | collective-permute-start | bytes 393224 | tf_op jit(solution)/shard_map/ppermute | solution.py:429
  117.5 4.6 %collective-permute-start.22 = (f32[2,32,128]{2,1,0:T(8,128)S(1)}, f32[2,32,128]{2,1,0:T(8,128)S(1)}, u32[]{:S(2)}, u32[]{:S(2)}) collective-permute-start(f32[2,32,128]{2,1,0:T(8,128)S(1)} %get-tuple-element.71), channel_id=1, source_target_pairs={{0,8},{4,12},{8,16},{12,20},{16,24},{20,28},{24,0},{28,4},{1,9},{5... | collective-permute-start | bytes 98312 | tf_op jit(solution)/shard_map/ppermute | solution.py:28
  117.6 4.6 %collective-permute-start.23 = (f32[2,32,128]{2,1,0:T(8,128)S(1)}, f32[2,32,128]{2,1,0:T(8,128)S(1)}, u32[]{:S(2)}, u32[]{:S(2)}) collective-permute-start(f32[2,32,128]{2,1,0:T(8,128)S(1)} %get-tuple-element.69), channel_id=1, source_target_pairs={{0,16},{4,20},{8,24},{12,28},{16,0},{20,4},{24,8},{28,12},{1,17},{... | collective-permute-start | bytes 98312 | tf_op jit(solution)/shard_map/ppermute | solution.py:28
  117.8 4.6 %collective-permute-start.24 = (f32[2,32,128]{2,1,0:T(8,128)S(1)}, f32[2,32,128]{2,1,0:T(8,128)S(1)}, u32[]{:S(2)}, u32[]{:S(2)}) collective-permute-start(f32[2,32,128]{2,1,0:T(8,128)S(1)} %get-tuple-element.70), channel_id=1, source_target_pairs={{0,24},{4,28},{8,0},{12,4},{16,8},{20,12},{24,16},{28,20},{1,25},{... | collective-permute-start | bytes 98312 | tf_op jit(solution)/shard_map/ppermute | solution.py:28
  122.5 5.2 %collective-permute-start.25 = (f32[2,32,128]{2,1,0:T(8,128)S(1)}, f32[2,32,128]{2,1,0:T(8,128)S(1)}, u32[]{:S(2)}, u32[]{:S(2)}) collective-permute-start(f32[2,32,128]{2,1,0:T(8,128)S(1)} %bitcast_add_fusion.refs_0_), channel_id=1, source_target_pairs={{0,1},{1,2},{2,3},{3,0},{4,5},{5,6},{6,7},{7,4},{8,9},{9,10},{10,1... | collective-permute-start | bytes 98312 | tf_op jit(solution)/shard_map/ppermute | solution.py:28
  126.6 2.8 %collective-permute-start.26 = (f32[2,32,128]{2,1,0:T(8,128)S(1)}, f32[2,32,128]{2,1,0:T(8,128)S(1)}, u32[]{:S(2)}, u32[]{:S(2)}) collective-permute-start(f32[2,32,128]{2,1,0:T(8,128)S(1)} %bitcast_add_fusion.refs_0_), channel_id=1, source_target_pairs={{0,2},{1,3},{2,0},{3,1},{4,6},{5,7},{6,4},{7,5},{8,10},{9,11},{10,... | collective-permute-start | bytes 98312 | tf_op jit(solution)/shard_map/ppermute | solution.py:28
  126.9 3.3 %collective-permute-start.27 = (f32[2,32,128]{2,1,0:T(8,128)S(1)}, f32[2,32,128]{2,1,0:T(8,128)S(1)}, u32[]{:S(2)}, u32[]{:S(2)}) collective-permute-start(f32[2,32,128]{2,1,0:T(8,128)S(1)} %bitcast_add_fusion.refs_0_), channel_id=1, source_target_pairs={{0,3},{1,0},{2,1},{3,2},{4,7},{5,4},{6,5},{7,6},{8,11},{9,8},{10,9... | collective-permute-start | bytes 98312 | tf_op jit(solution)/shard_map/ppermute | solution.py:28

commit v6 on v5

--- a/solution.py
+++ b/solution.py
@@ -26,6 +26,18 @@
     count = lax.axis_size(axis)
     pairs = [(source, (source + steps) % count) for source in range(count)]
     return lax.ppermute(value, axis, pairs)
+
+
+def swapped(value, axis, turn):
+    count = lax.axis_size(axis)
+    if count & (count - 1):
+        return shifted(value, axis, turn)
+    return lax.ppermute(value, axis, [(source, source ^ turn) for source in range(count)])
+
+
+def far_first(count):
+    half = (count + 1) // 2
+    return list(range(half, count)) + list(range(1, half))
 
 
 def phase_angle(q_vector, xcoord, ycoord, zcoord, x_extent, y_extent, z_extent):
@@ -495,7 +507,7 @@
     multiply(blocks, *extent)
 
     share = reduced_over_points(totals[-1], factor)
-    shares = [share] + [shifted(share, "gz", step) for step in range(1, slabs)]
+    shares = [share] + [swapped(share, "gz", step) for step in far_first(slabs)]
     return result(shares)[None]
 
 

time: 131 us -> 131 us (level)
    ppermute x0 -> x3, starting transfers between devices: none -> 4.69 us  [swapped(): lax.ppermute(value, axis, [(source, source ^ turn) for source in range(co...]
    ppermute x27 -> x24, starting transfers between devices: 78.4 us -> 73.8 us  [shifted(): return lax.ppermute(value, axis, pairs)]
    ppermute x27 -> x24, waiting for transfers between devices: 31.4 us -> 28.3 us  [shifted(): return lax.ppermute(value, axis, pairs)]
    ppermute x0 -> x3, waiting for transfers between devices: none -> 1.94 us  [swapped(): lax.ppermute(value, axis, [(source, source ^ turn) for source in range(co...]
  transfers between devices with their start and end apart: 28 -> 28, of which waited for: 11 -> 9; matrix products, arithmetic and copies ran while one was open for 1% -> 1% of each run, Pallas kernels for 7% -> 7%
where the time goes in v6:
time: 131 us; the launch traced here: 130 us
  starting transfers between devices  79.9 us (61%)
  waiting for transfers between devices  33.2 us (25%)
  Pallas kernels  12.6 us (10%)
  local copies, waits for them, and re-layouts  3.09 us (2%)
    ppermute x24, starting transfers between devices, shifted(): return lax.ppermute(value, axis, pairs)  73.8 us
    ppermute x24, waiting for transfers between devices, shifted(): return lax.ppermute(value, axis, pairs)  28.3 us
    pallas_call x3, Pallas kernels, pack(): pl.pallas_call(functools.partial(pack_kernel, parts, turns, start, stop),...  5.91 us
    ppermute x3, starting transfers between devices, swapped(): lax.ppermute(value, axis, [(source, source ^ turn) for source in range(co...  4.69 us
    pallas_call x3, Pallas kernels, chunk_products(): pl.pallas_call(functools.partial(chunk_kernel, offsets, before is None, f...  3.99 us
    ppermute x1, waiting for transfers between devices, reduced_over_points(): total = total + lax.ppermute(blocks[turn], 'ka', pairs)  2.9 us
    unnamed x13, local copies, waits for them, and re-layouts  2.88 us
  transfers between devices with their start and end apart: 28, of which 9 were waited for; matrix products, arithmetic and copies ran while one was open for 1% of the time, Pallas kernels for 7%

profile of v6, /device:TPU:1, one launch (start us, length us, event | category | flops | bytes accessed | tf_op | source)
XLA Modules:
  0.0 129.9 jit_solution(3034412568533017065)
XLA Ops:
  0.0 1.2 shard_map.37
  1.2 2.2 %collective-permute-start.3 = (f32[2,32,896]{2,1,0:T(8,128)S(1)}, f32[2,32,896]{2,1,0:T(8,128)S(1)}, u32[]{:S(2)}, u32[]{:S(2)}) collective-permute-start(f32[2,32,896]{2,1,0:T(8,128)S(1)} %get-tuple-element.40), channel_id=1, source_target_pairs={{0,8},{4,12},{8,16},{12,20},{16,24},{20,28},{24,0},{28,4},{1,9},{5... | collective-permute-start | bytes 688136 | tf_op jit(solution)/shard_map/ppermute | solution.py:28
  3.4 2.2 %shard_map.38 = (f32[2,32,896]{2,1,0:T(8,128)S(1)}, f32[2,32,896]{2,1,0:T(8,128)}, f32[2,32,896]{2,1,0:T(8,128)}, f32[2,32,896]{2,1,0:T(8,128)S(1)}, f32[2,32,896]{2,1,0:T(8,128)S(1)}) custom-call(f32[2,3,32,6400]{3,2,1,0:T(8,128)} %bitcast.22), custom_call_target="tpu_custom_call" | custom-call | bytes 2293760 | tf_op jit(solution)/shard_map/pallas_call | solution.py:180
  5.7 3.3 %collective-permute-start.2 = (f32[2,32,896]{2,1,0:T(8,128)S(1)}, f32[2,32,896]{2,1,0:T(8,128)S(1)}, u32[]{:S(2)}, u32[]{:S(2)}) collective-permute-start(f32[2,32,896]{2,1,0:T(8,128)S(1)} %get-tuple-element.39), channel_id=1, source_target_pairs={{0,20},{4,24},{8,28},{12,0},{16,4},{20,8},{24,12},{28,16},{1,21},{... | collective-permute-start | bytes 688136 | tf_op jit(solution)/shard_map/ppermute | solution.py:28
  9.0 1.2 collective-permute-start.5
  10.2 2.9 %collective-permute-start.6 = (f32[2,32,896]{2,1,0:T(8,128)S(1)}, f32[2,32,896]{2,1,0:T(8,128)S(1)}, u32[]{:S(2)}, u32[]{:S(2)}) collective-permute-start(f32[2,32,896]{2,1,0:T(8,128)S(1)} %get-tuple-element.44), channel_id=1, source_target_pairs={{0,28},{4,0},{8,4},{12,8},{16,12},{20,16},{24,20},{28,24},{1,29},{... | collective-permute-start | bytes 688136 | tf_op jit(solution)/shard_map/ppermute | solution.py:28
  13.3 0.1 copy.6
  13.4 0.1 convert_add_fusion
  13.5 0.0 collective-permute-done.3.refs_3_
  13.5 0.3 collective-permute-start
  13.8 2.4 %shard_map.40 = (f32[2,32,896]{2,1,0:T(8,128)}, f32[2,32,896]{2,1,0:T(8,128)S(1)}, f32[2,32,896]{2,1,0:T(8,128)S(1)}, f32[2,32,896]{2,1,0:T(8,128)}, f32[2,32,89...) custom-call(f32[2,3,32,6400]{3,2,1,0:T(8,128)} %bitcast.23), custom_call_target="tpu_custom_call" | custom-call | bytes 3670016 | tf_op jit(solution)/shard_map/pallas_call | solution.py:180
  16.2 0.7 copy-done
  16.9 0.7 copy-done.1
  17.6 0.7 copy-done.2
  18.3 0.7 copy-done.3
  19.0 6.6 %collective-permute-start.1 = (f32[2,32,896]{2,1,0:T(8,128)S(1)}, f32[2,32,896]{2,1,0:T(8,128)S(1)}, u32[]{:S(2)}, u32[]{:S(2)}) collective-permute-start(f32[2,32,896]{2,1,0:T(8,128)S(1)} %get-tuple-element.38), channel_id=1, source_target_pairs={{0,16},{4,20},{8,24},{12,28},{16,0},{20,4},{24,8},{28,12},{1,17},{... | collective-permute-start | bytes 688136 | tf_op jit(solution)/shard_map/ppermute | solution.py:28
  25.6 1.2 collective-permute-done.4.refs_4_
  26.8 0.0 collective-permute-start.7
  26.8 6.3 %collective-permute-done.5.refs_5_ = f32[2,32,896]{2,1,0:T(8,128)S(1)} collective-permute-done((f32[2,32,896]{2,1,0:T(8,128)}, f32[2,32,896]{2,1,0:T(8,128)S(1)}, u32[]{:S(2)}, u32[]{:S(2)}) %collective-permute-start.5) | collective-permute-done | bytes 229408 | tf_op jit(solution)/shard_map/ppermute | solution.py:28
  33.1 0.0 collective-permute-start.15
  33.1 0.1 dynamic-slice_maximum_fusion
  33.2 0.1 copy.7
  33.3 0.1 reshape.160
  33.4 9.1 %collective-permute-start.16 = (f32[2,32,896]{2,1,0:T(8,128)}, f32[2,32,896]{2,1,0:T(8,128)S(1)}, u32[]{:S(2)}, u32[]{:S(2)}) collective-permute-start(f32[2,32,896]{2,1,0:T(8,128)} %copy-done.3), channel_id=1, source_target_pairs={{0,4},{4,8},{8,12},{12,16},{16,20},{20,24},{24,28},{28,0},{1,5},{5... | collective-permute-start | bytes 688136 | tf_op jit(solution)/shard_map/ppermute | solution.py:28
  42.4 0.0 collective-permute-done.refs_0_
  42.4 12.2 %collective-permute-start.17 = (f32[2,32,896]{2,1,0:T(8,128)}, f32[2,32,896]{2,1,0:T(8,128)S(1)}, u32[]{:S(2)}, u32[]{:S(2)}) collective-permute-start(f32[2,32,896]{2,1,0:T(8,128)} %copy-done.2), channel_id=1, source_target_pairs={{0,20},{4,24},{8,28},{12,0},{16,4},{20,8},{24,12},{28,16},{1,21},{... | collective-permute-start | bytes 688136 | tf_op jit(solution)/shard_map/ppermute | solution.py:28
  54.6 0.0 collective-permute-done.1.refs_1_
  54.6 3.4 %collective-permute-start.18 = (f32[2,32,896]{2,1,0:T(8,128)}, f32[2,32,896]{2,1,0:T(8,128)S(1)}, u32[]{:S(2)}, u32[]{:S(2)}) collective-permute-start(f32[2,32,896]{2,1,0:T(8,128)} %copy-done.1), channel_id=1, source_target_pairs={{0,28},{4,0},{8,4},{12,8},{16,12},{20,16},{24,20},{28,24},{1,29},{... | collective-permute-start | bytes 688136 | tf_op jit(solution)/shard_map/ppermute | solution.py:28
  58.0 8.6 %collective-permute-done.7.refs_3_ = f32[2,32,896]{2,1,0:T(8,128)S(1)} collective-permute-done((f32[2,32,896]{2,1,0:T(8,128)}, f32[2,32,896]{2,1,0:T(8,128)S(1)}, u32[]{:S(2)}, u32[]{:S(2)}) %collective-permute-start.7) | collective-permute-done | bytes 229408 | tf_op jit(solution)/shard_map/ppermute | solution.py:28
  66.6 1.5 %collective-permute-start.20 = (f32[2,32,896]{2,1,0:T(8,128)S(1)}, f32[2,32,896]{2,1,0:T(8,128)S(1)}, u32[]{:S(2)}, u32[]{:S(2)}) collective-permute-start(f32[2,32,896]{2,1,0:T(8,128)S(1)} %get-tuple-element.64), channel_id=1, source_target_pairs={{0,8},{4,12},{8,16},{12,20},{16,24},{20,28},{24,0},{28,4},{1,9},{5... | collective-permute-start | bytes 688136 | tf_op jit(solution)/shard_map/ppermute | solution.py:28
  68.0 0.7 sine_multiply_fusion
  68.7 1.4 %shard_map.39.refs_10_ = f32[8,64,128]{2,1,0:T(8,128)S(1)} custom-call(f32[2,32,896]{2,1,0:T(8,128)S(1)} %collective-permute-done.refs_0_, f32[2,32,896]{2,1,0:T(8,128)S(1)} %collective-permute-done.1.refs_1_, f32[2,32,896]{2,1,0:T(8,128)S(1)} %collective-permute-done.2.refs_2_, f32[2,32,896]{2,1,0:T(8,128)S(1)} %collective-permute-done.3.refs_3_, ...), custom_call_target="tpu_custom_call" | custom-call | flops 469762048 | bytes 1835008 | tf_op jit(solution)/shard_map/pallas_call | solution.py:384
  70.1 1.9 %shard_map.41 = (f32[304,128]{1,0:T(8,128)S(1)}, f32[304,128]{1,0:T(8,128)S(1)}, f32[304,128]{1,0:T(8,128)S(1)}, f32[304,128]{1,0:T(8,128)S(1)}, f32[304,128]{1,...) custom-call(f32[2,3,32,6400]{3,2,1,0:T(8,128)} %bitcast.24), custom_call_target="tpu_custom_call" | custom-call | bytes 2490368 | tf_op jit(solution)/shard_map/pallas_call | solution.py:266
  72.0 0.0 collective-permute-done.16.refs_1_
  72.0 10.0 %collective-permute-start.10 = (f32[304,128]{1,0:T(8,128)S(1)}, f32[304,128]{1,0:T(8,128)S(1)}, u32[]{:S(2)}, u32[]{:S(2)}) collective-permute-start(f32[304,128]{1,0:T(8,128)S(1)} %get-tuple-element.52), channel_id=1, source_target_pairs={{0,20},{4,24},{8,28},{12,0},{16,4},{20,8},{24,12},{28,16},{1,21},{... | collective-permute-start | bytes 466952 | tf_op jit(solution)/shard_map/ppermute | solution.py:28
  82.0 0.0 collective-permute-done.17.refs_2_
  82.0 0.0 collective-permute-start.11
  82.1 0.0 collective-permute-done.18.refs_4_
  82.1 0.3 collective-permute-start.12
  82.4 0.0 collective-permute-done.19.refs_5_
  82.4 4.7 %collective-permute-start.13 = (f32[304,128]{1,0:T(8,128)S(1)}, f32[304,128]{1,0:T(8,128)S(1)}, u32[]{:S(2)}, u32[]{:S(2)}) collective-permute-start(f32[304,128]{1,0:T(8,128)S(1)} %get-tuple-element.55), channel_id=1, source_target_pairs={{0,24},{4,28},{8,0},{12,4},{16,8},{20,12},{24,16},{28,20},{1,25},{... | collective-permute-start | bytes 466952 | tf_op jit(solution)/shard_map/ppermute | solution.py:28
  87.1 0.0 collective-permute-done.20.refs_6_
  87.1 0.7 collective-permute-start.14
  87.8 0.0 collective-permute-done.10.refs_2_
  87.8 10.2 %collective-permute-start.8 = (f32[304,128]{1,0:T(8,128)S(1)}, f32[304,128]{1,0:T(8,128)S(1)}, u32[]{:S(2)}, u32[]{:S(2)}) collective-permute-start(f32[304,128]{1,0:T(8,128)S(1)} %get-tuple-element.50), channel_id=1, source_target_pairs={{0,16},{4,20},{8,24},{12,28},{16,0},{20,4},{24,8},{28,12},{1,17},{... | collective-permute-start | bytes 466952 | tf_op jit(solution)/shard_map/ppermute | solution.py:28
  97.9 0.0 collective-permute-done.11.refs_3_
  97.9 1.9 %collective-permute-start.9 = (f32[304,128]{1,0:T(8,128)S(1)}, f32[304,128]{1,0:T(8,128)S(1)}, u32[]{:S(2)}, u32[]{:S(2)}) collective-permute-start(f32[304,128]{1,0:T(8,128)S(1)} %get-tuple-element.51), channel_id=1, source_target_pairs={{0,4},{4,8},{8,12},{12,16},{16,20},{20,24},{24,28},{28,0},{1,5},{5... | collective-permute-start | bytes 466952 | tf_op jit(solution)/shard_map/ppermute | solution.py:28
  99.9 1.4 %shard_map.42.refs_10_ = f32[8,64,128]{2,1,0:T(8,128)S(1)} custom-call(f32[2,32,896]{2,1,0:T(8,128)S(1)} %collective-permute-done.15.refs_0_, f32[2,32,896]{2,1,0:T(8,128)S(1)} %collective-permute-done.16.refs_1_, f32[2,32,896]{2,1,0:T(8,128)S(1)} %collective-permute-done.17.refs_2_, f32[2,32,896]{2,1,0:T(8,128)S(1)} %collective-permute-done.7.refs_3_, ...), custom_call_target="tpu_custom_call" | custom-call | flops 469762048 | bytes 1835008 | tf_op jit(solution)/shard_map/pallas_call | solution.py:384
  101.2 0.8 collective-permute-done.13.refs_5_
  102.0 9.8 %collective-permute-done.8.refs_0_ = f32[304,128]{1,0:T(8,128)S(1)} collective-permute-done((f32[304,128]{1,0:T(8,128)S(1)}, f32[304,128]{1,0:T(8,128)S(1)}, u32[]{:S(2)}, u32[]{:S(2)}) %collective-permute-start.8) | collective-permute-done | bytes 155680 | tf_op jit(solution)/shard_map/ppermute | solution.py:28
  111.8 0.0 collective-permute-done.9.refs_1_
  111.8 1.3 shard_map.43
  113.1 1.4 %collective-permute-start.21 = (f32[4,2,32,128]{3,2,1,0:T(8,128)S(1)}, f32[4,2,32,128]{3,2,1,0:T(8,128)S(1)}, u32[]{:S(2)}, u32[]{:S(2)}) collective-permute-start(f32[4,2,32,128]{3,2,1,0:T(8,128)S(1)} %get-tuple-element.68), channel_id=1, source_target_pairs={{0,4},{4,0},{8,12},{12,8},{16,20},{20,16},{24,28},{28,24},{1,5},{5... | collective-permute-start | bytes 393224 | tf_op jit(solution)/shard_map/ppermute | solution.py:441
  114.5 2.9 %collective-permute-done.21 = f32[4,2,32,128]{3,2,1,0:T(8,128)S(1)} collective-permute-done((f32[4,2,32,128]{3,2,1,0:T(8,128)S(1)}, f32[4,2,32,128]{3,2,1,0:T(8,128)S(1)}, u32[]{:S(2)}, u32[]{:S(2)}) %collective-permute-start.21) | collective-permute-done | bytes 131104 | tf_op jit(solution)/shard_map/ppermute | solution.py:441
  117.5 0.1 collective-permute-start.22
  117.6 0.3 collective-permute-start.23
  117.8 3.0 %collective-permute-start.24 = (f32[2,32,128]{2,1,0:T(8,128)S(1)}, f32[2,32,128]{2,1,0:T(8,128)S(1)}, u32[]{:S(2)}, u32[]{:S(2)}) collective-permute-start(f32[2,32,128]{2,1,0:T(8,128)S(1)} %get-tuple-element.70), channel_id=1, source_target_pairs={{0,24},{4,28},{8,0},{12,4},{16,8},{20,12},{24,16},{28,20},{1,25},{... | collective-permute-start | bytes 98312 | tf_op jit(solution)/shard_map/ppermute | solution.py:28
  120.8 1.3 %collective-permute-done.22 = f32[2,32,128]{2,1,0:T(8,128)S(1)} collective-permute-done((f32[2,32,128]{2,1,0:T(8,128)S(1)}, f32[2,32,128]{2,1,0:T(8,128)S(1)}, u32[]{:S(2)}, u32[]{:S(2)}) %collective-permute-start.22) | collective-permute-done | bytes 32800 | tf_op jit(solution)/shard_map/ppermute | solution.py:28
  122.1 0.0 collective-permute-done.23
  122.1 0.3 collective-permute-done.24
  122.5 1.3 collective-permute-start.25
  123.8 3.4 %collective-permute-start.26 = (f32[2,32,128]{2,1,0:T(8,128)S(1)}, f32[2,32,128]{2,1,0:T(8,128)S(1)}, u32[]{:S(2)}, u32[]{:S(2)}) collective-permute-start(f32[2,32,128]{2,1,0:T(8,128)S(1)} %bitcast_add_fusion.refs_0_), channel_id=1, source_target_pairs={{0,3},{1,2},{2,1},{3,0},{4,7},{5,6},{6,5},{7,4},{8,11},{9,10},{10,... | collective-permute-start | bytes 98312 | tf_op jit(solution)/shard_map/ppermute | solution.py:35
  127.2 1.9 %collective-permute-done.26.refs_2_ = f32[2,32,128]{2,1,0:T(8,128)S(1)} collective-permute-done((f32[2,32,128]{2,1,0:T(8,128)S(1)}, f32[2,32,128]{2,1,0:T(8,128)S(1)}, u32[]{:S(2)}, u32[]{:S(2)}) %collective-permute-start.26) | collective-permute-done | bytes 32800 | tf_op jit(solution)/shard_map/ppermute | solution.py:35
  129.1 0.8 shard_map.44
  (29 shorter events, 0.2 us)
Async XLA Ops:
  0.0 13.3 %copy-start.5 = (f32[2,3]{1,0:T(2,128)S(1)}, f32[2,3]{1,0:T(2,128)}, u32[]{:S(2)}) copy-start(f32[2,3]{1,0:T(2,128)} %param.4) | copy-start | bytes 76
  0.0 13.4 %copy-start.4 = (s32[8,2,3]{0,1,2:T(2,128)S(1)}, s32[8,2,3]{0,1,2:T(2,128)}, u32[]{:S(2)}) copy-start(s32[8,2,3]{0,1,2:T(2,128)} %param.5) | copy-start | bytes 580
  1.2 12.2 %collective-permute-start.3 = (f32[2,32,896]{2,1,0:T(8,128)S(1)}, f32[2,32,896]{2,1,0:T(8,128)S(1)}, u32[]{:S(2)}, u32[]{:S(2)}) collective-permute-start(f32[2,32,896]{2,1,0:T(8,128)S(1)} %get-tuple-element.40), channel_id=1, source_target_pairs={{0,8},{4,12},{8,16},{12,20},{16,24},{20,28},{24,0},{28,4},{1,9},{5... | collective-permute-start | bytes 688136 | tf_op jit(solution)/shard_map/ppermute | solution.py:28
  5.7 13.3 %collective-permute-start.2 = (f32[2,32,896]{2,1,0:T(8,128)S(1)}, f32[2,32,896]{2,1,0:T(8,128)S(1)}, u32[]{:S(2)}, u32[]{:S(2)}) collective-permute-start(f32[2,32,896]{2,1,0:T(8,128)S(1)} %get-tuple-element.39), channel_id=1, source_target_pairs={{0,20},{4,24},{8,28},{12,0},{16,4},{20,8},{24,12},{28,16},{1,21},{... | collective-permute-start | bytes 688136 | tf_op jit(solution)/shard_map/ppermute | solution.py:28
  9.0 17.8 %collective-permute-start.4 = (f32[2,32,896]{2,1,0:T(8,128)}, f32[2,32,896]{2,1,0:T(8,128)S(1)}, u32[]{:S(2)}, u32[]{:S(2)}) collective-permute-start(f32[2,32,896]{2,1,0:T(8,128)} %get-tuple-element.42), channel_id=1, source_target_pairs={{0,4},{4,8},{8,12},{12,16},{16,20},{20,24},{24,28},{28,0},{1,5},{5... | collective-permute-start | bytes 688136 | tf_op jit(solution)/shard_map/ppermute | solution.py:28
  9.0 24.1 %collective-permute-start.5 = (f32[2,32,896]{2,1,0:T(8,128)}, f32[2,32,896]{2,1,0:T(8,128)S(1)}, u32[]{:S(2)}, u32[]{:S(2)}) collective-permute-start(f32[2,32,896]{2,1,0:T(8,128)} %get-tuple-element.43), channel_id=1, source_target_pairs={{0,12},{4,16},{8,20},{12,24},{16,28},{20,0},{24,4},{28,8},{1,13},{... | collective-permute-start | bytes 688136 | tf_op jit(solution)/shard_map/ppermute | solution.py:28
  10.2 23.1 %collective-permute-start.6 = (f32[2,32,896]{2,1,0:T(8,128)S(1)}, f32[2,32,896]{2,1,0:T(8,128)S(1)}, u32[]{:S(2)}, u32[]{:S(2)}) collective-permute-start(f32[2,32,896]{2,1,0:T(8,128)S(1)} %get-tuple-element.44), channel_id=1, source_target_pairs={{0,28},{4,0},{8,4},{12,8},{16,12},{20,16},{24,20},{28,24},{1,29},{... | collective-permute-start | bytes 688136 | tf_op jit(solution)/shard_map/ppermute | solution.py:28
  13.5 29.0 %collective-permute-start = (f32[2,32,896]{2,1,0:T(8,128)S(1)}, f32[2,32,896]{2,1,0:T(8,128)S(1)}, u32[]{:S(2)}, u32[]{:S(2)}) collective-permute-start(f32[2,32,896]{2,1,0:T(8,128)S(1)} %get-tuple-element.37), channel_id=1, source_target_pairs={{0,24},{4,28},{8,0},{12,4},{16,8},{20,12},{24,16},{28,20},{1,25},{... | collective-permute-start | bytes 688136 | tf_op jit(solution)/shard_map/ppermute | solution.py:28
  16.2 0.7 copy-start
  16.9 0.7 copy-start.1
  17.6 0.7 copy-start.2
  18.3 0.7 copy-start.3
  19.0 35.6 %collective-permute-start.1 = (f32[2,32,896]{2,1,0:T(8,128)S(1)}, f32[2,32,896]{2,1,0:T(8,128)S(1)}, u32[]{:S(2)}, u32[]{:S(2)}) collective-permute-start(f32[2,32,896]{2,1,0:T(8,128)S(1)} %get-tuple-element.38), channel_id=1, source_target_pairs={{0,16},{4,20},{8,24},{12,28},{16,0},{20,4},{24,8},{28,12},{1,17},{... | collective-permute-start | bytes 688136 | tf_op jit(solution)/shard_map/ppermute | solution.py:28
  26.8 39.8 %collective-permute-start.7 = (f32[2,32,896]{2,1,0:T(8,128)}, f32[2,32,896]{2,1,0:T(8,128)S(1)}, u32[]{:S(2)}, u32[]{:S(2)}) collective-permute-start(f32[2,32,896]{2,1,0:T(8,128)} %get-tuple-element.48), channel_id=1, source_target_pairs={{0,12},{4,16},{8,20},{12,24},{16,28},{20,0},{24,4},{28,8},{1,13},{... | collective-permute-start | bytes 688136 | tf_op jit(solution)/shard_map/ppermute | solution.py:28
  33.1 33.5 %collective-permute-start.15 = (f32[2,32,896]{2,1,0:T(8,128)}, f32[2,32,896]{2,1,0:T(8,128)S(1)}, u32[]{:S(2)}, u32[]{:S(2)}) collective-permute-start(f32[2,32,896]{2,1,0:T(8,128)} %get-tuple-element.58), channel_id=1, source_target_pairs={{0,16},{4,20},{8,24},{12,28},{16,0},{20,4},{24,8},{28,12},{1,17},{... | collective-permute-start | bytes 688136 | tf_op jit(solution)/shard_map/ppermute | solution.py:28
  33.4 38.6 %collective-permute-start.16 = (f32[2,32,896]{2,1,0:T(8,128)}, f32[2,32,896]{2,1,0:T(8,128)S(1)}, u32[]{:S(2)}, u32[]{:S(2)}) collective-permute-start(f32[2,32,896]{2,1,0:T(8,128)} %copy-done.3), channel_id=1, source_target_pairs={{0,4},{4,8},{8,12},{12,16},{16,20},{20,24},{24,28},{28,0},{1,5},{5... | collective-permute-start | bytes 688136 | tf_op jit(solution)/shard_map/ppermute | solution.py:28
  42.4 39.6 %collective-permute-start.17 = (f32[2,32,896]{2,1,0:T(8,128)}, f32[2,32,896]{2,1,0:T(8,128)S(1)}, u32[]{:S(2)}, u32[]{:S(2)}) collective-permute-start(f32[2,32,896]{2,1,0:T(8,128)} %copy-done.2), channel_id=1, source_target_pairs={{0,20},{4,24},{8,28},{12,0},{16,4},{20,8},{24,12},{28,16},{1,21},{... | collective-permute-start | bytes 688136 | tf_op jit(solution)/shard_map/ppermute | solution.py:28
  54.6 27.4 %collective-permute-start.18 = (f32[2,32,896]{2,1,0:T(8,128)}, f32[2,32,896]{2,1,0:T(8,128)S(1)}, u32[]{:S(2)}, u32[]{:S(2)}) collective-permute-start(f32[2,32,896]{2,1,0:T(8,128)} %copy-done.1), channel_id=1, source_target_pairs={{0,28},{4,0},{8,4},{12,8},{16,12},{20,16},{24,20},{28,24},{1,29},{... | collective-permute-start | bytes 688136 | tf_op jit(solution)/shard_map/ppermute | solution.py:28
  66.6 15.8 %collective-permute-start.19 = (f32[2,32,896]{2,1,0:T(8,128)}, f32[2,32,896]{2,1,0:T(8,128)S(1)}, u32[]{:S(2)}, u32[]{:S(2)}) collective-permute-start(f32[2,32,896]{2,1,0:T(8,128)} %copy-done), channel_id=1, source_target_pairs={{0,24},{4,28},{8,0},{12,4},{16,8},{20,12},{24,16},{28,20},{1,25},{... | collective-permute-start | bytes 688136 | tf_op jit(solution)/shard_map/ppermute | solution.py:28
  66.6 20.5 %collective-permute-start.20 = (f32[2,32,896]{2,1,0:T(8,128)S(1)}, f32[2,32,896]{2,1,0:T(8,128)S(1)}, u32[]{:S(2)}, u32[]{:S(2)}) collective-permute-start(f32[2,32,896]{2,1,0:T(8,128)S(1)} %get-tuple-element.64), channel_id=1, source_target_pairs={{0,8},{4,12},{8,16},{12,20},{16,24},{20,28},{24,0},{28,4},{1,9},{5... | collective-permute-start | bytes 688136 | tf_op jit(solution)/shard_map/ppermute | solution.py:28
  72.0 15.8 %collective-permute-start.10 = (f32[304,128]{1,0:T(8,128)S(1)}, f32[304,128]{1,0:T(8,128)S(1)}, u32[]{:S(2)}, u32[]{:S(2)}) collective-permute-start(f32[304,128]{1,0:T(8,128)S(1)} %get-tuple-element.52), channel_id=1, source_target_pairs={{0,20},{4,24},{8,28},{12,0},{16,4},{20,8},{24,12},{28,16},{1,21},{... | collective-permute-start | bytes 466952 | tf_op jit(solution)/shard_map/ppermute | solution.py:28
  82.0 15.9 %collective-permute-start.11 = (f32[304,128]{1,0:T(8,128)S(1)}, f32[304,128]{1,0:T(8,128)S(1)}, u32[]{:S(2)}, u32[]{:S(2)}) collective-permute-start(f32[304,128]{1,0:T(8,128)S(1)} %get-tuple-element.53), channel_id=1, source_target_pairs={{0,8},{4,12},{8,16},{12,20},{16,24},{20,28},{24,0},{28,4},{1,9},{5... | collective-permute-start | bytes 466952 | tf_op jit(solution)/shard_map/ppermute | solution.py:28
  82.1 19.2 %collective-permute-start.12 = (f32[304,128]{1,0:T(8,128)S(1)}, f32[304,128]{1,0:T(8,128)S(1)}, u32[]{:S(2)}, u32[]{:S(2)}) collective-permute-start(f32[304,128]{1,0:T(8,128)S(1)} %get-tuple-element.54), channel_id=1, source_target_pairs={{0,12},{4,16},{8,20},{12,24},{16,28},{20,0},{24,4},{28,8},{1,13},{... | collective-permute-start | bytes 466952 | tf_op jit(solution)/shard_map/ppermute | solution.py:28
  82.4 19.6 %collective-permute-start.13 = (f32[304,128]{1,0:T(8,128)S(1)}, f32[304,128]{1,0:T(8,128)S(1)}, u32[]{:S(2)}, u32[]{:S(2)}) collective-permute-start(f32[304,128]{1,0:T(8,128)S(1)} %get-tuple-element.55), channel_id=1, source_target_pairs={{0,24},{4,28},{8,0},{12,4},{16,8},{20,12},{24,16},{28,20},{1,25},{... | collective-permute-start | bytes 466952 | tf_op jit(solution)/shard_map/ppermute | solution.py:28
  87.1 14.9 %collective-permute-start.14 = (f32[304,128]{1,0:T(8,128)S(1)}, f32[304,128]{1,0:T(8,128)S(1)}, u32[]{:S(2)}, u32[]{:S(2)}) collective-permute-start(f32[304,128]{1,0:T(8,128)S(1)} %get-tuple-element.56), channel_id=1, source_target_pairs={{0,28},{4,0},{8,4},{12,8},{16,12},{20,16},{24,20},{28,24},{1,29},{... | collective-permute-start | bytes 466952 | tf_op jit(solution)/shard_map/ppermute | solution.py:28
  87.8 24.0 %collective-permute-start.8 = (f32[304,128]{1,0:T(8,128)S(1)}, f32[304,128]{1,0:T(8,128)S(1)}, u32[]{:S(2)}, u32[]{:S(2)}) collective-permute-start(f32[304,128]{1,0:T(8,128)S(1)} %get-tuple-element.50), channel_id=1, source_target_pairs={{0,16},{4,20},{8,24},{12,28},{16,0},{20,4},{24,8},{28,12},{1,17},{... | collective-permute-start | bytes 466952 | tf_op jit(solution)/shard_map/ppermute | solution.py:28
  97.9 13.9 %collective-permute-start.9 = (f32[304,128]{1,0:T(8,128)S(1)}, f32[304,128]{1,0:T(8,128)S(1)}, u32[]{:S(2)}, u32[]{:S(2)}) collective-permute-start(f32[304,128]{1,0:T(8,128)S(1)} %get-tuple-element.51), channel_id=1, source_target_pairs={{0,4},{4,8},{8,12},{12,16},{16,20},{20,24},{24,28},{28,0},{1,5},{5... | collective-permute-start | bytes 466952 | tf_op jit(solution)/shard_map/ppermute | solution.py:28
  113.1 4.3 %collective-permute-start.21 = (f32[4,2,32,128]{3,2,1,0:T(8,128)S(1)}, f32[4,2,32,128]{3,2,1,0:T(8,128)S(1)}, u32[]{:S(2)}, u32[]{:S(2)}) collective-permute-start(f32[4,2,32,128]{3,2,1,0:T(8,128)S(1)} %get-tuple-element.68), channel_id=1, source_target_pairs={{0,4},{4,0},{8,12},{12,8},{16,20},{20,16},{24,28},{28,24},{1,5},{5... | collective-permute-start | bytes 393224 | tf_op jit(solution)/shard_map/ppermute | solution.py:441
  117.5 4.6 %collective-permute-start.22 = (f32[2,32,128]{2,1,0:T(8,128)S(1)}, f32[2,32,128]{2,1,0:T(8,128)S(1)}, u32[]{:S(2)}, u32[]{:S(2)}) collective-permute-start(f32[2,32,128]{2,1,0:T(8,128)S(1)} %get-tuple-element.71), channel_id=1, source_target_pairs={{0,8},{4,12},{8,16},{12,20},{16,24},{20,28},{24,0},{28,4},{1,9},{5... | collective-permute-start | bytes 98312 | tf_op jit(solution)/shard_map/ppermute | solution.py:28
  117.6 4.6 %collective-permute-start.23 = (f32[2,32,128]{2,1,0:T(8,128)S(1)}, f32[2,32,128]{2,1,0:T(8,128)S(1)}, u32[]{:S(2)}, u32[]{:S(2)}) collective-permute-start(f32[2,32,128]{2,1,0:T(8,128)S(1)} %get-tuple-element.69), channel_id=1, source_target_pairs={{0,16},{4,20},{8,24},{12,28},{16,0},{20,4},{24,8},{28,12},{1,17},{... | collective-permute-start | bytes 98312 | tf_op jit(solution)/shard_map/ppermute | solution.py:28
  117.8 4.6 %collective-permute-start.24 = (f32[2,32,128]{2,1,0:T(8,128)S(1)}, f32[2,32,128]{2,1,0:T(8,128)S(1)}, u32[]{:S(2)}, u32[]{:S(2)}) collective-permute-start(f32[2,32,128]{2,1,0:T(8,128)S(1)} %get-tuple-element.70), channel_id=1, source_target_pairs={{0,24},{4,28},{8,0},{12,4},{16,8},{20,12},{24,16},{28,20},{1,25},{... | collective-permute-start | bytes 98312 | tf_op jit(solution)/shard_map/ppermute | solution.py:28
  122.5 4.7 %collective-permute-start.25 = (f32[2,32,128]{2,1,0:T(8,128)S(1)}, f32[2,32,128]{2,1,0:T(8,128)S(1)}, u32[]{:S(2)}, u32[]{:S(2)}) collective-permute-start(f32[2,32,128]{2,1,0:T(8,128)S(1)} %bitcast_add_fusion.refs_0_), channel_id=1, source_target_pairs={{0,2},{1,3},{2,0},{3,1},{4,6},{5,7},{6,4},{7,5},{8,10},{9,11},{10,... | collective-permute-start | bytes 98312 | tf_op jit(solution)/shard_map/ppermute | solution.py:35
  123.8 5.4 %collective-permute-start.26 = (f32[2,32,128]{2,1,0:T(8,128)S(1)}, f32[2,32,128]{2,1,0:T(8,128)S(1)}, u32[]{:S(2)}, u32[]{:S(2)}) collective-permute-start(f32[2,32,128]{2,1,0:T(8,128)S(1)} %bitcast_add_fusion.refs_0_), channel_id=1, source_target_pairs={{0,3},{1,2},{2,1},{3,0},{4,7},{5,6},{6,5},{7,4},{8,11},{9,10},{10,... | collective-permute-start | bytes 98312 | tf_op jit(solution)/shard_map/ppermute | solution.py:35
  127.2 1.9 %collective-permute-start.27 = (f32[2,32,128]{2,1,0:T(8,128)S(1)}, f32[2,32,128]{2,1,0:T(8,128)S(1)}, u32[]{:S(2)}, u32[]{:S(2)}) collective-permute-start(f32[2,32,128]{2,1,0:T(8,128)S(1)} %bitcast_add_fusion.refs_0_), channel_id=1, source_target_pairs={{0,1},{1,0},{2,3},{3,2},{4,5},{5,4},{6,7},{7,6},{8,9},{9,8},{10,11... | collective-permute-start | bytes 98312 | tf_op jit(solution)/shard_map/ppermute | solution.py:35
